TPU v7x, 256 devices: a whole 4x4x8 slice. The times are simulated.
256 devices in a mesh: row: 32 (over y, z), col: 8 (over x, core).
Axes of the slice: x: 4, y: 4, z: 8, core: 2. Of those that a mesh axis runs over, the one named last changes fastest.
Arguments:
- tokens: bfloat16 [1024, 6144], P('col', 'row'), may hold values from -12 to 12
- out_grad: bfloat16 [1024, 6144], P('col', 'row'), may hold values from -12 to 12
- image_ids: int32 [1024], replicated, may hold values from 0 to 7, as said below
- learn_rate: float32 [1], replicated, may hold values from 2 to 16
- in_weight: float32 [6144, 24576], P('row', 'col'), may hold values from -6 to 6
- out_weight: float32 [24576, 6144], P('col', 'row'), may hold values from -6 to 6
Outputs:
- input_grad: bfloat16 [1024, 6144], P('col', 'row')
- in_weight_next: float32 [6144, 24576], P('row', 'col')
- out_weight_next: float32 [24576, 6144], P('col', 'row')
- example_norm: float32 [8], replicated
Inputs may be any that keep to these rules, and one draw needn't show every extreme that they name: `image_ids`: each of the 8 images is named by exactly 128 tokens, in any order.
All inputs are finite; a program needn't handle non-finite values.
Results may differ from a plain program's by a relative error of at most 0.03.
Values may be sent and summed in bfloat16 or wider, within the bound.
No kernel may reach another device: no remote copies, remote signals or barrier semaphores. Data moves between devices by JAX's collectives and lax.ppermute only.
A program may use at most 128 MiB of HBM per device.

v0:
```python
import jax
import jax.numpy as jnp
from jax import lax
from jax.sharding import PartitionSpec as P

D = 6144
FF = 24576
TOK_IMG = 128


root_half = 0.7071067811865476
inv_root_tau = 0.3989422804014327


def gelu_exact(value):
    return 0.5 * value * (1.0 + lax.erf(value * root_half))


def gelu_slope(value):
    return (
        0.5 * (1.0 + lax.erf(value * root_half))
        + value * jnp.exp(-0.5 * value * value) * inv_root_tau
    )


def contract_rows(left, right):
    return lax.dot_general(
        left, right, (((0,), (0,)), ((), ())), preferred_element_type=jnp.float32
    )


def contract_cols(left, right):
    return lax.dot_general(
        left, right, (((1,), (1,)), ((), ())), preferred_element_type=jnp.float32
    )


def shards(tokens, out_grad, image_ids, learn_rate, in_weight, out_weight):
    scale_in = D ** (-0.5)
    scale_out = FF ** (-0.5)
    in_half = in_weight.astype(jnp.bfloat16)
    out_half = out_weight.astype(jnp.bfloat16)
    tok_all, grad_all = (
        lax.all_gather(tokens, "col", axis=0, tiled=True),
        lax.all_gather(out_grad, "col", axis=0, tiled=True),
    )
    row_piece = tok_all
    pre_act = lax.psum_scatter(
        (jnp.dot(row_piece, in_half, preferred_element_type=jnp.float32) * scale_in).astype(
            jnp.bfloat16
        ),
        "row",
        scatter_dimension=0,
        tiled=True,
    ).astype(jnp.float32)
    act_all = lax.all_gather(gelu_exact(pre_act).astype(jnp.bfloat16), "row", axis=0, tiled=True)
    row_piece = grad_all
    act_grad = lax.psum_scatter(
        (contract_cols(row_piece, out_half) * scale_out).astype(jnp.bfloat16),
        "row",
        scatter_dimension=0,
        tiled=True,
    ).astype(jnp.float32)
    hid_grad = (act_grad * gelu_slope(pre_act)).astype(jnp.bfloat16)
    hid_all = lax.all_gather(hid_grad, "row", axis=0, tiled=True)
    row_piece = hid_all
    input_grad = lax.psum_scatter(
        (contract_cols(row_piece, in_half) * scale_in).astype(jnp.bfloat16),
        "col",
        scatter_dimension=0,
        tiled=True,
    )
    image_count = image_ids.shape[0] // TOK_IMG
    order = jnp.argsort(image_ids, stable=True)

    def by_image(rows):
        return jnp.take(rows, order, axis=0).reshape(image_count, TOK_IMG, rows.shape[1])

    tok_img = by_image(tok_all)
    hid_img = by_image(hid_all)
    act_img = by_image(act_all)
    grad_img = by_image(grad_all)

    def one_image(running, pieces):
        block_in = contract_rows(pieces[0], pieces[1]) * scale_in
        block_out = contract_rows(pieces[2], pieces[3]) * scale_out
        squares = jnp.sum(block_in * block_in) + jnp.sum(block_out * block_out)
        return ((running[0] + block_in, running[1] + block_out), squares)

    zeros_in = jnp.zeros(in_weight.shape, jnp.float32)
    zeros_out = jnp.zeros(out_weight.shape, jnp.float32)
    (grad_in, grad_out), local_sums = lax.scan(
        one_image, (zeros_in, zeros_out), (tok_img, hid_img, act_img, grad_img)
    )
    example_sq = lax.psum(local_sums, ("row", "col"))
    example_norm = 0.5 * jnp.log(example_sq + 1e-06)
    in_weight_next = in_weight - learn_rate[0] * grad_in
    out_weight_next = out_weight - learn_rate[0] * grad_out
    return (input_grad, in_weight_next, out_weight_next, example_norm)


def solution(mesh):
    placed = (P("col", "row"), P("col", "row"), P(), P(), P("row", "col"), P("col", "row"))
    return jax.shard_map(
        shards,
        mesh=mesh,
        in_specs=placed,
        out_specs=(P("col", "row"), P("row", "col"), P("col", "row"), P()),
        check_vma=False,
    )
```

profile of v0, /device:TPU:1, one launch (start us, length us, event | category | flops | bytes accessed | tf_op | source)
XLA Modules:
  0.0 850.5 jit_solution(4668173064501753654)
XLA Ops:
  8.1 16.2 %all_gather.13 = bf16[1024,192]{1,0:T(8,128)(2,1)S(1)} all-gather(bf16[128,192]{1,0:T(8,128)(2,1)S(1)} %copy.13), channel_id=1, replica_groups=mesh['row'=32,'col'=8] {'col'}, dimensions={0}, use_global_device_ids=true | all-gather | bytes 442368 | tf_op jit(solution)/shard_map/all_gather | solution.py:44
  24.3 6.1 multiply_convert_fusion
  31.3 13.1 %all_gather.12 = bf16[1024,192]{1,0:T(8,128)(2,1)S(1)} all-gather(bf16[128,192]{1,0:T(8,128)(2,1)S(1)} %copy.12), channel_id=1, replica_groups=mesh['row'=32,'col'=8] {'col'}, dimensions={0}, use_global_device_ids=true | all-gather | bytes 442368 | tf_op jit(solution)/shard_map/all_gather | solution.py:45
  44.4 4.5 multiply_convert_fusion.1
  49.0 202.8 %reduce-scatter.8.cloned.1.call-done = bf16[32,3072]{1,0:T(8,128)(2,1)} async-done(((bf16[1024,3072]{1,0:T(8,128)(2,1)}), bf16[32,3072]{1,0:T(8,128)(2,1)}) %reduce-scatter.8.cloned.1.call-update) | async-done | bytes 196624 | tf_op jit(solution)/shard_map/reduce_scatter | solution.py:48
  251.8 227.5 %reduce-scatter.6.cloned.1.call-done = bf16[32,3072]{1,0:T(8,128)(2,1)} async-done(((bf16[1024,3072]{1,0:T(8,128)(2,1)}), bf16[32,3072]{1,0:T(8,128)(2,1)}) %reduce-scatter.6.cloned.1.call-update) | async-done | bytes 196624 | tf_op jit(solution)/shard_map/reduce_scatter | solution.py:58
  482.1 4.4 sort.17
  486.5 5.0 gather_fusion.3
  491.5 5.0 gather_fusion
  499.4 73.0 %all-gather.3.cloned.1.call-done = bf16[1024,3072]{1,0:T(8,128)(2,1)} async-done(((bf16[32,3072]{1,0:T(8,128)(2,1)}), bf16[1024,3072]{1,0:T(8,128)(2,1)}) %all-gather.3.cloned.1.call-update) | async-done | bytes 6291472 | tf_op jit(solution)/shard_map/all_gather | solution.py:65
  572.4 5.7 fusion.10
  579.2 15.8 %gather_fusion.1 = bf16[1024,3072]{1,0:T(8,128)(2,1)} fusion(bf16[1024,3072]{1,0:T(8,128)(2,1)} %all-gather.3.cloned.1.call-done, s32[1024]{0:T(1024)S(1)} %fusion.23), kind=kCustom, calls=%fused_computation.1.clone | custom fusion | bytes 12587008 | tf_op jit(solution)/shard_map/jit(_take)/gather | solution.py:77
  595.0 65.6 %all-gather.5.cloned.1.call-done = bf16[1024,3072]{1,0:T(8,128)(2,1)} async-done(((bf16[32,3072]{1,0:T(8,128)(2,1)}), bf16[1024,3072]{1,0:T(8,128)(2,1)}) %all-gather.5.cloned.1.call-update) | async-done | bytes 6291472 | tf_op jit(solution)/shard_map/all_gather | solution.py:56
  660.6 15.8 %gather_fusion.2 = bf16[1024,3072]{1,0:T(8,128)(2,1)} fusion(bf16[1024,3072]{1,0:T(8,128)(2,1)} %all-gather.5.cloned.1.call-done, s32[1024]{0:T(1024)S(1)} %fusion.23), kind=kCustom, calls=%fused_computation.3.clone | custom fusion | bytes 12587008 | tf_op jit(solution)/shard_map/jit(_take)/gather | solution.py:77
  676.3 10.6 %broadcast_select_fusion = (bf16[1024,3072]{1,0:T(8,128)(2,1)}, bf16[1024,3072]{1,0:T(8,128)(2,1)}) fusion(bf16[1024,3072]{1,0:T(8,128)(2,1)} %gather_fusion.2, pred[1024]{0:T(1024)(128)(4,1)S(1)} %compare_and_fusion, bf16[1024,3072]{1,0:T(8,128)(2,1)} %gather_fusion.1), kind=kLoop, calls=%fused_computation.22 | loop fusion | flops 6291456 | bytes 25166848 | tf_op jit(solution)/shard_map/jit(_take)/select_n | solution.py:77
  686.9 73.1 %while.15 = (s32[]{:T(128)}, f32[192,3072]{1,0:T(8,128)S(1)}, f32[3072,192]{0,1:T(8,128)}, f32[8]{0:T(128)S(1)}, bf16[8,128,192]{2,1,0:T(8,128)(2,1)}, /*index=5...) while((s32[]{:T(128)}, f32[192,3072]{1,0:T(8,128)S(1)}, ...), condition=%wide.region_7.10_spmd.clone, body=%wide.region_4.9_spmd.clone.sunk | while | flops 307888128 | bytes 11144342 | solution.py:92
  698.8 4.6 multiply_reduce_fusion.5
  708.0 4.6 multiply_reduce_fusion.5
  717.2 4.6 multiply_reduce_fusion.5
  726.5 4.6 multiply_reduce_fusion.5
  735.7 4.6 multiply_reduce_fusion.5
  745.0 4.6 multiply_reduce_fusion.5
  754.2 4.6 multiply_reduce_fusion.5
  760.0 74.8 %psum.7 = f32[8]{0:T(128)S(1)} all-reduce(f32[8]{0:T(128)S(1)} %get-tuple-element.54), channel_id=1, replica_groups=mesh['row'=32,'col'=8] {'row','col'}, use_global_device_ids=true, to_apply=%region_8.11 | all-reduce | flops 8 | bytes 64 | tf_op jit(solution)/shard_map/psum | solution.py:95
  (53 shorter events, 49.0 us)
Async XLA Ops:
  7.2 244.6 %reduce-scatter.8.cloned.1.call-start = ((), (), s32[]{:S(2)}) async-start(), calls=%async_computation.4 | async-start | bytes 6488064 | tf_op jit(solution)/shard_map/reduce_scatter | solution.py:48
  30.4 0.8 copy-start.3
  30.4 14.0 %copy-start = (f32[3072,192]{0,1:T(8,128)S(1)}, f32[3072,192]{0,1:T(8,128)}, u32[]{:S(2)}) copy-start(f32[3072,192]{0,1:T(8,128)} %param.17) | copy-start | bytes 7077892
  30.4 448.8 %reduce-scatter.6.cloned.1.call-start = ((), (), s32[]{:S(2)}) async-start(), calls=%async_computation.3 | async-start | bytes 6488064 | tf_op jit(solution)/shard_map/reduce_scatter | solution.py:58
  48.9 433.2 %copy-start.4 = (s32[1024]{0:T(1024)S(1)}, s32[1024]{0:T(1024)}, u32[]{:S(2)}) copy-start(s32[1024]{0:T(1024)} %param.14) | copy-start | bytes 12292
  48.9 523.5 %all-gather.3.cloned.1.call-start = ((), (), s32[]{:S(2)}) async-start(), calls=%async_computation.5 | async-start | bytes 6488064 | tf_op jit(solution)/shard_map/all_gather | solution.py:65
  481.3 179.3 %all-gather.5.cloned.1.call-start = ((), (), s32[]{:S(2)}) async-start(), calls=%async_computation.6 | async-start | bytes 6488064 | tf_op jit(solution)/shard_map/all_gather | solution.py:56
  481.9 360.5 %reduce-scatter.10.cloned.1.call-start = ((), (), s32[]{:S(2)}) async-start(), calls=%async_computation.7 | async-start | bytes 589824
  491.5 5.6 copy-start.2
  835.3 3.6 copy-start.1
Sparse Core Ops, SparseCore 0:
  30.6 221.1 reduce-scatter.7
  256.3 222.9 reduce-scatter.5
  481.9 90.5 all-gather.2
  574.9 85.6 all-gather.4
  662.9 28.4 reduce-scatter.9
where the time goes:
time: 851 us; the launch traced here: 850 us
  waiting for transfers between devices  569 us (67%)
  blocking collectives  104 us (12%)
  matrix products  79.5 us (9%)
  local copies, waits for them, and re-layouts  46.8 us (5%)
  other arithmetic  26.8 us (3%)
  between operations  14.5 us (2%)
  loops' own time  8.98 us (1%)
    reduce_scatter x1, waiting for transfers between devices, shards(): lax.psum_scatter((contract_cols(row_piece, out_half) * scale_out).astype(...  228 us
    reduce_scatter x1, waiting for transfers between devices, shards(): lax.psum_scatter((jnp.dot(row_piece, in_half, preferred_element_type=jnp....  203 us
    psum x1, blocking collectives, shards(): example_sq = lax.psum(local_sums, ('row', 'col'))  74.8 us
    all_gather x1, waiting for transfers between devices, shards(): hid_all = lax.all_gather(hid_grad, 'row', axis=0, tiled=True)  73 us
    all_gather x1, waiting for transfers between devices, shards(): lax.all_gather(gelu_exact(pre_act).astype(jnp.bfloat16), 'row', axis=0, t...  65.6 us
    dot_general x16, matrix products, contract_rows(): lax.dot_general(left, right, (((0,), (0,)), ((), ())), preferred_element_...  63.2 us
    gather x4, local copies, waits for them, and re-layouts, by_image(): jnp.take(rows, order, axis=0).reshape(image_count, TOK_IMG, rows.shape[1])  41.5 us
  transfers between devices with their start and end apart: 5, of which 4 were waited for; matrix products, arithmetic and copies ran while one was open for 17% of the time, Pallas kernels for 0%

commit v1 on v0

v1 whole, which is shorter than its diff:
```python
import functools

import jax
import jax.numpy as jnp
from jax import lax
from jax.experimental import pallas as pl
from jax.experimental.pallas import tpu as pltpu
from jax.sharding import Mesh, PartitionSpec as P

D = 6144
FF = 24576
IMAGES = 8
TOK_IMG = 128
TOKENS = 1024
FEAT = 192
NY, NZ, NX = 4, 8, 4
HID = 768
SCALE_IN = D ** (-0.5)
SCALE_OUT = FF ** (-0.5)
NORM_ROWS = 16

root_half = 0.7071067811865476
inv_root_tau = 0.3989422804014327

f32 = jnp.float32
bf16 = jnp.bfloat16
BIG = pltpu.CompilerParams(vmem_limit_bytes=48 * 1024 * 1024)


def dot(left, right, dims):
    return lax.dot_general(left, right, (dims, ((), ())), preferred_element_type=f32)


def split_hidden(weight):
    def body(w_ref, o_ref):
        o_ref[0] = w_ref[...].astype(bf16)

    return pl.pallas_call(
        body,
        grid=(NY,),
        in_specs=[pl.BlockSpec((FEAT, HID), lambda i: (0, i))],
        out_specs=pl.BlockSpec((1, FEAT, HID), lambda i: (i, 0, 0)),
        out_shape=jax.ShapeDtypeStruct((NY, FEAT, HID), bf16),
        compiler_params=BIG,
    )(weight)


def sort_and_project(own, other, order, weight, scale):
    def body(own_ref, oth_ref, p_ref, w_ref, x_ref, part_ref, acc):
        step = pl.program_id(0)
        pieces = [own_ref[0, i] for i in range(NX)] + [oth_ref[0, i] for i in range(NX)]
        rows = jnp.concatenate(pieces, axis=1)
        ordered = dot(rows, p_ref[...], ((1,), (0,))).astype(bf16)
        x_ref[...] = ordered
        prod = dot(ordered, w_ref[0], ((0,), (0,)))

        @pl.when(step == 0)
        def _():
            acc[...] = prod

        @pl.when(step > 0)
        def _():
            acc[...] += prod

        @pl.when(step == NY - 1)
        def _():
            part_ref[...] = (acc[...] * scale).astype(bf16)

    return pl.pallas_call(
        body,
        grid=(NY,),
        in_specs=[
            pl.BlockSpec((1, NX, FEAT, 128), lambda i: (i, 0, 0, 0)),
            pl.BlockSpec((1, NX, FEAT, 128), lambda i: (i, 0, 0, 0)),
            pl.BlockSpec((TOKENS, TOKENS), lambda i: (0, 0)),
            pl.BlockSpec((1, FEAT, HID), lambda i: (i, 0, 0)),
        ],
        out_specs=[
            pl.BlockSpec((FEAT, TOKENS), lambda i: (i, 0)),
            pl.BlockSpec((TOKENS, HID), lambda i: (0, 0)),
        ],
        out_shape=[
            jax.ShapeDtypeStruct((NY * FEAT, TOKENS), bf16),
            jax.ShapeDtypeStruct((TOKENS, HID), bf16),
        ],
        scratch_shapes=[pltpu.VMEM((TOKENS, HID), f32)],
        compiler_params=BIG,
    )(own, other, order, weight)


def image_grads(feats, hidden, scale):
    tile = 256

    def body(x_ref, h_ref, g_ref, sq_ref):
        step = pl.program_id(0)
        total = None
        sums = []
        for b in range(IMAGES):
            block = dot(
                x_ref[:, b * TOK_IMG : (b + 1) * TOK_IMG],
                h_ref[b * TOK_IMG : (b + 1) * TOK_IMG, :],
                ((1,), (0,)),
            )
            total = block if total is None else total + block
            squares = jnp.sum(block * block, axis=0, keepdims=True)
            lanes = squares[:, 0:128]
            for j in range(1, HID // 128):
                lanes = lanes + squares[:, j * 128 : (j + 1) * 128]
            sums.append(lanes)
        g_ref[...] = (total * scale).astype(bf16)
        found = jnp.concatenate(sums, axis=0) * (scale * scale)

        @pl.when(step == 0)
        def _():
            sq_ref[...] = found

        @pl.when(step > 0)
        def _():
            sq_ref[...] += found

    rows = NY * FEAT
    return pl.pallas_call(
        body,
        grid=(rows // tile,),
        in_specs=[
            pl.BlockSpec((tile, TOKENS), lambda i: (i, 0)),
            pl.BlockSpec((TOKENS, HID), lambda i: (0, 0)),
        ],
        out_specs=[
            pl.BlockSpec((tile, HID), lambda i: (i, 0)),
            pl.BlockSpec((IMAGES, 128), lambda i: (0, 0)),
        ],
        out_shape=[
            jax.ShapeDtypeStruct((rows, HID), bf16),
            jax.ShapeDtypeStruct((IMAGES, 128), f32),
        ],
        compiler_params=BIG,
    )(feats, hidden)


def input_grads(weight, hidden, order, norms):
    def body(w_ref, h_ref, p_ref, n_ref, o_ref):
        grad = (dot(w_ref[0], h_ref[...], ((1,), (1,))) * SCALE_IN).astype(bf16)
        placed = dot(grad, p_ref[...], ((1,), (1,))).astype(bf16)
        for core in range(2):
            for i in range(NX):
                at = (core * NX + i) * 128
                o_ref[core, 0, i, 0:FEAT, :] = placed[:, at : at + 128]
                o_ref[core, 0, i, FEAT:, :] = n_ref[...]

    rows = FEAT + NORM_ROWS
    return pl.pallas_call(
        body,
        grid=(NY,),
        in_specs=[
            pl.BlockSpec((1, FEAT, HID), lambda i: (i, 0, 0)),
            pl.BlockSpec((TOKENS, HID), lambda i: (0, 0)),
            pl.BlockSpec((TOKENS, TOKENS), lambda i: (0, 0)),
            pl.BlockSpec((NORM_ROWS, 128), lambda i: (0, 0)),
        ],
        out_specs=pl.BlockSpec((2, 1, NX, rows, 128), lambda i: (0, i, 0, 0, 0)),
        out_shape=jax.ShapeDtypeStruct((2, NY, NX, rows, 128), bf16),
        compiler_params=BIG,
    )(weight, hidden, order, norms)


def update(weight, grads, rate):
    def body(rate_ref, w_ref, g_ref, o_ref):
        o_ref[...] = w_ref[...] - rate_ref[0] * g_ref[0].astype(f32)

    return pl.pallas_call(
        body,
        grid=(NY,),
        in_specs=[
            pl.BlockSpec(memory_space=pltpu.SMEM),
            pl.BlockSpec((FEAT, HID), lambda i: (0, i)),
            pl.BlockSpec((1, FEAT, HID), lambda i: (i, 0, 0)),
        ],
        out_specs=pl.BlockSpec((FEAT, HID), lambda i: (0, i)),
        out_shape=jax.ShapeDtypeStruct(weight.shape, f32),
        compiler_params=BIG,
    )(rate, weight, grads)


def gelu_and_slope(pre):
    phi = 0.5 * (1.0 + lax.erf(pre * root_half))
    return pre * phi, phi + pre * jnp.exp(-0.5 * pre * pre) * inv_root_tau


def exchange(value, axes):
    return lax.all_to_all(value, axes, 0, 0, tiled=True)


def swap_cores(value):
    return lax.ppermute(value, "core", [(0, 1), (1, 0)])


def gather_yx(feats):
    own = exchange(jnp.broadcast_to(feats, (NY * NX, *feats.shape)), ("y", "x"))
    own = own.reshape(NY, NX, *feats.shape)
    return own, swap_cores(own)


def token_order(image_ids, core):
    at = jnp.arange(TOKENS)
    same = (image_ids[:, None] == image_ids[None, :]) & (at[None, :] < at[:, None])
    place = image_ids * TOK_IMG + jnp.sum(same.astype(jnp.int32), axis=1)
    halves = place.reshape(NX, 2, 128).transpose(1, 0, 2)
    halves = jnp.where(core == 0, halves, halves[::-1])
    return (halves.reshape(TOKENS)[:, None] == at[None, :]).astype(bf16)


def shards(tokens, out_grad, image_ids, learn_rate, in_weight, out_weight):
    core = lax.axis_index("core")
    out_weight_t = out_weight.T
    in_mine = exchange(split_hidden(in_weight).reshape(NY * FEAT, HID), "y").reshape(NY, FEAT, HID)
    out_mine = exchange(split_hidden(out_weight_t).reshape(NY * FEAT, HID), "y").reshape(
        NY, FEAT, HID
    )
    order = token_order(image_ids, core)
    tok_sorted, pre_part = sort_and_project(*gather_yx(tokens.T), order, in_mine, SCALE_IN)
    grad_sorted, grad_part = sort_and_project(*gather_yx(out_grad.T), order, out_mine, SCALE_OUT)
    both = jnp.concatenate(
        [
            pre_part.reshape(NZ, TOK_IMG, HID),
            grad_part.reshape(NZ, TOK_IMG, HID),
        ],
        axis=1,
    )
    summed = lax.psum_scatter(both, "z", scatter_dimension=0).astype(f32)
    pre_act, act_grad = summed[:TOK_IMG], summed[TOK_IMG:]
    act, slope = gelu_and_slope(pre_act)
    mine = jnp.stack([act.astype(bf16), (act_grad * slope).astype(bf16)])
    every = lax.all_gather(mine, "z")
    act_all = every[:, 0].reshape(TOKENS, HID)
    hid_all = every[:, 1].reshape(TOKENS, HID)
    in_sum, in_sq = image_grads(tok_sorted, hid_all, SCALE_IN)
    out_sum, out_sq = image_grads(grad_sorted, act_all, SCALE_OUT)
    squares = jnp.sum(in_sq + out_sq, axis=1)
    high = squares.astype(bf16)
    rest = squares - high.astype(f32)
    middle = rest.astype(bf16)
    low = (rest - middle.astype(f32)).astype(bf16)
    lanes = jnp.arange(128)[None, :]
    triple = jnp.stack([high, middle, low])
    spread = jnp.pad(jnp.tile(triple, (1, 2)), ((0, NORM_ROWS - 3), (0, 128 - 2 * IMAGES)))
    norms = jnp.where(lanes // IMAGES == core, spread, jnp.zeros_like(spread))
    parts = input_grads(in_mine, hid_all, order, norms)
    merged = (parts[0].astype(f32) + swap_cores(parts[1]).astype(f32)).astype(bf16)
    rows = FEAT + NORM_ROWS
    got = exchange(merged.reshape(NY * NX, rows, 128), ("y", "x"))
    got = jnp.sum(got.astype(f32), axis=0)
    input_grad = got[:FEAT].astype(bf16).T
    sq_here = jnp.sum(got[FEAT:], axis=0)
    sq_here = sq_here[:IMAGES] + sq_here[IMAGES : 2 * IMAGES]
    sq_all = exchange(jnp.broadcast_to(sq_here, (NZ, 8, IMAGES)), "z")
    example_sq = jnp.sum(sq_all[:, 0], axis=0)
    example_norm = 0.5 * jnp.log(example_sq + 1e-06)
    in_back = exchange(in_sum, "y").reshape(NY, FEAT, HID)
    out_back = exchange(out_sum, "y").reshape(NY, FEAT, HID)
    in_next = update(in_weight, in_back, learn_rate)
    out_next = update(out_weight_t, out_back, learn_rate).T
    return (input_grad, in_next, out_next, example_norm)


def solution(mesh):
    chips = Mesh(mesh.devices.reshape(NY, NZ, NX, 2), ("y", "z", "x", "core"))
    row, col = ("y", "z"), ("x", "core")
    placed = (P(col, row), P(col, row), P(), P(), P(row, col), P(col, row))
    return jax.shard_map(
        shards,
        mesh=chips,
        in_specs=placed,
        out_specs=(P(col, row), P(row, col), P(col, row), P()),
        check_vma=False,
    )
```

time: 851 us -> 281 us (0.33)
  waiting for transfers between devices: 569 us -> 145 us
  blocking collectives: 104 us -> 21.1 us
  matrix products: 79.5 us -> 0 us
  Pallas kernels: 0 us -> 37.9 us
  starting transfers between devices: 0.38 us -> 33.2 us
  local copies, waits for them, and re-layouts: 46.8 us -> 14.2 us
  other arithmetic: 26.8 us -> 10.9 us
  loops' own time: 8.98 us -> 0 us
    reduce_scatter x2 -> x1, waiting for transfers between devices: 430 us -> 48.5 us  [shards(): summed = lax.psum_scatter(both, 'z', scatter_dimension=0).astype(f32)]
    all_gather x2 -> x1, waiting for transfers between devices: 139 us -> 46.6 us  [shards(): every = lax.all_gather(mine, 'z')]
    dot_general x19 -> x0, matrix products: 79.5 us -> none  [the longest x16 63.2 us: contract_rows(): lax.dot_general(left, right, (((0,), (0,)), ((), ())), preferred_element_...]
    psum x1 -> x0, blocking collectives: 74.8 us -> none  [shards(): example_sq = lax.psum(local_sums, ('row', 'col'))]
    all_to_all x0 -> x7, waiting for transfers between devices: none -> 49.4 us  [exchange(): return lax.all_to_all(value, axes, 0, 0, tiled=True)]
    gather x4 -> x0, local copies, waits for them, and re-layouts: 41.5 us -> none  [by_image(): jnp.take(rows, order, axis=0).reshape(image_count, TOK_IMG, rows.shape[1])]
    pallas_call x0 -> x9, Pallas kernels: none -> 37.9 us  [the longest x2 15.7 us: sort_and_project(): pl.pallas_call(body, grid=(NY,), in_specs=[pl.BlockSpec((1, NX, FEAT, 128...]
    all_to_all x0 -> x7, starting transfers between devices: none -> 29.5 us  [exchange(): return lax.all_to_all(value, axes, 0, 0, tiled=True)]
  transfers between devices with their start and end apart: 5 -> 12, of which waited for: 4 -> 8; matrix products, arithmetic and copies ran while one was open for 17% -> 2% of each run, Pallas kernels for 0% -> 8%
where the time goes in v1:
time: 281 us; the launch traced here: 277 us
  waiting for transfers between devices  145 us (52%)
  Pallas kernels  37.9 us (13%)
  starting transfers between devices  33.2 us (12%)
  blocking collectives  21.1 us (8%)
  between operations  15 us (5%)
  local copies, waits for them, and re-layouts  14.2 us (5%)
  other arithmetic  10.9 us (4%)
    all_to_all x7, waiting for transfers between devices, exchange(): return lax.all_to_all(value, axes, 0, 0, tiled=True)  49.4 us
    reduce_scatter x1, waiting for transfers between devices, shards(): summed = lax.psum_scatter(both, 'z', scatter_dimension=0).astype(f32)  48.5 us
    all_gather x1, waiting for transfers between devices, shards(): every = lax.all_gather(mine, 'z')  46.6 us
    all_to_all x7, starting transfers between devices, exchange(): return lax.all_to_all(value, axes, 0, 0, tiled=True)  29.5 us
    all_to_all x1, blocking collectives, exchange(): return lax.all_to_all(value, axes, 0, 0, tiled=True)  21.1 us
    pallas_call x2, Pallas kernels, sort_and_project(): pl.pallas_call(body, grid=(NY,), in_specs=[pl.BlockSpec((1, NX, FEAT, 128...  15.7 us
    unnamed x34, local copies, waits for them, and re-layouts  7.64 us
    pallas_call x1, Pallas kernels, input_grads(): pl.pallas_call(body, grid=(NY,), in_specs=[pl.BlockSpec((1, FEAT, HID), l...  7.12 us
  transfers between devices with their start and end apart: 12, of which 8 were waited for; matrix products, arithmetic and copies ran while one was open for 2% of the time, Pallas kernels for 8%

profile of v1, /device:TPU:1, one launch (start us, length us, event | category | flops | bytes accessed | tf_op | source)
XLA Modules:
  0.0 276.7 jit_solution(12861747811126017361)
XLA Ops:
  8.1 21.1 %all_to_all.50 = bf16[16,192,128]{2,1,0:T(8,128)(2,1)} all-to-all(bf16[16,192,128]{2,1,0:T(8,128)(2,1)S(1)} %broadcast_in_dim.27), channel_id=1, replica_groups=mesh['y'=4,'z'=8,'x'=4,'core'=2] {'y','x'}, dimensions={0} | all-to-all | bytes 1572864 | tf_op jit(solution)/shard_map/all_to_all | solution.py:191
  30.3 4.3 %all-to-all-start.1 = ((bf16[16,192,128]{2,1,0:T(8,128)(2,1)}), bf16[16,192,128]{2,1,0:T(8,128)(2,1)}, u32[]{:S(2)}, u32[]{:S(2)}) async-start(bf16[16,192,128]{2,1,0:T(8,128)(2,1)} %broadcast_in_dim.26), calls=%async_computation.1 | async-start | bytes 1572864 | tf_op jit(solution)/shard_map/all_to_all | solution.py:191
  36.3 10.9 %all-to-all-done.1 = bf16[16,192,128]{2,1,0:T(8,128)(2,1)} async-done(((bf16[16,192,128]{2,1,0:T(8,128)(2,1)}), bf16[16,192,128]{2,1,0:T(8,128)(2,1)}, u32[]{:S(2)}, u32[]{:S(2)}) %all-to-all-start.1) | async-done | bytes 786464 | tf_op jit(solution)/shard_map/all_to_all | solution.py:191
  47.2 4.3 %all-to-all-start.3 = ((bf16[4,192,768]{2,1,0:T(8,128)(2,1)}), bf16[4,192,768]{2,1,0:T(8,128)(2,1)}, u32[]{:S(2)}, u32[]{:S(2)}) async-start(bf16[4,192,768]{2,1,0:T(8,128)(2,1)} %shard_map.95), calls=%async_computation.3 | async-start | bytes 2359296 | tf_op jit(solution)/shard_map/all_to_all | solution.py:191
  52.9 2.7 collective-permute-start.1
  55.6 9.4 %all-to-all-done.3.w_ref = bf16[4,192,768]{2,1,0:T(8,128)(2,1)} async-done(((bf16[4,192,768]{2,1,0:T(8,128)(2,1)}), bf16[4,192,768]{2,1,0:T(8,128)(2,1)}, u32[]{:S(2)}, u32[]{:S(2)}) %all-to-all-start.3) | async-done | bytes 1179680 | tf_op jit(solution)/shard_map/all_to_all | solution.py:191
  65.1 3.5 %all-to-all-start = ((bf16[4,192,768]{2,1,0:T(8,128)(2,1)}), bf16[4,192,768]{2,1,0:T(8,128)(2,1)S(1)}, u32[]{:S(2)}, u32[]{:S(2)}) async-start(bf16[4,192,768]{2,1,0:T(8,128)(2,1)} %copy-done.5), calls=%async_computation | async-start | bytes 2359296 | tf_op jit(solution)/shard_map/all_to_all | solution.py:191
  73.0 8.0 %shard_map.96 = (bf16[768,1024]{1,0:T(8,128)(2,1)S(1)}, bf16[1024,768]{1,0:T(8,128)(2,1)S(1)}) custom-call(bf16[4,4,192,128]{3,2,1,0:T(8,128)(2,1)} %bitcast.8.own_ref, bf16[4,4,192,128]{3,2,1,0:T(8,128)(2,1)S(1)} %copy-done.14, bf16[1024,1024]{1,0:T(8,128)(2,1)} %fusion.1.p_ref, bf16[4,192,768]{2,1,0:T(8,128)(2,1)} %all-to-all-done.3.w_ref), custom_call_target="tpu_custom_call" | custom-call | tf_op jit(solution)/shard_map/pallas_call | solution.py:69
  82.2 7.8 %shard_map.94 = (bf16[768,1024]{1,0:T(8,128)(2,1)S(1)}, bf16[1024,768]{1,0:T(8,128)(2,1)S(1)}) custom-call(bf16[4,4,192,128]{3,2,1,0:T(8,128)(2,1)} %bitcast.1.own_ref, bf16[4,4,192,128]{3,2,1,0:T(8,128)(2,1)S(1)} %collective-permute-done.oth_ref, bf16[1024,1024]{1,0:T(8,128)(2,1)} %fusion.1.p_ref, bf16[4,192,768]{2,1,0:T(8,128)(2,1)S(1)} %all-to-all-done.w_ref), custom_call_target="tpu_custom_call" | custom-call | tf_op jit(solution)/shard_map/pallas_call | solution.py:69
  93.0 48.5 %reduce-scatter.2.cloned.1.call-done = bf16[1,256,768]{2,1,0:T(8,128)(2,1)} async-done(((bf16[8,256,768]{2,1,0:T(8,128)(2,1)}), bf16[1,256,768]{2,1,0:T(8,128)(2,1)}) %reduce-scatter.2.cloned.1.call-update) | async-done | bytes 393232 | tf_op jit(solution)/shard_map/reduce_scatter | solution.py:230
  143.5 46.6 %all-gather.3.cloned.1.call-done = bf16[16,128,768]{2,1,0:T(8,128)(2,1)} async-done(((bf16[2,128,768]{2,1,0:T(8,128)(2,1)}), bf16[16,128,768]{2,1,0:T(8,128)(2,1)}) %all-gather.3.cloned.1.call-update) | async-done | bytes 3145744 | tf_op jit(solution)/shard_map/all_gather | solution.py:234
  192.5 3.8 %shard_map.97 = (bf16[768,768]{1,0:T(8,128)(2,1)}, f32[8,128]{1,0:T(8,128)S(1)}) custom-call(bf16[768,1024]{1,0:T(8,128)(2,1)S(1)} %copy-done.11, bf16[1024,768]{1,0:T(8,128)(2,1)S(1)} %bitcast.70), custom_call_target="tpu_custom_call" | custom-call | tf_op jit(solution)/shard_map/pallas_call | solution.py:122
  196.3 3.0 %shard_map.98 = (bf16[768,768]{1,0:T(8,128)(2,1)S(1)}, f32[8,128]{1,0:T(8,128)S(1)}) custom-call(bf16[768,1024]{1,0:T(8,128)(2,1)S(1)} %copy-done.9, bf16[1024,768]{1,0:T(8,128)(2,1)S(1)} %bitcast.74), custom_call_target="tpu_custom_call" | custom-call | tf_op jit(solution)/shard_map/pallas_call | solution.py:122
  200.5 4.3 %all-to-all-start.6 = ((bf16[4,192,768]{2,1,0:T(8,128)(2,1)}), bf16[4,192,768]{2,1,0:T(8,128)(2,1)}, u32[]{:S(2)}, u32[]{:S(2)}) async-start(bf16[4,192,768]{2,1,0:T(8,128)(2,1)} %bitcast.77), calls=%async_computation.7 | async-start | bytes 2359296 | tf_op jit(solution)/shard_map/all_to_all | solution.py:191
  204.9 7.1 %shard_map.99 = bf16[2,4,4,208,128]{4,3,2,1,0:T(8,128)(2,1)S(1)} custom-call(bf16[4,192,768]{2,1,0:T(8,128)(2,1)S(1)} %all-to-all-done.w_ref, bf16[1024,768]{1,0:T(8,128)(2,1)S(1)} %bitcast.71, bf16[1024,1024]{1,0:T(8,128)(2,1)} %fusion.1.p_ref, bf16[16,128]{1,0:T(8,128)(2,1)S(1)} %pad_select_fusion.n_ref), custom_call_target="tpu_custom_call" | custom-call | tf_op jit(solution)/shard_map/pallas_call | solution.py:152
  215.1 5.3 %all-to-all-done.6.g_ref = bf16[4,192,768]{2,1,0:T(8,128)(2,1)} async-done(((bf16[4,192,768]{2,1,0:T(8,128)(2,1)}), bf16[4,192,768]{2,1,0:T(8,128)(2,1)}, u32[]{:S(2)}, u32[]{:S(2)}) %all-to-all-start.6) | async-done | bytes 1179680 | tf_op jit(solution)/shard_map/all_to_all | solution.py:191
  220.5 3.5 %all-to-all-start.5 = ((bf16[4,192,768]{2,1,0:T(8,128)(2,1)}), bf16[4,192,768]{2,1,0:T(8,128)(2,1)S(1)}, u32[]{:S(2)}, u32[]{:S(2)}) async-start(bf16[4,192,768]{2,1,0:T(8,128)(2,1)} %bitcast.23), calls=%async_computation.6 | async-start | bytes 2359296 | tf_op jit(solution)/shard_map/all_to_all | solution.py:191
  224.0 2.7 fusion.2
  226.7 11.9 %all-to-all-done.5.g_ref = bf16[4,192,768]{2,1,0:T(8,128)(2,1)S(1)} async-done(((bf16[4,192,768]{2,1,0:T(8,128)(2,1)}), bf16[4,192,768]{2,1,0:T(8,128)(2,1)S(1)}, u32[]{:S(2)}, u32[]{:S(2)}) %all-to-all-start.5) | async-done | bytes 1179680 | tf_op jit(solution)/shard_map/all_to_all | solution.py:191
  238.6 4.7 %all-to-all-start.4 = ((bf16[16,208,128]{2,1,0:T(8,128)(2,1)}), bf16[16,208,128]{2,1,0:T(8,128)(2,1)}, u32[]{:S(2)}, u32[]{:S(2)}) async-start(bf16[16,208,128]{2,1,0:T(8,128)(2,1)} %bitcast.78), calls=%async_computation.5 | async-start | bytes 1703936 | tf_op jit(solution)/shard_map/all_to_all | solution.py:191
  244.1 3.9 %shard_map.101 = f32[192,3072]{1,0:T(8,128)} custom-call(f32[1]{0:T(128)S(6)} %copy.15.rate_ref, f32[192,3072]{1,0:T(8,128)S(1)} %bitcast.73, bf16[4,192,768]{2,1,0:T(8,128)(2,1)} %all-to-all-done.6.g_ref), custom_call_target="tpu_custom_call" | custom-call | tf_op jit(solution)/shard_map/pallas_call | solution.py:171
  250.1 5.6 %all-to-all-done.4 = bf16[16,208,128]{2,1,0:T(8,128)(2,1)} async-done(((bf16[16,208,128]{2,1,0:T(8,128)(2,1)}), bf16[16,208,128]{2,1,0:T(8,128)(2,1)}, u32[]{:S(2)}, u32[]{:S(2)}) %all-to-all-start.4) | async-done | bytes 852000 | tf_op jit(solution)/shard_map/all_to_all | solution.py:191
  257.6 4.8 %all-to-all-start.7 = ((f32[8,8,8]{2,1,0:T(8,128)}), f32[8,8,8]{2,1,0:T(8,128)S(1)}, u32[]{:S(2)}, u32[]{:S(2)}) async-start(f32[8,8,8]{2,1,0:T(8,128)} %broadcast_in_dim.30), calls=%async_computation.8 | async-start | bytes 65536 | tf_op jit(solution)/shard_map/all_to_all | solution.py:191
  263.1 6.3 %all-to-all-done.7 = f32[8,8,8]{2,1,0:T(8,128)S(1)} async-done(((f32[8,8,8]{2,1,0:T(8,128)}), f32[8,8,8]{2,1,0:T(8,128)S(1)}, u32[]{:S(2)}, u32[]{:S(2)}) %all-to-all-start.7) | async-done | bytes 2080 | tf_op jit(solution)/shard_map/all_to_all | solution.py:191
  (77 shorter events, 27.6 us)
Async XLA Ops:
  7.2 22.1 %copy-start.15 = (bf16[128,192]{0,1:T(8,128)(2,1)S(1)}, bf16[128,192]{0,1:T(8,128)(2,1)}, u32[]{:S(2)}) copy-start(bf16[128,192]{0,1:T(8,128)(2,1)} %param.6) | copy-start | bytes 147460
  8.1 26.5 %copy-start = (f32[3072,192]{0,1:T(8,128)S(1)}, f32[3072,192]{0,1:T(8,128)}, u32[]{:S(2)}) copy-start(f32[3072,192]{0,1:T(8,128)} %param.11) | copy-start | bytes 7077892
  30.3 16.9 %all-to-all-start.1 = ((bf16[16,192,128]{2,1,0:T(8,128)(2,1)}), bf16[16,192,128]{2,1,0:T(8,128)(2,1)}, u32[]{:S(2)}, u32[]{:S(2)}) async-start(bf16[16,192,128]{2,1,0:T(8,128)(2,1)} %broadcast_in_dim.26), calls=%async_computation.1 | async-start | bytes 1572864 | tf_op jit(solution)/shard_map/all_to_all | solution.py:191
  36.3 15.2 %copy-start.2 = (f32[192,3072]{1,0:T(8,128)S(1)}, f32[192,3072]{1,0:T(8,128)}, u32[]{:S(2)}) copy-start(f32[192,3072]{1,0:T(8,128)} %w_ref.3) | copy-start | bytes 7077892
  47.2 17.9 %all-to-all-start.3 = ((bf16[4,192,768]{2,1,0:T(8,128)(2,1)}), bf16[4,192,768]{2,1,0:T(8,128)(2,1)}, u32[]{:S(2)}, u32[]{:S(2)}) async-start(bf16[4,192,768]{2,1,0:T(8,128)(2,1)} %shard_map.95), calls=%async_computation.3 | async-start | bytes 2359296 | tf_op jit(solution)/shard_map/all_to_all | solution.py:191
  52.9 15.8 %copy-start.16 = (s32[1024]{0:T(1024)S(1)}, s32[1024]{0:T(1024)}, u32[]{:S(2)}) copy-start(s32[1024]{0:T(1024)} %param.8) | copy-start | bytes 12292
  52.9 18.1 %collective-permute-start.1 = (bf16[4,4,192,128]{3,2,1,0:T(8,128)(2,1)}, bf16[4,4,192,128]{3,2,1,0:T(8,128)(2,1)S(1)}, u32[]{:S(2)}, u32[]{:S(2)}) collective-permute-start(bf16[4,4,192,128]{3,2,1,0:T(8,128)(2,1)} %bitcast.8.own_ref), channel_id=1, source_target_pairs={{0,1},{1,0},{2,3},{3,2},{4,5},{5,4},{6,7},{7,6},{8,9},{9,8},{10,11... | collective-permute-start | bytes 2359304 | tf_op jit(solution)/shard_map/ppermute | solution.py:195
  55.6 26.5 %collective-permute-start = (bf16[4,4,192,128]{3,2,1,0:T(8,128)(2,1)}, bf16[4,4,192,128]{3,2,1,0:T(8,128)(2,1)S(1)}, u32[]{:S(2)}, u32[]{:S(2)}) collective-permute-start(bf16[4,4,192,128]{3,2,1,0:T(8,128)(2,1)} %bitcast.1.own_ref), channel_id=1, source_target_pairs={{0,1},{1,0},{2,3},{3,2},{4,5},{5,4},{6,7},{7,6},{8,9},{9,8},{10,11... | collective-permute-start | bytes 2359304 | tf_op jit(solution)/shard_map/ppermute | solution.py:195
  65.1 17.1 %all-to-all-start = ((bf16[4,192,768]{2,1,0:T(8,128)(2,1)}), bf16[4,192,768]{2,1,0:T(8,128)(2,1)S(1)}, u32[]{:S(2)}, u32[]{:S(2)}) async-start(bf16[4,192,768]{2,1,0:T(8,128)(2,1)} %copy-done.5), calls=%async_computation | async-start | bytes 2359296 | tf_op jit(solution)/shard_map/all_to_all | solution.py:191
  68.6 72.8 %reduce-scatter.2.cloned.1.call-start = ((), (), s32[]{:S(2)}) async-start(), calls=%async_computation.9 | async-start | bytes 3538944 | tf_op jit(solution)/shard_map/reduce_scatter | solution.py:230
  81.0 1.2 copy-start.8
  93.0 97.2 %all-gather.3.cloned.1.call-start = ((), (), s32[]{:S(2)}) async-start(), calls=%async_computation.10 | async-start | bytes 3538944 | tf_op jit(solution)/shard_map/all_gather | solution.py:234
  190.1 2.4 copy-start.11
  192.4 3.9 %copy-start.9 = (bf16[768,1024]{1,0:T(8,128)(2,1)S(1)}, bf16[768,1024]{1,0:T(8,128)(2,1)}, u32[]{:S(2)}) copy-start(bf16[768,1024]{1,0:T(8,128)(2,1)} %copy-done.8) | copy-start | bytes 4718596
  200.5 19.9 %all-to-all-start.6 = ((bf16[4,192,768]{2,1,0:T(8,128)(2,1)}), bf16[4,192,768]{2,1,0:T(8,128)(2,1)}, u32[]{:S(2)}, u32[]{:S(2)}) async-start(bf16[4,192,768]{2,1,0:T(8,128)(2,1)} %bitcast.77), calls=%async_computation.7 | async-start | bytes 2359296 | tf_op jit(solution)/shard_map/all_to_all | solution.py:191
  212.1 1.2 copy-start.4
  214.2 9.8 %collective-permute-start.2 = (bf16[4,4,208,128]{3,2,1,0:T(8,128)(2,1)}, bf16[4,4,208,128]{3,2,1,0:T(8,128)(2,1)}, u32[]{:S(2)}, u32[]{:S(2)}) collective-permute-start(bf16[4,4,208,128]{3,2,1,0:T(8,128)(2,1)} %slice_bitcast_fusion), channel_id=1, source_target_pairs={{0,1},{1,0},{2,3},{3,2},{4,5},{5,4},{6,7},{7,6},{8,9},{9,8},{10,11... | collective-permute-start | bytes 2555912 | tf_op jit(solution)/shard_map/ppermute | solution.py:195
  220.5 18.2 %all-to-all-start.5 = ((bf16[4,192,768]{2,1,0:T(8,128)(2,1)}), bf16[4,192,768]{2,1,0:T(8,128)(2,1)S(1)}, u32[]{:S(2)}, u32[]{:S(2)}) async-start(bf16[4,192,768]{2,1,0:T(8,128)(2,1)} %bitcast.23), calls=%async_computation.6 | async-start | bytes 2359296 | tf_op jit(solution)/shard_map/all_to_all | solution.py:191
  224.0 20.0 %copy-start.1 = (f32[3072,192]{0,1:T(8,128)S(1)}, f32[3072,192]{0,1:T(8,128)}, u32[]{:S(2)}) copy-start(f32[3072,192]{0,1:T(8,128)} %param.11) | copy-start | bytes 7077892
  238.6 4.7 %copy-start.6 = (bf16[4,192,768]{2,1,0:T(8,128)(2,1)}, bf16[4,192,768]{2,1,0:T(8,128)(2,1)S(1)}, u32[]{:S(2)}) copy-start(bf16[4,192,768]{2,1,0:T(8,128)(2,1)S(1)} %all-to-all-done.5.g_ref) | copy-start | bytes 3538948
  238.6 17.0 %all-to-all-start.4 = ((bf16[16,208,128]{2,1,0:T(8,128)(2,1)}), bf16[16,208,128]{2,1,0:T(8,128)(2,1)}, u32[]{:S(2)}, u32[]{:S(2)}) async-start(bf16[16,208,128]{2,1,0:T(8,128)(2,1)} %bitcast.78), calls=%async_computation.5 | async-start | bytes 1703936 | tf_op jit(solution)/shard_map/all_to_all | solution.py:191
  244.0 4.0 %copy-start.3 = (f32[192,3072]{1,0:T(8,128)S(1)}, f32[192,3072]{1,0:T(8,128)}, u32[]{:S(2)}) copy-start(f32[192,3072]{1,0:T(8,128)} %w_ref.3) | copy-start | bytes 7077892
  244.0 4.0 %copy-start.7 = (bf16[4,192,768]{2,1,0:T(8,128)(2,1)S(1)}, bf16[4,192,768]{2,1,0:T(8,128)(2,1)}, u32[]{:S(2)}) copy-start(bf16[4,192,768]{2,1,0:T(8,128)(2,1)} %copy-done.6) | copy-start | bytes 3538948
  257.6 11.7 %all-to-all-start.7 = ((f32[8,8,8]{2,1,0:T(8,128)}), f32[8,8,8]{2,1,0:T(8,128)S(1)}, u32[]{:S(2)}, u32[]{:S(2)}) async-start(f32[8,8,8]{2,1,0:T(8,128)} %broadcast_in_dim.30), calls=%async_computation.8 | async-start | bytes 65536 | tf_op jit(solution)/shard_map/all_to_all | solution.py:191
  (5 other events, 5.2 us)
Sparse Core Ops, SparseCore 0:
  93.1 48.3 reduce-scatter.1
  143.6 46.4 all-gather.2

commit v2 on v0

v2 whole, which is shorter than its diff:
```python
import functools

import jax
import jax.numpy as jnp
from jax import lax
from jax.experimental import pallas as pl
from jax.experimental.pallas import tpu as pltpu
from jax.sharding import Mesh, PartitionSpec as P

D = 6144
FF = 24576
IMAGES = 8
TOK_IMG = 128
TOKENS = 1024
FEAT = 192
NY, NZ, NX = 4, 8, 4
HID = 768
SCALE_IN = D ** (-0.5)
SCALE_OUT = FF ** (-0.5)
NORM_ROWS = 16

root_half = 0.7071067811865476
inv_root_tau = 0.3989422804014327

f32 = jnp.float32
bf16 = jnp.bfloat16
WIDE = HID + TOK_IMG
SENT = 2 * TOK_IMG + NORM_ROWS
BIG = pltpu.CompilerParams(vmem_limit_bytes=40 * 1024 * 1024)
VMEM = pl.BlockSpec(memory_space=pltpu.VMEM)
SMEM = pl.BlockSpec(memory_space=pltpu.SMEM)


def dot(left, right, dims):
    return lax.dot_general(left, right, (dims, ((), ())), preferred_element_type=f32)


def split_hidden(in_weight, out_weight_t):
    def body(a_ref, b_ref, o_ref):
        o_ref[0, 0] = a_ref[...].astype(bf16)
        o_ref[0, 1] = b_ref[...].astype(bf16)

    return pl.pallas_call(
        body,
        grid=(NY,),
        in_specs=[pl.BlockSpec((FEAT, HID), lambda i: (0, i))] * 2,
        out_specs=pl.BlockSpec((1, 2, FEAT, HID), lambda i: (i, 0, 0, 0)),
        out_shape=jax.ShapeDtypeStruct((NY, 2, FEAT, HID), bf16),
        compiler_params=BIG,
    )(in_weight, out_weight_t)


def behind(mine, step, size):
    return lax.rem(mine - step + size, size)


def sort_tokens(here, own, other, order):
    def body(here_ref, *refs):
        pieces, (p_ref, x_ref, t_ref, pair_ref, rows) = refs[:8], refs[8:]
        for s in range(NY):
            at = pl.multiple_of(behind(here_ref[0], s, NY) * FEAT, FEAT)
            for u in range(NX):
                x = behind(here_ref[2], u, NX)
                for o in range(2):
                    core = here_ref[3] if o == 0 else 1 - here_ref[3]
                    lane = pl.multiple_of((x * 2 + core) * 128, 128)
                    for a in range(2):
                        rows[a, pl.ds(at, FEAT), pl.ds(lane, 128)] = pieces[o * NX + u][s, a]
        tile = 2 * TOK_IMG
        for a in range(2):

            def one(t, carry, a=a):
                at = pl.multiple_of(t * tile, tile)
                ordered = dot(rows[a], p_ref[:, pl.ds(at, tile)], ((1,), (0,))).astype(bf16)
                x_ref[a, :, pl.ds(at, tile)] = ordered
                turned = ordered.T
                t_ref[a, pl.ds(at, tile), :] = turned
                for k in range(2):
                    image = slice(k * TOK_IMG, (k + 1) * TOK_IMG)
                    pairs = dot(turned[image], ordered[:, image], ((1,), (0,)))
                    pair_ref[2 * t + k, a * TOK_IMG : (a + 1) * TOK_IMG, :] = pairs.astype(bf16)
                return carry

            lax.fori_loop(0, TOKENS // tile, one, 0)

    return pl.pallas_call(
        body,
        in_specs=[SMEM] + [VMEM] * 9,
        out_specs=[VMEM] * 3,
        out_shape=[
            jax.ShapeDtypeStruct((2, NY * FEAT, TOKENS), bf16),
            jax.ShapeDtypeStruct((2, TOKENS, NY * FEAT), bf16),
            jax.ShapeDtypeStruct((IMAGES, 2 * TOK_IMG, TOK_IMG), bf16),
        ],
        scratch_shapes=[pltpu.VMEM((2, NY * FEAT, TOKENS), bf16)],
        compiler_params=BIG,
    )(here, *own, *other, order)


def project(rows, pairs, weights):
    def body(r_ref, p_ref, w_ref, o_ref):
        tile = 2 * TOK_IMG
        o_ref[:, :, HID:] = p_ref[...]
        for a, scale in enumerate((SCALE_IN, SCALE_OUT)):
            weight = w_ref[:, a].reshape(NY * FEAT, HID)

            def one(t, carry, a=a, scale=scale, weight=weight):
                at = pl.multiple_of(t * tile, tile)
                prod = dot(r_ref[a, pl.ds(at, tile), :], weight, ((1,), (0,)))
                prod = (prod * scale).astype(bf16).reshape(2, TOK_IMG, HID)
                o_ref[pl.ds(2 * t, 2), a * TOK_IMG : (a + 1) * TOK_IMG, 0:HID] = prod
                return carry

            lax.fori_loop(0, TOKENS // tile, one, 0)

    return pl.pallas_call(
        body,
        in_specs=[VMEM] * 3,
        out_specs=VMEM,
        out_shape=jax.ShapeDtypeStruct((IMAGES, 2 * TOK_IMG, WIDE), bf16),
        compiler_params=BIG,
    )(rows, pairs, weights)


def activate(here, summed):
    def body(here_ref, s_ref, o_ref):
        pre = s_ref[0:TOK_IMG, 0:HID].astype(f32)
        act, slope = gelu_and_slope(pre)
        act = act.astype(bf16)
        hid = (s_ref[TOK_IMG:, 0:HID].astype(f32) * slope).astype(bf16)
        o_ref[0:TOK_IMG, :] = act
        o_ref[TOK_IMG : 2 * TOK_IMG, :] = hid
        pairs = s_ref[:, HID:].astype(f32)
        both = dot(hid, hid, ((1,), (1,))) * pairs[0:TOK_IMG] * (SCALE_IN * SCALE_IN)
        both += dot(act, act, ((1,), (1,))) * pairs[TOK_IMG:] * (SCALE_OUT * SCALE_OUT)
        square = jnp.sum(jnp.sum(both, axis=0, keepdims=True), axis=1, keepdims=True)
        high = square.astype(bf16).astype(f32)
        middle = (square - high).astype(bf16).astype(f32)
        low = square - high - middle
        source = (here_ref[0] * NX + here_ref[2]) * 2 + here_ref[3]
        spot = lax.rem(source, 16) * IMAGES + here_ref[1]
        row = lax.broadcasted_iota(jnp.int32, (NORM_ROWS, 128), 0)
        lane = lax.broadcasted_iota(jnp.int32, (NORM_ROWS, 128), 1)
        kind = row - lax.div(source, 16) * 3
        value = jnp.where(kind == 0, high, jnp.where(kind == 1, middle, low))
        kept = (lane == spot) & (kind >= 0) & (kind < 3)
        o_ref[2 * TOK_IMG :, :] = jnp.zeros((NORM_ROWS, HID), bf16)
        o_ref[2 * TOK_IMG :, 0:128] = jnp.where(kept, value, 0.0).astype(bf16)

    return pl.pallas_call(
        body,
        in_specs=[SMEM, VMEM],
        out_specs=VMEM,
        out_shape=jax.ShapeDtypeStruct((SENT, HID), bf16),
        compiler_params=BIG,
    )(here, summed)


def weight_grads(feats, every):
    def body(x_ref, e_ref, g_ref):
        tile = 256
        for w, scale in enumerate((SCALE_IN, SCALE_OUT)):
            rows = slice((1 - w) * TOK_IMG, (2 - w) * TOK_IMG)
            for n in range(HID // tile):
                cols = slice(n * tile, (n + 1) * tile)
                hidden = e_ref[:, rows, cols].reshape(TOKENS, tile)
                grad = dot(x_ref[w], hidden, ((1,), (0,))) * scale
                g_ref[:, w, :, cols] = grad.astype(bf16).reshape(NY, FEAT, tile)

    return pl.pallas_call(
        body,
        in_specs=[VMEM] * 2,
        out_specs=VMEM,
        out_shape=jax.ShapeDtypeStruct((NY, 2, FEAT, HID), bf16),
        compiler_params=BIG,
    )(feats, every)


def input_grads(here, weights, every, order):
    def body(here_ref, w_ref, e_ref, p_ref, own_ref, oth_ref):
        tile = 2 * TOK_IMG
        hidden = e_ref[:, TOK_IMG : 2 * TOK_IMG, :].reshape(TOKENS, HID)
        weight = w_ref[:, 0].reshape(NY * FEAT, HID)
        norms = e_ref[0, 2 * TOK_IMG :, 0:128].astype(f32)
        for b in range(1, IMAGES):
            norms += e_ref[b, 2 * TOK_IMG :, 0:128].astype(f32)
        norms = norms.astype(bf16)

        def one(x, carry):
            at = pl.multiple_of(x * tile, tile)
            rows = dot(p_ref[pl.ds(at, tile), :], hidden, ((1,), (0,))).astype(bf16)
            grad = (dot(weight, rows, ((1,), (1,))) * SCALE_IN).astype(bf16)
            left, right = grad[:, :128], grad[:, 128:]
            u = lax.rem(x - here_ref[2] + NX, NX)
            for core in range(2):

                @pl.when(here_ref[3] == core)
                def _():
                    halves = (left, right) if core == 0 else (right, left)
                    for ref, half in zip((own_ref, oth_ref), halves):
                        for y in range(NY):
                            v = lax.rem(y - here_ref[0] + NY, NY)
                            ref[u, v, 0:FEAT, :] = half[y * FEAT : (y + 1) * FEAT]
                            ref[u, v, FEAT:, :] = norms

            return carry

        lax.fori_loop(0, NX, one, 0)

    return pl.pallas_call(
        body,
        in_specs=[SMEM] + [VMEM] * 3,
        out_specs=[VMEM] * 2,
        out_shape=[jax.ShapeDtypeStruct((NX, NY, FEAT + NORM_ROWS, 128), bf16)] * 2,
        compiler_params=BIG,
    )(here, weights, every, order)


def update(rate, in_weight, out_weight_t, grads):
    def body(rate_ref, a_ref, b_ref, g_ref, a_out, b_out):
        a_out[...] = a_ref[...] - rate_ref[0] * g_ref[0, 0].astype(f32)
        b_out[...] = b_ref[...] - rate_ref[0] * g_ref[0, 1].astype(f32)

    block = pl.BlockSpec((FEAT, HID), lambda i: (0, i))
    return pl.pallas_call(
        body,
        grid=(NY,),
        in_specs=[
            pl.BlockSpec(memory_space=pltpu.SMEM),
            block,
            block,
            pl.BlockSpec((1, 2, FEAT, HID), lambda i: (i, 0, 0, 0)),
        ],
        out_specs=[block, block],
        out_shape=[jax.ShapeDtypeStruct(in_weight.shape, f32)] * 2,
        compiler_params=BIG,
    )(rate, in_weight, out_weight_t, grads)


def behind(mine, step, size):
    return lax.rem(mine - step + size, size)


def gelu_and_slope(pre):
    phi = 0.5 * (1.0 + lax.erf(pre * root_half))
    return pre * phi, phi + pre * jnp.exp(-0.5 * pre * pre) * inv_root_tau


def exchange(value, axes):
    return lax.all_to_all(value, axes, 0, 0, tiled=True)


def swap_cores(value):
    return lax.ppermute(value, "core", [(0, 1), (1, 0)])


def ahead(value, axis, step):
    return lax.ppermute(value, axis, [(i, (i + step) % 4) for i in range(4)])


def ring_gather(value, axis):
    near, back, far = ahead(value, axis, 1), ahead(value, axis, 3), ahead(value, axis, 2)
    return [value, near, far, back]


def token_order(image_ids):
    at = jnp.arange(TOKENS)
    same = (image_ids[:, None] == image_ids[None, :]) & (at[None, :] < at[:, None])
    place = image_ids * TOK_IMG + jnp.sum(same.astype(jnp.int32), axis=1)
    return (place[:, None] == at[None, :]).astype(bf16)


def ring_sum(chunks, axis):
    total = chunks[0].astype(f32)
    for s in (1, 3, 2):
        total += ahead(chunks[s], axis, s).astype(f32)
    return total


def shards(tokens, out_grad, image_ids, learn_rate, in_weight, out_weight):
    here = jnp.stack([lax.axis_index(a) for a in ("y", "z", "x", "core")]).astype(jnp.int32)
    out_weight_t = out_weight.T
    halves = split_hidden(in_weight, out_weight_t)
    along_y = jnp.stack(ring_gather(jnp.stack([tokens.T, out_grad.T]), "y"))
    halves, along_y = lax.optimization_barrier((halves, along_y))
    weights = exchange(halves.reshape(NY * 2 * FEAT, HID), "y").reshape(NY, 2, FEAT, HID)
    own = ring_gather(along_y, "x")
    other = [swap_cores(piece) for piece in own]
    order = token_order(image_ids)
    feats, rows, pairs = sort_tokens(here, own, other, order)
    parts = project(rows, pairs, weights)
    summed = lax.psum_scatter(parts, "z", scatter_dimension=0)
    every = lax.all_gather(activate(here, summed), "z")
    grads = weight_grads(feats, every)
    mine, theirs = input_grads(here, weights, every, order)
    grads = exchange(grads.reshape(NY * 2 * FEAT, HID), "y").reshape(NY, 2, FEAT, HID)
    merged = (mine.astype(f32) + swap_cores(theirs).astype(f32)).astype(bf16)
    along_x = ring_sum(merged, "x").astype(bf16)
    got = ring_sum(along_x, "y")
    input_grad = got[:FEAT].astype(bf16).T
    example_sq = jnp.sum(got[FEAT:].reshape(NORM_ROWS * 16, IMAGES), axis=0)
    example_norm = 0.5 * jnp.log(example_sq + 1e-06)
    in_next, out_next = update(learn_rate, in_weight, out_weight_t, grads)
    return (input_grad, in_next, out_next.T, example_norm)


def solution(mesh):
    chips = Mesh(mesh.devices.reshape(NY, NZ, NX, 2), ("y", "z", "x", "core"))
    row, col = ("y", "z"), ("x", "core")
    placed = (P(col, row), P(col, row), P(), P(), P(row, col), P(col, row))
    return jax.shard_map(
        shards,
        mesh=chips,
        in_specs=placed,
        out_specs=(P(col, row), P(row, col), P(col, row), P()),
        check_vma=False,
    )
```

time: 851 us -> 239 us (0.28)
  waiting for transfers between devices: 569 us -> 129 us
  blocking collectives: 104 us -> 0 us
  matrix products: 79.5 us -> 0 us
  starting transfers between devices: 0.38 us -> 36.7 us
  Pallas kernels: 0 us -> 31.2 us
  local copies, waits for them, and re-layouts: 46.8 us -> 22.1 us
  other arithmetic: 26.8 us -> 4.15 us
  loops' own time: 8.98 us -> 0 us
    reduce_scatter x2 -> x1, waiting for transfers between devices: 430 us -> 52.1 us  [shards(): summed = lax.psum_scatter(parts, 'z', scatter_dimension=0)]
    all_gather x2 -> x1, waiting for transfers between devices: 139 us -> 45.9 us  [shards(): every = lax.all_gather(activate(here, summed), 'z')]
    dot_general x19 -> x0, matrix products: 79.5 us -> none  [the longest x16 63.2 us: contract_rows(): lax.dot_general(left, right, (((0,), (0,)), ((), ())), preferred_element_...]
    psum x1 -> x0, blocking collectives: 74.8 us -> none  [shards(): example_sq = lax.psum(local_sums, ('row', 'col'))]
    gather x4 -> x0, local copies, waits for them, and re-layouts: 41.5 us -> none  [by_image(): jnp.take(rows, order, axis=0).reshape(image_count, TOK_IMG, rows.shape[1])]
    pallas_call x0 -> x7, Pallas kernels: none -> 31.2 us  [the longest x1 10.2 us: sort_tokens(): pl.pallas_call(body, in_specs=[SMEM] + [VMEM] * 9, out_specs=[VMEM] * 3,...]
    ppermute x0 -> x17, waiting for transfers between devices: none -> 30.9 us  [the longest x12 29.3 us: ahead(): return lax.ppermute(value, axis, [(i, (i + step) % 4) for i in range(4)])]
    all_gather x2 -> x0, blocking collectives: 29.3 us -> none  [the longest x1 16.2 us: shards(): lax.all_gather(tokens, 'col', axis=0, tiled=True)]
  transfers between devices with their start and end apart: 5 -> 21, of which waited for: 4 -> 10; matrix products, arithmetic and copies ran while one was open for 17% -> 2% of each run, Pallas kernels for 0% -> 6%
where the time goes in v2:
time: 239 us; the launch traced here: 238 us
  waiting for transfers between devices  129 us (54%)
  starting transfers between devices  36.7 us (15%)
  Pallas kernels  31.2 us (13%)
  local copies, waits for them, and re-layouts  22.1 us (9%)
  between operations  14.9 us (6%)
  other arithmetic  4.15 us (2%)
    reduce_scatter x1, waiting for transfers between devices, shards(): summed = lax.psum_scatter(parts, 'z', scatter_dimension=0)  52.1 us
    all_gather x1, waiting for transfers between devices, shards(): every = lax.all_gather(activate(here, summed), 'z')  45.9 us
    ppermute x12, waiting for transfers between devices, ahead(): return lax.ppermute(value, axis, [(i, (i + step) % 4) for i in range(4)])  29.3 us
    unnamed x38, local copies, waits for them, and re-layouts  21.3 us
    ppermute x12, starting transfers between devices, ahead(): return lax.ppermute(value, axis, [(i, (i + step) % 4) for i in range(4)])  19.2 us
    pallas_call x1, Pallas kernels, sort_tokens(): pl.pallas_call(body, in_specs=[SMEM] + [VMEM] * 9, out_specs=[VMEM] * 3,...  10.2 us
    ppermute x5, starting transfers between devices, swap_cores(): return lax.ppermute(value, 'core', [(0, 1), (1, 0)])  9.18 us
    all_to_all x2, starting transfers between devices, exchange(): return lax.all_to_all(value, axes, 0, 0, tiled=True)  8.14 us
  transfers between devices with their start and end apart: 21, of which 10 were waited for; matrix products, arithmetic and copies ran while one was open for 2% of the time, Pallas kernels for 6%

profile of v2, /device:TPU:1, one launch (start us, length us, event | category | flops | bytes accessed | tf_op | source)
XLA Modules:
  0.0 237.9 jit_solution(7459808221764424402)
XLA Ops:
  8.0 2.2 collective-permute-start
  10.2 2.6 %collective-permute-start.1 = (bf16[2,192,128]{2,1,0:T(8,128)(2,1)S(1)}, bf16[2,192,128]{2,1,0:T(8,128)(2,1)S(1)}, u32[]{:S(2)}, u32[]{:S(2)}) collective-permute-start(bf16[2,192,128]{2,1,0:T(8,128)(2,1)S(1)} %get-tuple-element.29), channel_id=1, source_target_pairs={{0,128},{64,192},{128,0},{192,64},{1,129},{65,193},{129,1},{193,65... | collective-permute-start | bytes 294920 | tf_op jit(solution)/shard_map/ppermute | solution.py:258
  19.4 3.6 %all-to-all-start = ((bf16[4,384,768]{2,1,0:T(8,128)(2,1)}), bf16[4,384,768]{2,1,0:T(8,128)(2,1)S(1)}, u32[]{:S(2)}, u32[]{:S(2)}) async-start(bf16[4,384,768]{2,1,0:T(8,128)(2,1)} %bitcast.53), calls=%async_computation | async-start | bytes 4718592 | tf_op jit(solution)/shard_map/all_to_all | solution.py:250
  24.4 2.5 %collective-permute-start.4 = (bf16[4,2,192,128]{3,2,1,0:T(8,128)(2,1)S(1)}, bf16[4,2,192,128]{3,2,1,0:T(8,128)(2,1)S(1)}, u32[]{:S(2)}, u32[]{:S(2)}) collective-permute-start(bf16[4,2,192,128]{3,2,1,0:T(8,128)(2,1)S(1)} %pad_maximum_fusion.refs_0_), channel_id=1, source_target_pairs={{0,4},{2,6},{4,0},{6,2},{1,5},{3,7},{5,1},{7,3},{8,12},{10,14},{12... | collective-permute-start | bytes 1179656 | tf_op jit(solution)/shard_map/ppermute | solution.py:258
  28.5 2.4 %collective-permute-start.6 = (bf16[4,2,192,128]{3,2,1,0:T(8,128)(2,1)S(1)}, bf16[4,2,192,128]{3,2,1,0:T(8,128)(2,1)}, u32[]{:S(2)}, u32[]{:S(2)}) collective-permute-start(bf16[4,2,192,128]{3,2,1,0:T(8,128)(2,1)S(1)} %pad_maximum_fusion.refs_0_), channel_id=1, source_target_pairs={{0,1},{1,0},{2,3},{3,2},{4,5},{5,4},{6,7},{7,6},{8,9},{9,8},{10,11... | collective-permute-start | bytes 1179656 | tf_op jit(solution)/shard_map/ppermute | solution.py:254
  30.9 2.5 %collective-permute-done.3.refs_1_ = bf16[4,2,192,128]{3,2,1,0:T(8,128)(2,1)S(1)} collective-permute-done((bf16[4,2,192,128]{3,2,1,0:T(8,128)(2,1)S(1)}, bf16[4,2,192,128]{3,2,1,0:T(8,128)(2,1)S(1)}, u32[]{:S(2)}, u32[]{:S(2)}) %collective-permute-start.3) | collective-permute-done | bytes 393248 | tf_op jit(solution)/shard_map/ppermute | solution.py:258
  33.4 3.5 %collective-permute-start.7 = (bf16[4,2,192,128]{3,2,1,0:T(8,128)(2,1)S(1)}, bf16[4,2,192,128]{3,2,1,0:T(8,128)(2,1)}, u32[]{:S(2)}, u32[]{:S(2)}) collective-permute-start(bf16[4,2,192,128]{3,2,1,0:T(8,128)(2,1)S(1)} %collective-permute-done.3.refs_1_), channel_id=1, source_target_pairs={{0,1},{1,0},{2,3},{3,2},{4,5},{5,4},{6,7},{7,6},{8,9},{9,8},{10,11... | collective-permute-start | bytes 1179656 | tf_op jit(solution)/shard_map/ppermute | solution.py:254
  36.9 5.9 %collective-permute-done.4.refs_2_ = bf16[4,2,192,128]{3,2,1,0:T(8,128)(2,1)S(1)} collective-permute-done((bf16[4,2,192,128]{3,2,1,0:T(8,128)(2,1)S(1)}, bf16[4,2,192,128]{3,2,1,0:T(8,128)(2,1)S(1)}, u32[]{:S(2)}, u32[]{:S(2)}) %collective-permute-start.4) | collective-permute-done | bytes 393248 | tf_op jit(solution)/shard_map/ppermute | solution.py:258
  42.9 2.4 %collective-permute-start.8 = (bf16[4,2,192,128]{3,2,1,0:T(8,128)(2,1)S(1)}, bf16[4,2,192,128]{3,2,1,0:T(8,128)(2,1)}, u32[]{:S(2)}, u32[]{:S(2)}) collective-permute-start(bf16[4,2,192,128]{3,2,1,0:T(8,128)(2,1)S(1)} %collective-permute-done.4.refs_2_), channel_id=1, source_target_pairs={{0,1},{1,0},{2,3},{3,2},{4,5},{5,4},{6,7},{7,6},{8,9},{9,8},{10,11... | collective-permute-start | bytes 1179656 | tf_op jit(solution)/shard_map/ppermute | solution.py:254
  49.5 10.2 %shard_map.94 = (bf16[2,768,1024]{2,1,0:T(8,128)(2,1)S(1)}, bf16[2,1024,768]{2,1,0:T(8,128)(2,1)S(1)}, bf16[8,256,128]{2,1,0:T(8,128)(2,1)S(1)}) custom-call(s32[4]{0:T(128)S(1)} %pad_add_fusion.here_ref, bf16[4,2,192,128]{3,2,1,0:T(8,128)(2,1)S(1)} %pad_maximum_fusion.refs_0_, bf16[4,2,192,128]{3,2,1,0:T(8,128)(2,1)S(1)} %copy-done.15, ...), custom_call_target="tpu_custom_call" | custom-call | tf_op jit(solution)/shard_map/pallas_call | solution.py:86
  64.4 1.9 copy-done.12
  66.3 4.1 %shard_map.95 = bf16[8,256,896]{2,1,0:T(8,128)(2,1)S(1)} custom-call(bf16[2,1024,768]{2,1,0:T(8,128)(2,1)S(1)} %copy-done.12, bf16[8,256,128]{2,1,0:T(8,128)(2,1)S(1)} %get-tuple-element.16.p_ref, bf16[4,2,192,768]{3,2,1,0:T(8,128)(2,1)S(1)} %bitcast.47), custom_call_target="tpu_custom_call" | custom-call | tf_op jit(solution)/shard_map/pallas_call | solution.py:116
  70.4 1.8 copy-done.2
  72.4 52.1 %reduce-scatter.2.cloned.1.call-done = bf16[1,256,896]{2,1,0:T(8,128)(2,1)} async-done(((bf16[8,256,896]{2,1,0:T(8,128)(2,1)}), bf16[1,256,896]{2,1,0:T(8,128)(2,1)}) %reduce-scatter.2.cloned.1.call-update) | async-done | bytes 458768 | tf_op jit(solution)/shard_map/reduce_scatter | solution.py:292
  125.5 1.8 shard_map.96
  127.3 45.9 %all-gather.3.cloned.1.call-done = bf16[2176,768]{1,0:T(8,128)(2,1)} async-done(((bf16[272,768]{1,0:T(8,128)(2,1)}), bf16[2176,768]{1,0:T(8,128)(2,1)}) %all-gather.3.cloned.1.call-update) | async-done | bytes 3342352 | tf_op jit(solution)/shard_map/all_gather | solution.py:293
  174.9 1.9 copy-done.3
  176.8 6.0 %shard_map.97 = (bf16[4,4,208,128]{3,2,1,0:T(8,128)(2,1)S(1)}, bf16[4,4,208,128]{3,2,1,0:T(8,128)(2,1)}) custom-call(s32[4]{0:T(128)S(1)} %pad_add_fusion.here_ref, bf16[4,2,192,768]{3,2,1,0:T(8,128)(2,1)S(1)} %bitcast.48, bf16[8,272,768]{2,1,0:T(8,128)(2,1)S(1)} %bitcast.49, bf16[1024,1024]{1,0:T(8,128)(2,1)S(1)} %copy-done.1), custom_call_target="tpu_custom_call" | custom-call | tf_op jit(solution)/shard_map/pallas_call | solution.py:210
  183.5 4.0 %shard_map.98 = bf16[4,2,192,768]{3,2,1,0:T(8,128)(2,1)} custom-call(bf16[2,768,1024]{2,1,0:T(8,128)(2,1)S(1)} %copy-done.10, bf16[8,272,768]{2,1,0:T(8,128)(2,1)S(1)} %bitcast.50), custom_call_target="tpu_custom_call" | custom-call | tf_op jit(solution)/shard_map/pallas_call | solution.py:170
  187.5 4.5 %all-to-all-start.1 = ((bf16[4,384,768]{2,1,0:T(8,128)(2,1)}), bf16[4,384,768]{2,1,0:T(8,128)(2,1)}, u32[]{:S(2)}, u32[]{:S(2)}) async-start(bf16[4,384,768]{2,1,0:T(8,128)(2,1)} %bitcast.26), calls=%async_computation.2 | async-start | bytes 4718592 | tf_op jit(solution)/shard_map/all_to_all | solution.py:250
  197.9 4.0 %collective-permute-done.11 = bf16[4,208,128]{2,1,0:T(8,128)(2,1)S(1)} collective-permute-done((bf16[4,208,128]{2,1,0:T(8,128)(2,1)S(1)}, bf16[4,208,128]{2,1,0:T(8,128)(2,1)S(1)}, u32[]{:S(2)}, u32[]{:S(2)}) %collective-permute-start.11) | collective-permute-done | bytes 213024 | tf_op jit(solution)/shard_map/ppermute | solution.py:258
  201.9 5.4 %collective-permute-done.13 = bf16[4,208,128]{2,1,0:T(8,128)(2,1)S(1)} collective-permute-done((bf16[4,208,128]{2,1,0:T(8,128)(2,1)S(1)}, bf16[4,208,128]{2,1,0:T(8,128)(2,1)S(1)}, u32[]{:S(2)}, u32[]{:S(2)}) %collective-permute-start.13) | collective-permute-done | bytes 213024 | tf_op jit(solution)/shard_map/ppermute | solution.py:258
  212.2 10.7 %collective-permute-done.14 = bf16[208,128]{1,0:T(8,128)(2,1)S(1)} collective-permute-done((bf16[208,128]{1,0:T(8,128)(2,1)S(1)}, bf16[208,128]{1,0:T(8,128)(2,1)S(1)}, u32[]{:S(2)}, u32[]{:S(2)}) %collective-permute-start.14) | collective-permute-done | bytes 53280 | tf_op jit(solution)/shard_map/ppermute | solution.py:258
  226.6 4.5 %shard_map.99 = (f32[192,3072]{1,0:T(8,128)}, f32[192,3072]{1,0:T(8,128)}) custom-call(f32[1]{0:T(128)S(6)} %copy.10.rate_ref, f32[192,3072]{1,0:T(8,128)S(1)} %copy-done.5, f32[192,3072]{1,0:T(8,128)S(1)} %bitcast.52, bf16[4,2,192,768]{3,2,1,0:T(8,128)(2,1)} %bitcast.27.g_ref), custom_call_target="tpu_custom_call" | custom-call | tf_op jit(solution)/shard_map/pallas_call | solution.py:225
  (81 shorter events, 36.5 us)
Async XLA Ops:
  8.0 11.3 %collective-permute-start = (bf16[2,192,128]{2,1,0:T(8,128)(2,1)S(1)}, bf16[2,192,128]{2,1,0:T(8,128)(2,1)S(1)}, u32[]{:S(2)}, u32[]{:S(2)}) collective-permute-start(bf16[2,192,128]{2,1,0:T(8,128)(2,1)S(1)} %get-tuple-element.29), channel_id=1, source_target_pairs={{0,64},{64,128},{128,192},{192,0},{1,65},{65,129},{129,193},{193,1... | collective-permute-start | bytes 294920 | tf_op jit(solution)/shard_map/ppermute | solution.py:258
  10.2 9.1 %collective-permute-start.1 = (bf16[2,192,128]{2,1,0:T(8,128)(2,1)S(1)}, bf16[2,192,128]{2,1,0:T(8,128)(2,1)S(1)}, u32[]{:S(2)}, u32[]{:S(2)}) collective-permute-start(bf16[2,192,128]{2,1,0:T(8,128)(2,1)S(1)} %get-tuple-element.29), channel_id=1, source_target_pairs={{0,128},{64,192},{128,0},{192,64},{1,129},{65,193},{129,1},{193,65... | collective-permute-start | bytes 294920 | tf_op jit(solution)/shard_map/ppermute | solution.py:258
  12.8 6.5 %collective-permute-start.2 = (bf16[2,192,128]{2,1,0:T(8,128)(2,1)S(1)}, bf16[2,192,128]{2,1,0:T(8,128)(2,1)S(1)}, u32[]{:S(2)}, u32[]{:S(2)}) collective-permute-start(bf16[2,192,128]{2,1,0:T(8,128)(2,1)S(1)} %get-tuple-element.29), channel_id=1, source_target_pairs={{0,192},{64,0},{128,64},{192,128},{1,193},{65,1},{129,65},{193,129... | collective-permute-start | bytes 294920 | tf_op jit(solution)/shard_map/ppermute | solution.py:258
  19.4 8.6 %copy-start.18 = (s32[1024]{0:T(1024)S(1)}, s32[1024]{0:T(1024)}, u32[]{:S(2)}) copy-start(s32[1024]{0:T(1024)} %param.8) | copy-start | bytes 12292
  19.4 45.0 %all-to-all-start = ((bf16[4,384,768]{2,1,0:T(8,128)(2,1)}), bf16[4,384,768]{2,1,0:T(8,128)(2,1)S(1)}, u32[]{:S(2)}, u32[]{:S(2)}) async-start(bf16[4,384,768]{2,1,0:T(8,128)(2,1)} %bitcast.53), calls=%async_computation | async-start | bytes 4718592 | tf_op jit(solution)/shard_map/all_to_all | solution.py:250
  23.0 101.5 %reduce-scatter.2.cloned.1.call-start = ((), (), s32[]{:S(2)}) async-start(), calls=%async_computation.3 | async-start | bytes 4128768 | tf_op jit(solution)/shard_map/reduce_scatter | solution.py:292
  23.1 10.4 %collective-permute-start.3 = (bf16[4,2,192,128]{3,2,1,0:T(8,128)(2,1)S(1)}, bf16[4,2,192,128]{3,2,1,0:T(8,128)(2,1)S(1)}, u32[]{:S(2)}, u32[]{:S(2)}) collective-permute-start(bf16[4,2,192,128]{3,2,1,0:T(8,128)(2,1)S(1)} %pad_maximum_fusion.refs_0_), channel_id=1, source_target_pairs={{0,2},{2,4},{4,6},{6,0},{1,3},{3,5},{5,7},{7,1},{8,10},{10,12},{12... | collective-permute-start | bytes 1179656 | tf_op jit(solution)/shard_map/ppermute | solution.py:258
  24.4 18.5 %collective-permute-start.4 = (bf16[4,2,192,128]{3,2,1,0:T(8,128)(2,1)S(1)}, bf16[4,2,192,128]{3,2,1,0:T(8,128)(2,1)S(1)}, u32[]{:S(2)}, u32[]{:S(2)}) collective-permute-start(bf16[4,2,192,128]{3,2,1,0:T(8,128)(2,1)S(1)} %pad_maximum_fusion.refs_0_), channel_id=1, source_target_pairs={{0,4},{2,6},{4,0},{6,2},{1,5},{3,7},{5,1},{7,3},{8,12},{10,14},{12... | collective-permute-start | bytes 1179656 | tf_op jit(solution)/shard_map/ppermute | solution.py:258
  26.8 18.5 %collective-permute-start.5 = (bf16[4,2,192,128]{3,2,1,0:T(8,128)(2,1)S(1)}, bf16[4,2,192,128]{3,2,1,0:T(8,128)(2,1)}, u32[]{:S(2)}, u32[]{:S(2)}) collective-permute-start(bf16[4,2,192,128]{3,2,1,0:T(8,128)(2,1)S(1)} %pad_maximum_fusion.refs_0_), channel_id=1, source_target_pairs={{0,6},{2,0},{4,2},{6,4},{1,7},{3,1},{5,3},{7,5},{8,14},{10,8},{12,... | collective-permute-start | bytes 1179656 | tf_op jit(solution)/shard_map/ppermute | solution.py:258
  28.5 17.4 %collective-permute-start.6 = (bf16[4,2,192,128]{3,2,1,0:T(8,128)(2,1)S(1)}, bf16[4,2,192,128]{3,2,1,0:T(8,128)(2,1)}, u32[]{:S(2)}, u32[]{:S(2)}) collective-permute-start(bf16[4,2,192,128]{3,2,1,0:T(8,128)(2,1)S(1)} %pad_maximum_fusion.refs_0_), channel_id=1, source_target_pairs={{0,1},{1,0},{2,3},{3,2},{4,5},{5,4},{6,7},{7,6},{8,9},{9,8},{10,11... | collective-permute-start | bytes 1179656 | tf_op jit(solution)/shard_map/ppermute | solution.py:254
  33.4 13.3 %copy-start.14 = (bf16[4,2,192,128]{3,2,1,0:T(8,128)(2,1)}, bf16[4,2,192,128]{3,2,1,0:T(8,128)(2,1)S(1)}, u32[]{:S(2)}) copy-start(bf16[4,2,192,128]{3,2,1,0:T(8,128)(2,1)S(1)} %collective-permute-done.3.refs_1_) | copy-start | bytes 1179652
  33.4 12.5 %collective-permute-start.7 = (bf16[4,2,192,128]{3,2,1,0:T(8,128)(2,1)S(1)}, bf16[4,2,192,128]{3,2,1,0:T(8,128)(2,1)}, u32[]{:S(2)}, u32[]{:S(2)}) collective-permute-start(bf16[4,2,192,128]{3,2,1,0:T(8,128)(2,1)S(1)} %collective-permute-done.3.refs_1_), channel_id=1, source_target_pairs={{0,1},{1,0},{2,3},{3,2},{4,5},{5,4},{6,7},{7,6},{8,9},{9,8},{10,11... | collective-permute-start | bytes 1179656 | tf_op jit(solution)/shard_map/ppermute | solution.py:254
  42.9 3.9 %collective-permute-start.8 = (bf16[4,2,192,128]{3,2,1,0:T(8,128)(2,1)S(1)}, bf16[4,2,192,128]{3,2,1,0:T(8,128)(2,1)}, u32[]{:S(2)}, u32[]{:S(2)}) collective-permute-start(bf16[4,2,192,128]{3,2,1,0:T(8,128)(2,1)S(1)} %collective-permute-done.4.refs_2_), channel_id=1, source_target_pairs={{0,1},{1,0},{2,3},{3,2},{4,5},{5,4},{6,7},{7,6},{8,9},{9,8},{10,11... | collective-permute-start | bytes 1179656 | tf_op jit(solution)/shard_map/ppermute | solution.py:254
  45.3 2.3 collective-permute-start.9
  72.2 101.1 %all-gather.3.cloned.1.call-start = ((), (), s32[]{:S(2)}) async-start(), calls=%async_computation.4 | async-start | bytes 3760128 | tf_op jit(solution)/shard_map/all_gather | solution.py:293
  182.8 9.2 %collective-permute-start.10 = (bf16[4,4,208,128]{3,2,1,0:T(8,128)(2,1)}, bf16[4,4,208,128]{3,2,1,0:T(8,128)(2,1)}, u32[]{:S(2)}, u32[]{:S(2)}) collective-permute-start(bf16[4,4,208,128]{3,2,1,0:T(8,128)(2,1)} %get-tuple-element.18), channel_id=1, source_target_pairs={{0,1},{1,0},{2,3},{3,2},{4,5},{5,4},{6,7},{7,6},{8,9},{9,8},{10,11... | collective-permute-start | bytes 2555912 | tf_op jit(solution)/shard_map/ppermute | solution.py:254
  187.5 37.4 %all-to-all-start.1 = ((bf16[4,384,768]{2,1,0:T(8,128)(2,1)}), bf16[4,384,768]{2,1,0:T(8,128)(2,1)}, u32[]{:S(2)}, u32[]{:S(2)}) async-start(bf16[4,384,768]{2,1,0:T(8,128)(2,1)} %bitcast.26), calls=%async_computation.2 | async-start | bytes 4718592 | tf_op jit(solution)/shard_map/all_to_all | solution.py:250
  192.0 32.9 %copy-start.5 = (f32[192,3072]{1,0:T(8,128)S(1)}, f32[192,3072]{1,0:T(8,128)}, u32[]{:S(2)}) copy-start(f32[192,3072]{1,0:T(8,128)} %a_ref.3) | copy-start | bytes 7077892
  193.6 8.3 %collective-permute-start.11 = (bf16[4,208,128]{2,1,0:T(8,128)(2,1)S(1)}, bf16[4,208,128]{2,1,0:T(8,128)(2,1)S(1)}, u32[]{:S(2)}, u32[]{:S(2)}) collective-permute-start(bf16[4,208,128]{2,1,0:T(8,128)(2,1)S(1)} %get-tuple-element.22), channel_id=1, source_target_pairs={{0,2},{2,4},{4,6},{6,0},{1,3},{3,5},{5,7},{7,1},{8,10},{10,12},{12... | collective-permute-start | bytes 638984 | tf_op jit(solution)/shard_map/ppermute | solution.py:258
  194.9 7.0 %collective-permute-start.12 = (bf16[4,208,128]{2,1,0:T(8,128)(2,1)S(1)}, bf16[4,208,128]{2,1,0:T(8,128)(2,1)S(1)}, u32[]{:S(2)}, u32[]{:S(2)}) collective-permute-start(bf16[4,208,128]{2,1,0:T(8,128)(2,1)S(1)} %get-tuple-element.24), channel_id=1, source_target_pairs={{0,6},{2,0},{4,2},{6,4},{1,7},{3,1},{5,3},{7,5},{8,14},{10,8},{12,... | collective-permute-start | bytes 638984 | tf_op jit(solution)/shard_map/ppermute | solution.py:258
  196.4 10.9 %collective-permute-start.13 = (bf16[4,208,128]{2,1,0:T(8,128)(2,1)S(1)}, bf16[4,208,128]{2,1,0:T(8,128)(2,1)S(1)}, u32[]{:S(2)}, u32[]{:S(2)}) collective-permute-start(bf16[4,208,128]{2,1,0:T(8,128)(2,1)S(1)} %get-tuple-element.23), channel_id=1, source_target_pairs={{0,4},{2,6},{4,0},{6,2},{1,5},{3,7},{5,1},{7,3},{8,12},{10,14},{12... | collective-permute-start | bytes 638984 | tf_op jit(solution)/shard_map/ppermute | solution.py:258
  207.4 15.5 %collective-permute-start.14 = (bf16[208,128]{1,0:T(8,128)(2,1)S(1)}, bf16[208,128]{1,0:T(8,128)(2,1)S(1)}, u32[]{:S(2)}, u32[]{:S(2)}) collective-permute-start(bf16[208,128]{1,0:T(8,128)(2,1)S(1)} %get-tuple-element.25), channel_id=1, source_target_pairs={{0,64},{64,128},{128,192},{192,0},{1,65},{65,129},{129,193},{193,1... | collective-permute-start | bytes 159752 | tf_op jit(solution)/shard_map/ppermute | solution.py:258
  208.6 14.4 %collective-permute-start.15 = (bf16[208,128]{1,0:T(8,128)(2,1)S(1)}, bf16[208,128]{1,0:T(8,128)(2,1)S(1)}, u32[]{:S(2)}, u32[]{:S(2)}) collective-permute-start(bf16[208,128]{1,0:T(8,128)(2,1)S(1)} %get-tuple-element.27), channel_id=1, source_target_pairs={{0,192},{64,0},{128,64},{192,128},{1,193},{65,1},{129,65},{193,129... | collective-permute-start | bytes 159752 | tf_op jit(solution)/shard_map/ppermute | solution.py:258
  210.2 13.4 %collective-permute-start.16 = (bf16[208,128]{1,0:T(8,128)(2,1)S(1)}, bf16[208,128]{1,0:T(8,128)(2,1)S(1)}, u32[]{:S(2)}, u32[]{:S(2)}) collective-permute-start(bf16[208,128]{1,0:T(8,128)(2,1)S(1)} %get-tuple-element.26), channel_id=1, source_target_pairs={{0,128},{64,192},{128,0},{192,64},{1,129},{65,193},{129,1},{193,65... | collective-permute-start | bytes 159752 | tf_op jit(solution)/shard_map/ppermute | solution.py:258
  (16 other events, 31.9 us)
Sparse Core Ops, SparseCore 0:
  72.3 52.1 reduce-scatter.1
  127.5 45.7 all-gather.2

commit v3 on v2

v3 whole, which is shorter than its diff:
```python
import functools

import jax
import jax.numpy as jnp
from jax import lax
from jax.experimental import pallas as pl
from jax.experimental.pallas import tpu as pltpu
from jax.sharding import Mesh, PartitionSpec as P

D = 6144
FF = 24576
IMAGES = 8
TOK_IMG = 128
TOKENS = 1024
FEAT = 192
NY, NZ, NX = 4, 8, 4
HID = 768
SCALE_IN = D ** (-0.5)
SCALE_OUT = FF ** (-0.5)
NORM_ROWS = 16

root_half = 0.7071067811865476
inv_root_tau = 0.3989422804014327

f32 = jnp.float32
bf16 = jnp.bfloat16
WIDE = HID + TOK_IMG
SENT = 2 * TOK_IMG + NORM_ROWS
MIB = 1024 * 1024
SMALL = pltpu.CompilerParams(vmem_limit_bytes=8 * MIB)
MIDDLE = pltpu.CompilerParams(vmem_limit_bytes=24 * MIB)
WHOLE = pltpu.CompilerParams(vmem_limit_bytes=56 * MIB)
VMEM = pl.BlockSpec(memory_space=pltpu.VMEM)
SMEM = pl.BlockSpec(memory_space=pltpu.SMEM)
HBM = pl.BlockSpec(memory_space=pltpu.HBM)
ANY = pl.BlockSpec(memory_space=pl.ANY)
TILE = 4 * TOK_IMG
TILES = TOKENS // TILE
PAIR = 2 * TOK_IMG


def dot(left, right, dims):
    return lax.dot_general(left, right, (dims, ((), ())), preferred_element_type=f32)


def in_hbm(value):
    return pltpu.with_memory_space_constraint(value, pltpu.HBM)


def split_hidden(in_weight, out_weight_t):
    def body(a_ref, b_ref, o_ref):
        o_ref[0, 0] = a_ref[...].astype(bf16)
        o_ref[0, 1] = b_ref[...].astype(bf16)

    return pl.pallas_call(
        body,
        grid=(NY,),
        in_specs=[pl.BlockSpec((FEAT, HID), lambda i: (0, i))] * 2,
        out_specs=pl.BlockSpec((1, 2, FEAT, HID), lambda i: (i, 0, 0, 0)),
        out_shape=pltpu.HBM((NY, 2, FEAT, HID), bf16),
        compiler_params=MIDDLE,
    )(in_hbm(in_weight), in_hbm(out_weight_t))


def fill_order(place_ref, order_ref):
    def one(r, carry):
        at = pl.ds(pl.multiple_of(r * PAIR, PAIR), PAIR)
        place = jnp.concatenate([place_ref[at, :]] * (TOKENS // 128), axis=1)
        column = lax.broadcasted_iota(jnp.int32, (PAIR, TOKENS), 1)
        order_ref[at, :] = jnp.where(place == column, 1.0, 0.0).astype(bf16)
        return carry

    lax.fori_loop(0, TOKENS // PAIR, one, 0)


def behind(mine, step, size):
    return lax.rem(mine - step + size, size)


def sort_tokens(here, own, other, place):
    def body(here_ref, *refs):
        pieces, (p_ref, x_ref, t_ref, pair_ref) = refs[:8], refs[8:12]
        rows, place_buf, p_buf, x_buf, t_buf, pair_buf, in_sem, p_sem, x_sem, t_sem, pair_sem = refs[12:]

        def load(piece):
            o, u = divmod(piece, NX)
            core = here_ref[3] if o == 0 else 1 - here_ref[3]
            lane = pl.multiple_of((behind(here_ref[2], u, NX) * 2 + core) * 128, 128)
            return pltpu.make_async_copy(
                pieces[piece], rows.at[:, :, :, pl.ds(lane, 128)], in_sem.at[piece]
            )

        def stores(a, t):
            at = pl.ds(pl.multiple_of(t * TILE, TILE), TILE)
            return (
                pltpu.make_async_copy(x_buf.at[a, :, at], x_ref.at[a, :, at], x_sem.at[a, t]),
                pltpu.make_async_copy(t_buf.at[a, at], t_ref.at[a, at], t_sem.at[a, t]),
            )

        p_load = pltpu.make_async_copy(p_ref, place_buf, p_sem)
        pair_store = pltpu.make_async_copy(pair_buf, pair_ref, pair_sem)
        loads = [load(piece) for piece in range(8)]
        p_load.start()
        for copy in loads:
            copy.start()
        p_load.wait()
        fill_order(place_buf, p_buf)
        for copy in loads:
            copy.wait()

        def one(i, carry):
            a, t = lax.div(i, TILES), lax.rem(i, TILES)
            at = pl.ds(pl.multiple_of(t * TILE, TILE), TILE)
            given = rows[:, a].reshape(NY * FEAT, TOKENS)
            ordered = dot(given, p_buf[:, at], ((1,), (0,))).astype(bf16)
            x_buf[a, :, at] = ordered
            turned = ordered.T
            t_buf[a, at, :] = turned
            for k in range(4):
                image = slice(k * TOK_IMG, (k + 1) * TOK_IMG)
                pairs = dot(turned[image], ordered[:, image], ((1,), (0,)))
                pair_buf[4 * t + k, a] = pairs.astype(bf16)
            for copy in stores(a, t):
                copy.start()
            return carry

        def finish(i, carry):
            for copy in stores(lax.div(i, TILES), lax.rem(i, TILES)):
                copy.wait()
            return carry

        lax.fori_loop(0, 2 * TILES, one, 0)
        pair_store.start()
        lax.fori_loop(0, 2 * TILES, finish, 0)
        pair_store.wait()

    feats, rows = (2, NY * FEAT, TOKENS), (2, TOKENS, NY * FEAT)
    pairs = (IMAGES, 2, TOK_IMG, TOK_IMG)
    return pl.pallas_call(
        body,
        in_specs=[SMEM] + [HBM] * 9,
        out_specs=[HBM] * 3,
        out_shape=[pltpu.HBM(shape, bf16) for shape in (feats, rows, pairs)],
        scratch_shapes=[
            pltpu.VMEM((NY, 2, FEAT, TOKENS), bf16),
            pltpu.VMEM((TOKENS, 128), jnp.int32),
            pltpu.VMEM((TOKENS, TOKENS), bf16),
            pltpu.VMEM(feats, bf16),
            pltpu.VMEM(rows, bf16),
            pltpu.VMEM(pairs, bf16),
            pltpu.SemaphoreType.DMA((8,)),
            pltpu.SemaphoreType.DMA,
            pltpu.SemaphoreType.DMA((2, TILES)),
            pltpu.SemaphoreType.DMA((2, TILES)),
            pltpu.SemaphoreType.DMA,
        ],
        compiler_params=MIDDLE,
    )(here, *map(in_hbm, (*own, *other, place)))


def project(here, rows, pairs, weights):
    def body(here_ref, r_ref, p_ref, w_ref, o_ref, r_buf, w_buf, o_buf, r_sem, w_sem, p_sem, o_sem):
        w_loads = [
            pltpu.make_async_copy(
                w_ref.at[behind(here_ref[0], s, NY)], w_buf.at[:, s], w_sem.at[s]
            )
            for s in range(NY)
        ]
        p_load = pltpu.make_async_copy(p_ref, o_buf.at[:, :, :, pl.ds(HID, TOK_IMG)], p_sem)

        def load(a):
            return pltpu.make_async_copy(r_ref.at[a], r_buf.at[a], r_sem.at[a])

        def store(a, t):
            part = (pl.ds(4 * t, 4), a)
            return pltpu.make_async_copy(o_buf.at[part], o_ref.at[part], o_sem.at[a, t])

        for copy in w_loads:
            copy.start()
        load(0).start()
        p_load.start()
        load(1).start()
        for copy in w_loads:
            copy.wait()
        load(0).wait()
        p_load.wait()

        def one(i, carry):
            a, t = lax.div(i, TILES), lax.rem(i, TILES)

            @pl.when(i == TILES)
            def _():
                load(1).wait()

            at = pl.ds(pl.multiple_of(t * TILE, TILE), TILE)
            weight = w_buf[a].reshape(NY * FEAT, HID)
            scale = jnp.where(a == 0, f32(SCALE_IN), f32(SCALE_OUT))
            prod = dot(r_buf[a, at, :], weight, ((1,), (0,)))
            prod = (prod * scale).astype(bf16).reshape(4, TOK_IMG, HID)
            o_buf[pl.ds(4 * t, 4), a, :, 0:HID] = prod
            store(a, t).start()
            return carry

        def finish(i, carry):
            store(lax.div(i, TILES), lax.rem(i, TILES)).wait()
            return carry

        lax.fori_loop(0, 2 * TILES, one, 0)
        lax.fori_loop(0, 2 * TILES, finish, 0)

    given = (IMAGES, 2, TOK_IMG, WIDE)
    return pl.pallas_call(
        body,
        in_specs=[SMEM, HBM, HBM, ANY],
        out_specs=HBM,
        out_shape=pltpu.HBM(given, bf16),
        scratch_shapes=[
            pltpu.VMEM((2, TOKENS, NY * FEAT), bf16),
            pltpu.VMEM((2, NY, FEAT, HID), bf16),
            pltpu.VMEM(given, bf16),
            pltpu.SemaphoreType.DMA((2,)),
            pltpu.SemaphoreType.DMA((NY,)),
            pltpu.SemaphoreType.DMA,
            pltpu.SemaphoreType.DMA((2, TILES)),
        ],
        compiler_params=MIDDLE,
    )(here, in_hbm(rows), in_hbm(pairs), weights)


def activate(here, summed):
    def body(here_ref, s_ref, o_ref):
        pre = s_ref[0:TOK_IMG, 0:HID].astype(f32)
        act, slope = gelu_and_slope(pre)
        act = act.astype(bf16)
        hid = (s_ref[TOK_IMG:, 0:HID].astype(f32) * slope).astype(bf16)
        o_ref[0:TOK_IMG, :] = act
        o_ref[TOK_IMG : 2 * TOK_IMG, :] = hid
        pairs = s_ref[:, HID:].astype(f32)
        both = dot(hid, hid, ((1,), (1,))) * pairs[0:TOK_IMG] * (SCALE_IN * SCALE_IN)
        both += dot(act, act, ((1,), (1,))) * pairs[TOK_IMG:] * (SCALE_OUT * SCALE_OUT)
        square = jnp.sum(jnp.sum(both, axis=0, keepdims=True), axis=1, keepdims=True)
        high = square.astype(bf16).astype(f32)
        middle = (square - high).astype(bf16).astype(f32)
        low = square - high - middle
        source = (here_ref[0] * NX + here_ref[2]) * 2 + here_ref[3]
        spot = lax.rem(source, 16) * IMAGES + here_ref[1]
        row = lax.broadcasted_iota(jnp.int32, (NORM_ROWS, 128), 0)
        lane = lax.broadcasted_iota(jnp.int32, (NORM_ROWS, 128), 1)
        kind = row - lax.div(source, 16) * 3
        value = jnp.where(kind == 0, high, jnp.where(kind == 1, middle, low))
        kept = (lane == spot) & (kind >= 0) & (kind < 3)
        o_ref[2 * TOK_IMG :, :] = jnp.zeros((NORM_ROWS, HID), bf16)
        o_ref[2 * TOK_IMG :, 0:128] = jnp.where(kept, value, 0.0).astype(bf16)

    return pl.pallas_call(
        body,
        in_specs=[SMEM, VMEM],
        out_specs=VMEM,
        out_shape=jax.ShapeDtypeStruct((SENT, HID), bf16),
        compiler_params=SMALL,
    )(here, summed)


def all_grads(here, weights, feats, every, place):
    rows = FEAT + NORM_ROWS

    def body(here_ref, w_ref, x_ref, e_ref, p_ref, g_ref, own_ref, oth_ref, *refs):
        w_buf, x_buf, e_buf, n_buf, place_buf, p_buf, g_buf, o_buf = refs[:8]
        w_sem, x_sem, e_sem, n_sem, p_sem, g_sem, o_sem = refs[8:]
        w_load = pltpu.make_async_copy(w_ref.at[:, 0], w_buf, w_sem)
        n_load = pltpu.make_async_copy(
            e_ref.at[:, pl.ds(2 * TOK_IMG, NORM_ROWS), pl.ds(0, 128)], n_buf, n_sem
        )

        def e_load(w):
            part = pl.ds((1 - w) * TOK_IMG, TOK_IMG)
            return pltpu.make_async_copy(e_ref.at[:, part], e_buf.at[w], e_sem.at[w])

        def x_load(w):
            return pltpu.make_async_copy(x_ref.at[w], x_buf.at[w], x_sem.at[w])

        def g_stores(w):
            for s in range(NY):
                y = behind(here_ref[0], s, NY)
                yield pltpu.make_async_copy(g_buf.at[w, s], g_ref.at[y, w], g_sem.at[w, s])

        def stores(x):
            u = lax.rem(x - here_ref[2] + NX, NX)
            yield pltpu.make_async_copy(o_buf.at[1, u], oth_ref.at[u], o_sem.at[1, x])
            yield pltpu.make_async_copy(o_buf.at[0, u], own_ref.at[u], o_sem.at[0, x])

        p_load = pltpu.make_async_copy(p_ref, place_buf, p_sem)
        p_load.start()
        e_load(0).start()
        w_load.start()
        n_load.start()
        x_load(0).start()
        e_load(1).start()
        x_load(1).start()
        p_load.wait()
        fill_order(place_buf, p_buf)
        n_load.wait()
        norms = n_buf[0].astype(f32)
        for b in range(1, IMAGES):
            norms += n_buf[b].astype(f32)
        norms = norms.astype(bf16)
        e_load(0).wait()
        w_load.wait()

        def one(x, carry):
            at = pl.multiple_of(x * PAIR, PAIR)
            hidden = e_buf[0].reshape(TOKENS, HID)
            placed = dot(p_buf[pl.ds(at, PAIR), :], hidden, ((1,), (0,))).astype(bf16)
            weight = w_buf[...].reshape(NY * FEAT, HID)
            grad = (dot(weight, placed, ((1,), (1,))) * SCALE_IN).astype(bf16)
            u = lax.rem(x - here_ref[2] + NX, NX)
            for core in range(2):
                o = lax.rem(core + here_ref[3], 2)
                half = grad[:, core * 128 : (core + 1) * 128]
                for y in range(NY):
                    v = lax.rem(y - here_ref[0] + NY, NY)
                    o_buf[o, u, v, 0:FEAT, :] = half[y * FEAT : (y + 1) * FEAT]
                    o_buf[o, u, v, FEAT:, :] = norms
            for copy in stores(x):
                copy.start()
            return carry

        lax.fori_loop(0, NX, one, 0)
        tile = 256
        steps = HID // tile

        def two(i, carry):
            w, n = lax.div(i, steps), lax.rem(i, steps)

            @pl.when(n == 0)
            def _():
                x_load(w).wait()

            @pl.when(i == steps)
            def _():
                e_load(w).wait()

            cols = pl.ds(pl.multiple_of(n * tile, tile), tile)
            hidden = e_buf[w, :, :, cols].reshape(TOKENS, tile)
            scale = jnp.where(w == 0, f32(SCALE_IN), f32(SCALE_OUT))
            grad = dot(x_buf[w], hidden, ((1,), (0,))) * scale
            g_buf[w, :, :, cols] = grad.astype(bf16).reshape(NY, FEAT, tile)

            @pl.when(n == steps - 1)
            def _():
                for copy in g_stores(w):
                    copy.start()

            return carry

        lax.fori_loop(0, 2 * steps, two, 0)
        for x in range(NX):
            for copy in stores(x):
                copy.wait()
        for w in range(2):
            for copy in g_stores(w):
                copy.wait()

    sums = (NX, NY, rows, 128)
    grads = (NY, 2, FEAT, HID)
    return pl.pallas_call(
        body,
        in_specs=[SMEM] + [HBM] * 4,
        out_specs=[HBM] * 3,
        out_shape=[pltpu.HBM(shape, bf16) for shape in (grads, sums, sums)],
        scratch_shapes=[
            pltpu.VMEM((NY, FEAT, HID), bf16),
            pltpu.VMEM((2, NY * FEAT, TOKENS), bf16),
            pltpu.VMEM((2, IMAGES, TOK_IMG, HID), bf16),
            pltpu.VMEM((IMAGES, NORM_ROWS, 128), bf16),
            pltpu.VMEM((TOKENS, 128), jnp.int32),
            pltpu.VMEM((TOKENS, TOKENS), bf16),
            pltpu.VMEM((2, NY, FEAT, HID), bf16),
            pltpu.VMEM((2, *sums), bf16),
            pltpu.SemaphoreType.DMA,
            pltpu.SemaphoreType.DMA((2,)),
            pltpu.SemaphoreType.DMA((2,)),
            pltpu.SemaphoreType.DMA,
            pltpu.SemaphoreType.DMA,
            pltpu.SemaphoreType.DMA((2, NY)),
            pltpu.SemaphoreType.DMA((2, NX)),
        ],
        compiler_params=MIDDLE,
    )(here, *map(in_hbm, (weights, feats, every, place)))


def update(rate, in_weight, out_weight_t, grads):
    def body(rate_ref, a_ref, b_ref, g_ref, a_out, b_out, w_buf, g_buf, w_sem, g_sem, o_sem):
        def loads(y):
            cols = pl.ds(pl.multiple_of(y * HID, HID), HID)
            return (
                pltpu.make_async_copy(g_ref.at[y], g_buf.at[y], g_sem.at[y]),
                pltpu.make_async_copy(a_ref.at[:, cols], w_buf.at[0, y], w_sem.at[0, y]),
                pltpu.make_async_copy(b_ref.at[:, cols], w_buf.at[1, y], w_sem.at[1, y]),
            )

        def stores(y):
            cols = pl.ds(pl.multiple_of(y * HID, HID), HID)
            return (
                pltpu.make_async_copy(w_buf.at[0, y], a_out.at[:, cols], o_sem.at[0, y]),
                pltpu.make_async_copy(w_buf.at[1, y], b_out.at[:, cols], o_sem.at[1, y]),
            )

        def begin(y, carry):
            for copy in loads(y):
                copy.start()
            return carry

        def one(y, carry):
            for copy in loads(y):
                copy.wait()
            for w in range(2):
                w_buf[w, y] = w_buf[w, y] - rate_ref[0] * g_buf[y, w].astype(f32)
            for copy in stores(y):
                copy.start()
            return carry

        def finish(y, carry):
            for copy in stores(y):
                copy.wait()
            return carry

        lax.fori_loop(0, NY, begin, 0)
        lax.fori_loop(0, NY, one, 0)
        lax.fori_loop(0, NY, finish, 0)

    return pl.pallas_call(
        body,
        in_specs=[SMEM, HBM, HBM, ANY],
        out_specs=[HBM] * 2,
        out_shape=[pltpu.HBM(in_weight.shape, f32)] * 2,
        scratch_shapes=[
            pltpu.VMEM((2, NY, FEAT, HID), f32),
            pltpu.VMEM((NY, 2, FEAT, HID), bf16),
            pltpu.SemaphoreType.DMA((2, NY)),
            pltpu.SemaphoreType.DMA((NY,)),
            pltpu.SemaphoreType.DMA((2, NY)),
        ],
        compiler_params=MIDDLE,
    )(rate, in_hbm(in_weight), in_hbm(out_weight_t), grads)


def gelu_and_slope(pre):
    phi = 0.5 * (1.0 + lax.erf(pre * root_half))
    return pre * phi, phi + pre * jnp.exp(-0.5 * pre * pre) * inv_root_tau


def exchange(value, axes):
    return lax.all_to_all(value, axes, 0, 0, tiled=True)


def swap_cores(value):
    return lax.ppermute(value, "core", [(0, 1), (1, 0)])


def ahead(value, axis, step):
    return lax.ppermute(value, axis, [(i, (i + step) % 4) for i in range(4)])


def ring_gather(value, axis):
    near, back, far = ahead(value, axis, 1), ahead(value, axis, 3), ahead(value, axis, 2)
    return [value, near, far, back]


def token_place(image_ids):
    at = jnp.arange(TOKENS)
    same = (image_ids[:, None] == image_ids[None, :]) & (at[None, :] < at[:, None])
    place = image_ids * TOK_IMG + jnp.sum(same.astype(jnp.int32), axis=1)
    return jnp.broadcast_to(place[:, None], (TOKENS, 128))


def ring_sum(chunks, axis):
    total = chunks[0].astype(f32)
    for s in (1, 3, 2):
        total += ahead(chunks[s], axis, s).astype(f32)
    return total


def shards(tokens, out_grad, image_ids, learn_rate, in_weight, out_weight):
    here = jnp.stack([lax.axis_index(a) for a in ("y", "z", "x", "core")]).astype(jnp.int32)
    out_weight_t = out_weight.T
    halves = split_hidden(in_weight, out_weight_t)
    along_y = jnp.stack(ring_gather(jnp.stack([tokens.T, out_grad.T]), "y"))
    halves, along_y = lax.optimization_barrier((halves, along_y))
    weights = exchange(halves.reshape(NY * 2 * FEAT, HID), "y").reshape(NY, 2, FEAT, HID)
    own = ring_gather(along_y, "x")
    place, own[1] = lax.optimization_barrier((token_place(image_ids), own[1]))
    other = [swap_cores(piece) for piece in own]
    feats, rows, pairs = sort_tokens(here, own, other, place)
    parts = project(here, rows, pairs, weights).reshape(IMAGES, 2 * TOK_IMG, WIDE)
    summed = lax.psum_scatter(parts, "z", scatter_dimension=0)
    every = lax.all_gather(activate(here, summed), "z")
    grads, mine, theirs = all_grads(here, weights, feats, every, place)
    grads = exchange(grads.reshape(NY * 2 * FEAT, HID), "y").reshape(NY, 2, FEAT, HID)
    merged = (mine.astype(f32) + swap_cores(theirs).astype(f32)).astype(bf16)
    along_x = ring_sum(merged, "x").astype(bf16)
    got = ring_sum(along_x, "y")
    input_grad = got[:FEAT].astype(bf16).T
    example_sq = jnp.sum(got[FEAT:].reshape(NORM_ROWS * 16, IMAGES), axis=0)
    example_norm = 0.5 * jnp.log(example_sq + 1e-06)
    in_next, out_next = update(learn_rate, in_weight, out_weight_t, grads)
    return (input_grad, in_next, out_next.T, example_norm)


def solution(mesh):
    chips = Mesh(mesh.devices.reshape(NY, NZ, NX, 2), ("y", "z", "x", "core"))
    row, col = ("y", "z"), ("x", "core")
    placed = (P(col, row), P(col, row), P(), P(), P(row, col), P(col, row))
    return jax.shard_map(
        shards,
        mesh=chips,
        in_specs=placed,
        out_specs=(P(col, row), P(row, col), P(col, row), P()),
        check_vma=False,
    )
```

time: 239 us -> 224 us (0.937)
  local copies, waits for them, and re-layouts: 22.1 us -> 2.86 us
  Pallas kernels: 31.2 us -> 36.9 us
    unnamed x38 -> x14, local copies, waits for them, and re-layouts: 21.3 us -> 1.05 us
    pallas_call x1, Pallas kernels: 0.63 us -> 4.31 us  [split_hidden(): pl.pallas_call(body, grid=(NY,), in_specs=[pl.BlockSpec((FEAT, HID), lamb...]
    pallas_call x5 -> x4, Pallas kernels: 28.7 us -> 30.8 us  [the longest x1 11.3 us: all_grads(): pl.pallas_call(body, in_specs=[SMEM] + [HBM] * 4, out_specs=[HBM] * 3, ou...]
  transfers between devices with their start and end apart: 21 -> 21, of which waited for: 10 -> 9; matrix products, arithmetic and copies ran while one was open for 2% -> 2% of each run, Pallas kernels for 6% -> 6%
where the time goes in v3:
time: 224 us; the launch traced here: 223 us
  waiting for transfers between devices  128 us (57%)
  Pallas kernels  36.9 us (16%)
  starting transfers between devices  36.4 us (16%)
  between operations  14.9 us (7%)
  other arithmetic  3.6 us (2%)
  local copies, waits for them, and re-layouts  2.86 us (1%)
    reduce_scatter x1, waiting for transfers between devices, shards(): summed = lax.psum_scatter(parts, 'z', scatter_dimension=0)  52.3 us
    all_gather x1, waiting for transfers between devices, shards(): every = lax.all_gather(activate(here, summed), 'z')  46 us
    ppermute x12, waiting for transfers between devices, ahead(): return lax.ppermute(value, axis, [(i, (i + step) % 4) for i in range(4)])  28 us
    ppermute x12, starting transfers between devices, ahead(): return lax.ppermute(value, axis, [(i, (i + step) % 4) for i in range(4)])  19.2 us
    pallas_call x1, Pallas kernels, all_grads(): pl.pallas_call(body, in_specs=[SMEM] + [HBM] * 4, out_specs=[HBM] * 3, ou...  11.3 us
    ppermute x5, starting transfers between devices, swap_cores(): return lax.ppermute(value, 'core', [(0, 1), (1, 0)])  9.22 us
    pallas_call x1, Pallas kernels, sort_tokens(): pl.pallas_call(body, in_specs=[SMEM] + [HBM] * 9, out_specs=[HBM] * 3, ou...  9.02 us
    all_to_all x2, starting transfers between devices, exchange(): return lax.all_to_all(value, axes, 0, 0, tiled=True)  7.92 us
  transfers between devices with their start and end apart: 21, of which 9 were waited for; matrix products, arithmetic and copies ran while one was open for 2% of the time, Pallas kernels for 6%

profile of v3, /device:TPU:1, one launch (start us, length us, event | category | flops | bytes accessed | tf_op | source)
XLA Modules:
  0.0 223.0 jit_solution(5587376097038979294)
XLA Ops:
  8.0 2.2 collective-permute-start
  10.2 2.6 %collective-permute-start.1 = (bf16[2,192,128]{2,1,0:T(8,128)(2,1)S(1)}, bf16[2,192,128]{2,1,0:T(8,128)(2,1)S(1)}, u32[]{:S(2)}, u32[]{:S(2)}) collective-permute-start(bf16[2,192,128]{2,1,0:T(8,128)(2,1)S(1)} %get-tuple-element.35), channel_id=1, source_target_pairs={{0,128},{64,192},{128,0},{192,64},{1,129},{65,193},{129,1},{193,65... | collective-permute-start | bytes 294920 | tf_op jit(solution)/shard_map/ppermute | solution.py:462
  13.9 4.3 %shard_map.93 = bf16[4,2,192,768]{3,2,1,0:T(8,128)(2,1)} custom-call(f32[192,3072]{1,0:T(8,128)} %a_ref.3, f32[192,3072]{1,0:T(8,128)} %bitcast.53), custom_call_target="tpu_custom_call" | custom-call | tf_op jit(solution)/shard_map/pallas_call | solution.py:55
  18.3 3.8 %all-to-all-start = ((bf16[4,384,768]{2,1,0:T(8,128)(2,1)}), bf16[4,384,768]{2,1,0:T(8,128)(2,1)S(1)}, u32[]{:S(2)}, u32[]{:S(2)}) async-start(bf16[4,384,768]{2,1,0:T(8,128)(2,1)} %bitcast.55), calls=%async_computation | async-start | bytes 4718592 | tf_op jit(solution)/shard_map/all_to_all | solution.py:454
  23.4 2.5 %collective-permute-start.4 = (bf16[4,2,192,128]{3,2,1,0:T(8,128)(2,1)S(1)}, bf16[4,2,192,128]{3,2,1,0:T(8,128)(2,1)S(1)}, u32[]{:S(2)}, u32[]{:S(2)}) collective-permute-start(bf16[4,2,192,128]{3,2,1,0:T(8,128)(2,1)S(1)} %pad_maximum_fusion.refs_0_), channel_id=1, source_target_pairs={{0,4},{2,6},{4,0},{6,2},{1,5},{3,7},{5,1},{7,3},{8,12},{10,14},{12... | collective-permute-start | bytes 1179656 | tf_op jit(solution)/shard_map/ppermute | solution.py:462
  27.6 2.4 %collective-permute-start.6 = (bf16[4,2,192,128]{3,2,1,0:T(8,128)(2,1)S(1)}, bf16[4,2,192,128]{3,2,1,0:T(8,128)(2,1)}, u32[]{:S(2)}, u32[]{:S(2)}) collective-permute-start(bf16[4,2,192,128]{3,2,1,0:T(8,128)(2,1)S(1)} %pad_maximum_fusion.refs_0_), channel_id=1, source_target_pairs={{0,1},{1,0},{2,3},{3,2},{4,5},{5,4},{6,7},{7,6},{8,9},{9,8},{10,11... | collective-permute-start | bytes 1179656 | tf_op jit(solution)/shard_map/ppermute | solution.py:458
  30.0 2.5 %collective-permute-done.3.refs_1_ = bf16[4,2,192,128]{3,2,1,0:T(8,128)(2,1)S(1)} collective-permute-done((bf16[4,2,192,128]{3,2,1,0:T(8,128)(2,1)S(1)}, bf16[4,2,192,128]{3,2,1,0:T(8,128)(2,1)S(1)}, u32[]{:S(2)}, u32[]{:S(2)}) %collective-permute-start.3) | collective-permute-done | bytes 393248 | tf_op jit(solution)/shard_map/ppermute | solution.py:462
  33.5 3.5 %collective-permute-start.7 = (bf16[4,2,192,128]{3,2,1,0:T(8,128)(2,1)S(1)}, bf16[4,2,192,128]{3,2,1,0:T(8,128)(2,1)}, u32[]{:S(2)}, u32[]{:S(2)}) collective-permute-start(bf16[4,2,192,128]{3,2,1,0:T(8,128)(2,1)S(1)} %collective-permute-done.3.refs_1_), channel_id=1, source_target_pairs={{0,1},{1,0},{2,3},{3,2},{4,5},{5,4},{6,7},{7,6},{8,9},{9,8},{10,11... | collective-permute-start | bytes 1179656 | tf_op jit(solution)/shard_map/ppermute | solution.py:458
  37.0 4.9 %collective-permute-done.4.refs_2_ = bf16[4,2,192,128]{3,2,1,0:T(8,128)(2,1)S(1)} collective-permute-done((bf16[4,2,192,128]{3,2,1,0:T(8,128)(2,1)S(1)}, bf16[4,2,192,128]{3,2,1,0:T(8,128)(2,1)S(1)}, u32[]{:S(2)}, u32[]{:S(2)}) %collective-permute-start.4) | collective-permute-done | bytes 393248 | tf_op jit(solution)/shard_map/ppermute | solution.py:462
  41.9 2.4 %collective-permute-start.8 = (bf16[4,2,192,128]{3,2,1,0:T(8,128)(2,1)S(1)}, bf16[4,2,192,128]{3,2,1,0:T(8,128)(2,1)}, u32[]{:S(2)}, u32[]{:S(2)}) collective-permute-start(bf16[4,2,192,128]{3,2,1,0:T(8,128)(2,1)S(1)} %collective-permute-done.4.refs_2_), channel_id=1, source_target_pairs={{0,1},{1,0},{2,3},{3,2},{4,5},{5,4},{6,7},{7,6},{8,9},{9,8},{10,11... | collective-permute-start | bytes 1179656 | tf_op jit(solution)/shard_map/ppermute | solution.py:458
  46.6 9.0 %shard_map.94 = (bf16[2,768,1024]{2,1,0:T(8,128)(2,1)}, bf16[2,1024,768]{2,1,0:T(8,128)(2,1)}, bf16[8,2,128,128]{3,2,1,0:T(8,128)(2,1)}) custom-call(s32[4]{0:T(128)S(1)} %pad_add_fusion.here_ref, bf16[4,2,192,128]{3,2,1,0:T(8,128)(2,1)} %copy-done.2, bf16[4,2,192,128]{3,2,1,0:T(8,128)(2,1)} %copy-done.4, bf16[4,2,192,128]{3,2,1,0:T(8,128)(2,1)} %copy-done.5, ...), custom_call_target="tpu_custom_call" | custom-call | tf_op jit(solution)/shard_map/pallas_call | solution.py:139
  55.7 6.5 %shard_map.95 = bf16[8,2,128,896]{3,2,1,0:T(8,128)(2,1)} custom-call(s32[4]{0:T(128)S(1)} %pad_add_fusion.here_ref, bf16[2,1024,768]{2,1,0:T(8,128)(2,1)} %get-tuple-element.21.r_ref, bf16[8,2,128,128]{3,2,1,0:T(8,128)(2,1)} %get-tuple-element.22.p_ref, bf16[4,2,192,768]{3,2,1,0:T(8,128)(2,1)S(1)} %bitcast.48), custom_call_target="tpu_custom_call" | custom-call | tf_op jit(solution)/shard_map/pallas_call | solution.py:212
  62.3 52.3 %reduce-scatter.2.cloned.1.call-done = bf16[1,256,896]{2,1,0:T(8,128)(2,1)} async-done(((bf16[8,256,896]{2,1,0:T(8,128)(2,1)}), bf16[1,256,896]{2,1,0:T(8,128)(2,1)}) %reduce-scatter.2.cloned.1.call-update) | async-done | bytes 458768 | tf_op jit(solution)/shard_map/reduce_scatter | solution.py:496
  115.6 1.8 shard_map.96
  117.4 46.0 %all-gather.3.cloned.1.call-done = bf16[2176,768]{1,0:T(8,128)(2,1)} async-done(((bf16[272,768]{1,0:T(8,128)(2,1)}), bf16[2176,768]{1,0:T(8,128)(2,1)}) %all-gather.3.cloned.1.call-update) | async-done | bytes 3342352 | tf_op jit(solution)/shard_map/all_gather | solution.py:497
  163.4 11.3 %shard_map.97 = (bf16[4,2,192,768]{3,2,1,0:T(8,128)(2,1)}, bf16[4,4,208,128]{3,2,1,0:T(8,128)(2,1)}, bf16[4,4,208,128]{3,2,1,0:T(8,128)(2,1)}) custom-call(s32[4]{0:T(128)S(1)} %pad_add_fusion.here_ref, bf16[4,2,192,768]{3,2,1,0:T(8,128)(2,1)} %bitcast.49, bf16[2,768,1024]{2,1,0:T(8,128)(2,1)} %get-tuple-element.20.x_ref, bf16[8,272,768]{2,1,0:T(8,128)(2,1)} %bitcast.56, ...), custom_call_target="tpu_custom_call" | custom-call | tf_op jit(solution)/shard_map/pallas_call | solution.py:366
  175.4 4.1 %all-to-all-start.1 = ((bf16[4,384,768]{2,1,0:T(8,128)(2,1)}), bf16[4,384,768]{2,1,0:T(8,128)(2,1)S(1)}, u32[]{:S(2)}, u32[]{:S(2)}) async-start(bf16[4,384,768]{2,1,0:T(8,128)(2,1)} %bitcast.57), calls=%async_computation.2 | async-start | bytes 4718592 | tf_op jit(solution)/shard_map/all_to_all | solution.py:454
  182.3 1.5 collective-permute-start.12
  183.7 1.5 collective-permute-start.13
  185.2 3.6 %collective-permute-done.11 = bf16[4,208,128]{2,1,0:T(8,128)(2,1)S(1)} collective-permute-done((bf16[4,208,128]{2,1,0:T(8,128)(2,1)S(1)}, bf16[4,208,128]{2,1,0:T(8,128)(2,1)S(1)}, u32[]{:S(2)}, u32[]{:S(2)}) %collective-permute-start.11) | collective-permute-done | bytes 213024 | tf_op jit(solution)/shard_map/ppermute | solution.py:462
  188.8 5.5 %collective-permute-done.13 = bf16[4,208,128]{2,1,0:T(8,128)(2,1)S(1)} collective-permute-done((bf16[4,208,128]{2,1,0:T(8,128)(2,1)S(1)}, bf16[4,208,128]{2,1,0:T(8,128)(2,1)S(1)}, u32[]{:S(2)}, u32[]{:S(2)}) %collective-permute-start.13) | collective-permute-done | bytes 213024 | tf_op jit(solution)/shard_map/ppermute | solution.py:462
  195.6 1.5 collective-permute-start.15
  199.3 11.6 %collective-permute-done.14 = bf16[208,128]{1,0:T(8,128)(2,1)S(1)} collective-permute-done((bf16[208,128]{1,0:T(8,128)(2,1)S(1)}, bf16[208,128]{1,0:T(8,128)(2,1)S(1)}, u32[]{:S(2)}, u32[]{:S(2)}) %collective-permute-start.14) | collective-permute-done | bytes 53280 | tf_op jit(solution)/shard_map/ppermute | solution.py:462
  212.2 4.0 %shard_map.98 = (f32[192,3072]{1,0:T(8,128)}, f32[192,3072]{1,0:T(8,128)}) custom-call(f32[1]{0:T(128)S(6)} %copy.10.rate_ref, f32[192,3072]{1,0:T(8,128)} %a_ref.3, f32[192,3072]{1,0:T(8,128)} %bitcast.54, bf16[4,2,192,768]{3,2,1,0:T(8,128)(2,1)S(1)} %bitcast.50), custom_call_target="tpu_custom_call" | custom-call | tf_op jit(solution)/shard_map/pallas_call | solution.py:432
  (56 shorter events, 17.0 us)
Async XLA Ops:
  8.0 10.2 %collective-permute-start = (bf16[2,192,128]{2,1,0:T(8,128)(2,1)S(1)}, bf16[2,192,128]{2,1,0:T(8,128)(2,1)S(1)}, u32[]{:S(2)}, u32[]{:S(2)}) collective-permute-start(bf16[2,192,128]{2,1,0:T(8,128)(2,1)S(1)} %get-tuple-element.35), channel_id=1, source_target_pairs={{0,64},{64,128},{128,192},{192,0},{1,65},{65,129},{129,193},{193,1... | collective-permute-start | bytes 294920 | tf_op jit(solution)/shard_map/ppermute | solution.py:462
  10.2 8.0 %collective-permute-start.1 = (bf16[2,192,128]{2,1,0:T(8,128)(2,1)S(1)}, bf16[2,192,128]{2,1,0:T(8,128)(2,1)S(1)}, u32[]{:S(2)}, u32[]{:S(2)}) collective-permute-start(bf16[2,192,128]{2,1,0:T(8,128)(2,1)S(1)} %get-tuple-element.35), channel_id=1, source_target_pairs={{0,128},{64,192},{128,0},{192,64},{1,129},{65,193},{129,1},{193,65... | collective-permute-start | bytes 294920 | tf_op jit(solution)/shard_map/ppermute | solution.py:462
  12.8 5.4 %collective-permute-start.2 = (bf16[2,192,128]{2,1,0:T(8,128)(2,1)S(1)}, bf16[2,192,128]{2,1,0:T(8,128)(2,1)S(1)}, u32[]{:S(2)}, u32[]{:S(2)}) collective-permute-start(bf16[2,192,128]{2,1,0:T(8,128)(2,1)S(1)} %get-tuple-element.35), channel_id=1, source_target_pairs={{0,192},{64,0},{128,64},{192,128},{1,193},{65,1},{129,65},{193,129... | collective-permute-start | bytes 294920 | tf_op jit(solution)/shard_map/ppermute | solution.py:462
  18.3 9.3 %copy-start.2 = (bf16[4,2,192,128]{3,2,1,0:T(8,128)(2,1)}, bf16[4,2,192,128]{3,2,1,0:T(8,128)(2,1)S(1)}, u32[]{:S(2)}) copy-start(bf16[4,2,192,128]{3,2,1,0:T(8,128)(2,1)S(1)} %pad_maximum_fusion.refs_0_) | copy-start | bytes 1179652
  18.3 8.7 %copy-start.6 = (s32[1024]{0:T(1024)S(1)}, s32[1024]{0:T(1024)}, u32[]{:S(2)}) copy-start(s32[1024]{0:T(1024)} %param.8) | copy-start | bytes 12292
  18.3 37.4 %all-to-all-start = ((bf16[4,384,768]{2,1,0:T(8,128)(2,1)}), bf16[4,384,768]{2,1,0:T(8,128)(2,1)S(1)}, u32[]{:S(2)}, u32[]{:S(2)}) async-start(bf16[4,384,768]{2,1,0:T(8,128)(2,1)} %bitcast.55), calls=%async_computation | async-start | bytes 4718592 | tf_op jit(solution)/shard_map/all_to_all | solution.py:454
  22.1 92.5 %reduce-scatter.2.cloned.1.call-start = ((), (), s32[]{:S(2)}) async-start(), calls=%async_computation.3 | async-start | bytes 4128768 | tf_op jit(solution)/shard_map/reduce_scatter | solution.py:496
  22.1 10.4 %collective-permute-start.3 = (bf16[4,2,192,128]{3,2,1,0:T(8,128)(2,1)S(1)}, bf16[4,2,192,128]{3,2,1,0:T(8,128)(2,1)S(1)}, u32[]{:S(2)}, u32[]{:S(2)}) collective-permute-start(bf16[4,2,192,128]{3,2,1,0:T(8,128)(2,1)S(1)} %pad_maximum_fusion.refs_0_), channel_id=1, source_target_pairs={{0,2},{2,4},{4,6},{6,0},{1,3},{3,5},{5,7},{7,1},{8,10},{10,12},{12... | collective-permute-start | bytes 1179656 | tf_op jit(solution)/shard_map/ppermute | solution.py:462
  23.4 18.5 %collective-permute-start.4 = (bf16[4,2,192,128]{3,2,1,0:T(8,128)(2,1)S(1)}, bf16[4,2,192,128]{3,2,1,0:T(8,128)(2,1)S(1)}, u32[]{:S(2)}, u32[]{:S(2)}) collective-permute-start(bf16[4,2,192,128]{3,2,1,0:T(8,128)(2,1)S(1)} %pad_maximum_fusion.refs_0_), channel_id=1, source_target_pairs={{0,4},{2,6},{4,0},{6,2},{1,5},{3,7},{5,1},{7,3},{8,12},{10,14},{12... | collective-permute-start | bytes 1179656 | tf_op jit(solution)/shard_map/ppermute | solution.py:462
  25.9 18.5 %collective-permute-start.5 = (bf16[4,2,192,128]{3,2,1,0:T(8,128)(2,1)S(1)}, bf16[4,2,192,128]{3,2,1,0:T(8,128)(2,1)}, u32[]{:S(2)}, u32[]{:S(2)}) collective-permute-start(bf16[4,2,192,128]{3,2,1,0:T(8,128)(2,1)S(1)} %pad_maximum_fusion.refs_0_), channel_id=1, source_target_pairs={{0,6},{2,0},{4,2},{6,4},{1,7},{3,1},{5,3},{7,5},{8,14},{10,8},{12,... | collective-permute-start | bytes 1179656 | tf_op jit(solution)/shard_map/ppermute | solution.py:462
  27.6 17.0 %collective-permute-start.6 = (bf16[4,2,192,128]{3,2,1,0:T(8,128)(2,1)S(1)}, bf16[4,2,192,128]{3,2,1,0:T(8,128)(2,1)}, u32[]{:S(2)}, u32[]{:S(2)}) collective-permute-start(bf16[4,2,192,128]{3,2,1,0:T(8,128)(2,1)S(1)} %pad_maximum_fusion.refs_0_), channel_id=1, source_target_pairs={{0,1},{1,0},{2,3},{3,2},{4,5},{5,4},{6,7},{7,6},{8,9},{9,8},{10,11... | collective-permute-start | bytes 1179656 | tf_op jit(solution)/shard_map/ppermute | solution.py:458
  32.5 14.1 %copy-start.4 = (bf16[4,2,192,128]{3,2,1,0:T(8,128)(2,1)}, bf16[4,2,192,128]{3,2,1,0:T(8,128)(2,1)S(1)}, u32[]{:S(2)}) copy-start(bf16[4,2,192,128]{3,2,1,0:T(8,128)(2,1)S(1)} %collective-permute-done.3.refs_1_) | copy-start | bytes 1179652
  33.5 11.0 %collective-permute-start.7 = (bf16[4,2,192,128]{3,2,1,0:T(8,128)(2,1)S(1)}, bf16[4,2,192,128]{3,2,1,0:T(8,128)(2,1)}, u32[]{:S(2)}, u32[]{:S(2)}) collective-permute-start(bf16[4,2,192,128]{3,2,1,0:T(8,128)(2,1)S(1)} %collective-permute-done.3.refs_1_), channel_id=1, source_target_pairs={{0,1},{1,0},{2,3},{3,2},{4,5},{5,4},{6,7},{7,6},{8,9},{9,8},{10,11... | collective-permute-start | bytes 1179656 | tf_op jit(solution)/shard_map/ppermute | solution.py:458
  41.9 3.9 %collective-permute-start.8 = (bf16[4,2,192,128]{3,2,1,0:T(8,128)(2,1)S(1)}, bf16[4,2,192,128]{3,2,1,0:T(8,128)(2,1)}, u32[]{:S(2)}, u32[]{:S(2)}) collective-permute-start(bf16[4,2,192,128]{3,2,1,0:T(8,128)(2,1)S(1)} %collective-permute-done.4.refs_2_), channel_id=1, source_target_pairs={{0,1},{1,0},{2,3},{3,2},{4,5},{5,4},{6,7},{7,6},{8,9},{9,8},{10,11... | collective-permute-start | bytes 1179656 | tf_op jit(solution)/shard_map/ppermute | solution.py:458
  44.4 2.3 %collective-permute-start.9 = (bf16[4,2,192,128]{3,2,1,0:T(8,128)(2,1)}, bf16[4,2,192,128]{3,2,1,0:T(8,128)(2,1)}, u32[]{:S(2)}, u32[]{:S(2)}) collective-permute-start(bf16[4,2,192,128]{3,2,1,0:T(8,128)(2,1)} %collective-permute-done.5.refs_3_), channel_id=1, source_target_pairs={{0,1},{1,0},{2,3},{3,2},{4,5},{5,4},{6,7},{7,6},{8,9},{9,8},{10,11... | collective-permute-start | bytes 1179656 | tf_op jit(solution)/shard_map/ppermute | solution.py:458
  62.3 101.1 %all-gather.3.cloned.1.call-start = ((), (), s32[]{:S(2)}) async-start(), calls=%async_computation.4 | async-start | bytes 3760128 | tf_op jit(solution)/shard_map/all_gather | solution.py:497
  174.6 4.9 %collective-permute-start.10 = (bf16[4,4,208,128]{3,2,1,0:T(8,128)(2,1)}, bf16[4,4,208,128]{3,2,1,0:T(8,128)(2,1)}, u32[]{:S(2)}, u32[]{:S(2)}) collective-permute-start(bf16[4,4,208,128]{3,2,1,0:T(8,128)(2,1)} %get-tuple-element.24), channel_id=1, source_target_pairs={{0,1},{1,0},{2,3},{3,2},{4,5},{5,4},{6,7},{7,6},{8,9},{9,8},{10,11... | collective-permute-start | bytes 2555912 | tf_op jit(solution)/shard_map/ppermute | solution.py:458
  175.4 36.8 %all-to-all-start.1 = ((bf16[4,384,768]{2,1,0:T(8,128)(2,1)}), bf16[4,384,768]{2,1,0:T(8,128)(2,1)S(1)}, u32[]{:S(2)}, u32[]{:S(2)}) async-start(bf16[4,384,768]{2,1,0:T(8,128)(2,1)} %bitcast.57), calls=%async_computation.2 | async-start | bytes 4718592 | tf_op jit(solution)/shard_map/all_to_all | solution.py:454
  181.0 7.8 %collective-permute-start.11 = (bf16[4,208,128]{2,1,0:T(8,128)(2,1)S(1)}, bf16[4,208,128]{2,1,0:T(8,128)(2,1)S(1)}, u32[]{:S(2)}, u32[]{:S(2)}) collective-permute-start(bf16[4,208,128]{2,1,0:T(8,128)(2,1)S(1)} %get-tuple-element.28), channel_id=1, source_target_pairs={{0,2},{2,4},{4,6},{6,0},{1,3},{3,5},{5,7},{7,1},{8,10},{10,12},{12... | collective-permute-start | bytes 638984 | tf_op jit(solution)/shard_map/ppermute | solution.py:462
  182.3 6.5 %collective-permute-start.12 = (bf16[4,208,128]{2,1,0:T(8,128)(2,1)S(1)}, bf16[4,208,128]{2,1,0:T(8,128)(2,1)S(1)}, u32[]{:S(2)}, u32[]{:S(2)}) collective-permute-start(bf16[4,208,128]{2,1,0:T(8,128)(2,1)S(1)} %get-tuple-element.30), channel_id=1, source_target_pairs={{0,6},{2,0},{4,2},{6,4},{1,7},{3,1},{5,3},{7,5},{8,14},{10,8},{12,... | collective-permute-start | bytes 638984 | tf_op jit(solution)/shard_map/ppermute | solution.py:462
  183.7 10.5 %collective-permute-start.13 = (bf16[4,208,128]{2,1,0:T(8,128)(2,1)S(1)}, bf16[4,208,128]{2,1,0:T(8,128)(2,1)S(1)}, u32[]{:S(2)}, u32[]{:S(2)}) collective-permute-start(bf16[4,208,128]{2,1,0:T(8,128)(2,1)S(1)} %get-tuple-element.29), channel_id=1, source_target_pairs={{0,4},{2,6},{4,0},{6,2},{1,5},{3,7},{5,1},{7,3},{8,12},{10,14},{12... | collective-permute-start | bytes 638984 | tf_op jit(solution)/shard_map/ppermute | solution.py:462
  194.4 16.4 %collective-permute-start.14 = (bf16[208,128]{1,0:T(8,128)(2,1)S(1)}, bf16[208,128]{1,0:T(8,128)(2,1)S(1)}, u32[]{:S(2)}, u32[]{:S(2)}) collective-permute-start(bf16[208,128]{1,0:T(8,128)(2,1)S(1)} %get-tuple-element.31), channel_id=1, source_target_pairs={{0,64},{64,128},{128,192},{192,0},{1,65},{65,129},{129,193},{193,1... | collective-permute-start | bytes 159752 | tf_op jit(solution)/shard_map/ppermute | solution.py:462
  195.6 15.2 %collective-permute-start.15 = (bf16[208,128]{1,0:T(8,128)(2,1)S(1)}, bf16[208,128]{1,0:T(8,128)(2,1)S(1)}, u32[]{:S(2)}, u32[]{:S(2)}) collective-permute-start(bf16[208,128]{1,0:T(8,128)(2,1)S(1)} %get-tuple-element.33), channel_id=1, source_target_pairs={{0,192},{64,0},{128,64},{192,128},{1,193},{65,1},{129,65},{193,129... | collective-permute-start | bytes 159752 | tf_op jit(solution)/shard_map/ppermute | solution.py:462
  197.2 13.7 %collective-permute-start.16 = (bf16[208,128]{1,0:T(8,128)(2,1)S(1)}, bf16[208,128]{1,0:T(8,128)(2,1)S(1)}, u32[]{:S(2)}, u32[]{:S(2)}) collective-permute-start(bf16[208,128]{1,0:T(8,128)(2,1)S(1)} %get-tuple-element.32), channel_id=1, source_target_pairs={{0,128},{64,192},{128,0},{192,64},{1,129},{65,193},{129,1},{193,65... | collective-permute-start | bytes 159752 | tf_op jit(solution)/shard_map/ppermute | solution.py:462
  (4 other events, 16.4 us)
Sparse Core Ops, SparseCore 0:
  62.4 52.1 reduce-scatter.1
  117.5 45.7 all-gather.2

commit v4 on v3

--- a/solution.py
+++ b/solution.py
@@ -18,14 +18,13 @@
 SCALE_IN = D ** (-0.5)
 SCALE_OUT = FF ** (-0.5)
 NORM_ROWS = 16
+PAIR_ROWS = 2 * TOK_IMG // 8
 
 root_half = 0.7071067811865476
 inv_root_tau = 0.3989422804014327
 
 f32 = jnp.float32
 bf16 = jnp.bfloat16
-WIDE = HID + TOK_IMG
-SENT = 2 * TOK_IMG + NORM_ROWS
 MIB = 1024 * 1024
 SMALL = pltpu.CompilerParams(vmem_limit_bytes=8 * MIB)
 MIDDLE = pltpu.CompilerParams(vmem_limit_bytes=24 * MIB)
@@ -97,6 +96,9 @@
                 pltpu.make_async_copy(t_buf.at[a, at], t_ref.at[a, at], t_sem.at[a, t]),
             )
 
+        share = here_ref[2] * 2 + here_ref[3]
+        pair_array = lax.div(share, 4)
+        pair_row = lax.rem(share, 4) * PAIR_ROWS
         p_load = pltpu.make_async_copy(p_ref, place_buf, p_sem)
         pair_store = pltpu.make_async_copy(pair_buf, pair_ref, pair_sem)
         loads = [load(piece) for piece in range(8)]
@@ -114,12 +116,16 @@
             given = rows[:, a].reshape(NY * FEAT, TOKENS)
             ordered = dot(given, p_buf[:, at], ((1,), (0,))).astype(bf16)
             x_buf[a, :, at] = ordered
-            turned = ordered.T
-            t_buf[a, at, :] = turned
-            for k in range(4):
-                image = slice(k * TOK_IMG, (k + 1) * TOK_IMG)
-                pairs = dot(turned[image], ordered[:, image], ((1,), (0,)))
-                pair_buf[4 * t + k, a] = pairs.astype(bf16)
+            t_buf[a, at, :] = ordered.T
+
+            @pl.when(a == pair_array)
+            def _():
+                for k in range(TILE // TOK_IMG):
+                    start = t * TILE + k * TOK_IMG + pair_row
+                    some = t_buf[a, pl.ds(pl.multiple_of(start, PAIR_ROWS), PAIR_ROWS), :]
+                    image = ordered[:, k * TOK_IMG : (k + 1) * TOK_IMG]
+                    pair_buf[TILE // TOK_IMG * t + k] = dot(some, image, ((1,), (0,)))
+
             for copy in stores(a, t):
                 copy.start()
             return carry
@@ -135,19 +141,19 @@
         pair_store.wait()
 
     feats, rows = (2, NY * FEAT, TOKENS), (2, TOKENS, NY * FEAT)
-    pairs = (IMAGES, 2, TOK_IMG, TOK_IMG)
+    pairs = (IMAGES, PAIR_ROWS, TOK_IMG)
     return pl.pallas_call(
         body,
         in_specs=[SMEM] + [HBM] * 9,
         out_specs=[HBM] * 3,
-        out_shape=[pltpu.HBM(shape, bf16) for shape in (feats, rows, pairs)],
+        out_shape=[pltpu.HBM(feats, bf16), pltpu.HBM(rows, bf16), pltpu.HBM(pairs, f32)],
         scratch_shapes=[
             pltpu.VMEM((NY, 2, FEAT, TOKENS), bf16),
             pltpu.VMEM((TOKENS, 128), jnp.int32),
             pltpu.VMEM((TOKENS, TOKENS), bf16),
             pltpu.VMEM(feats, bf16),
             pltpu.VMEM(rows, bf16),
-            pltpu.VMEM(pairs, bf16),
+            pltpu.VMEM(pairs, f32),
             pltpu.SemaphoreType.DMA((8,)),
             pltpu.SemaphoreType.DMA,
             pltpu.SemaphoreType.DMA((2, TILES)),
@@ -158,15 +164,14 @@
     )(here, *map(in_hbm, (*own, *other, place)))
 
 
-def project(here, rows, pairs, weights):
-    def body(here_ref, r_ref, p_ref, w_ref, o_ref, r_buf, w_buf, o_buf, r_sem, w_sem, p_sem, o_sem):
+def project(here, rows, weights):
+    def body(here_ref, r_ref, w_ref, o_ref, r_buf, w_buf, o_buf, r_sem, w_sem, o_sem):
         w_loads = [
             pltpu.make_async_copy(
                 w_ref.at[behind(here_ref[0], s, NY)], w_buf.at[:, s], w_sem.at[s]
             )
             for s in range(NY)
         ]
-        p_load = pltpu.make_async_copy(p_ref, o_buf.at[:, :, :, pl.ds(HID, TOK_IMG)], p_sem)
 
         def load(a):
             return pltpu.make_async_copy(r_ref.at[a], r_buf.at[a], r_sem.at[a])
@@ -178,12 +183,10 @@
         for copy in w_loads:
             copy.start()
         load(0).start()
-        p_load.start()
         load(1).start()
         for copy in w_loads:
             copy.wait()
         load(0).wait()
-        p_load.wait()
 
         def one(i, carry):
             a, t = lax.div(i, TILES), lax.rem(i, TILES)
@@ -197,7 +200,7 @@
             scale = jnp.where(a == 0, f32(SCALE_IN), f32(SCALE_OUT))
             prod = dot(r_buf[a, at, :], weight, ((1,), (0,)))
             prod = (prod * scale).astype(bf16).reshape(4, TOK_IMG, HID)
-            o_buf[pl.ds(4 * t, 4), a, :, 0:HID] = prod
+            o_buf[pl.ds(4 * t, 4), a] = prod
             store(a, t).start()
             return carry
 
@@ -208,10 +211,10 @@
         lax.fori_loop(0, 2 * TILES, one, 0)
         lax.fori_loop(0, 2 * TILES, finish, 0)
 
-    given = (IMAGES, 2, TOK_IMG, WIDE)
+    given = (IMAGES, 2, TOK_IMG, HID)
     return pl.pallas_call(
         body,
-        in_specs=[SMEM, HBM, HBM, ANY],
+        in_specs=[SMEM, HBM, ANY],
         out_specs=HBM,
         out_shape=pltpu.HBM(given, bf16),
         scratch_shapes=[
@@ -220,24 +223,22 @@
             pltpu.VMEM(given, bf16),
             pltpu.SemaphoreType.DMA((2,)),
             pltpu.SemaphoreType.DMA((NY,)),
-            pltpu.SemaphoreType.DMA,
             pltpu.SemaphoreType.DMA((2, TILES)),
         ],
         compiler_params=MIDDLE,
-    )(here, in_hbm(rows), in_hbm(pairs), weights)
-
-
-def activate(here, summed):
-    def body(here_ref, s_ref, o_ref):
-        pre = s_ref[0:TOK_IMG, 0:HID].astype(f32)
+    )(here, in_hbm(rows), weights)
+
+
+def activate(here, summed, pairs):
+    def body(here_ref, s_ref, p_ref, o_ref, n_ref):
+        pre = s_ref[0:TOK_IMG, :].astype(f32)
         act, slope = gelu_and_slope(pre)
         act = act.astype(bf16)
-        hid = (s_ref[TOK_IMG:, 0:HID].astype(f32) * slope).astype(bf16)
+        hid = (s_ref[TOK_IMG:, :].astype(f32) * slope).astype(bf16)
         o_ref[0:TOK_IMG, :] = act
-        o_ref[TOK_IMG : 2 * TOK_IMG, :] = hid
-        pairs = s_ref[:, HID:].astype(f32)
-        both = dot(hid, hid, ((1,), (1,))) * pairs[0:TOK_IMG] * (SCALE_IN * SCALE_IN)
-        both += dot(act, act, ((1,), (1,))) * pairs[TOK_IMG:] * (SCALE_OUT * SCALE_OUT)
+        o_ref[TOK_IMG:, :] = hid
+        both = dot(hid, hid, ((1,), (1,))) * p_ref[0:TOK_IMG] * (SCALE_IN * SCALE_IN)
+        both += dot(act, act, ((1,), (1,))) * p_ref[TOK_IMG:] * (SCALE_OUT * SCALE_OUT)
         square = jnp.sum(jnp.sum(both, axis=0, keepdims=True), axis=1, keepdims=True)
         high = square.astype(bf16).astype(f32)
         middle = (square - high).astype(bf16).astype(f32)
@@ -249,28 +250,28 @@
         kind = row - lax.div(source, 16) * 3
         value = jnp.where(kind == 0, high, jnp.where(kind == 1, middle, low))
         kept = (lane == spot) & (kind >= 0) & (kind < 3)
-        o_ref[2 * TOK_IMG :, :] = jnp.zeros((NORM_ROWS, HID), bf16)
-        o_ref[2 * TOK_IMG :, 0:128] = jnp.where(kept, value, 0.0).astype(bf16)
+        n_ref[...] = jnp.where(kept, value, 0.0).astype(bf16)
 
     return pl.pallas_call(
         body,
-        in_specs=[SMEM, VMEM],
-        out_specs=VMEM,
-        out_shape=jax.ShapeDtypeStruct((SENT, HID), bf16),
+        in_specs=[SMEM, VMEM, VMEM],
+        out_specs=[VMEM, VMEM],
+        out_shape=[
+            jax.ShapeDtypeStruct((2 * TOK_IMG, HID), bf16),
+            jax.ShapeDtypeStruct((NORM_ROWS, 128), bf16),
+        ],
         compiler_params=SMALL,
-    )(here, summed)
-
-
-def all_grads(here, weights, feats, every, place):
+    )(here, summed, pairs)
+
+
+def all_grads(here, weights, feats, every, norms, place):
     rows = FEAT + NORM_ROWS
 
-    def body(here_ref, w_ref, x_ref, e_ref, p_ref, g_ref, own_ref, oth_ref, *refs):
+    def body(here_ref, w_ref, x_ref, e_ref, n_ref, p_ref, g_ref, own_ref, oth_ref, *refs):
         w_buf, x_buf, e_buf, n_buf, place_buf, p_buf, g_buf, o_buf = refs[:8]
         w_sem, x_sem, e_sem, n_sem, p_sem, g_sem, o_sem = refs[8:]
         w_load = pltpu.make_async_copy(w_ref.at[:, 0], w_buf, w_sem)
-        n_load = pltpu.make_async_copy(
-            e_ref.at[:, pl.ds(2 * TOK_IMG, NORM_ROWS), pl.ds(0, 128)], n_buf, n_sem
-        )
+        n_load = pltpu.make_async_copy(n_ref, n_buf, n_sem)
 
         def e_load(w):
             part = pl.ds((1 - w) * TOK_IMG, TOK_IMG)
@@ -365,7 +366,7 @@
     grads = (NY, 2, FEAT, HID)
     return pl.pallas_call(
         body,
-        in_specs=[SMEM] + [HBM] * 4,
+        in_specs=[SMEM] + [HBM] * 3 + [ANY, HBM],
         out_specs=[HBM] * 3,
         out_shape=[pltpu.HBM(shape, bf16) for shape in (grads, sums, sums)],
         scratch_shapes=[
@@ -386,7 +387,7 @@
             pltpu.SemaphoreType.DMA((2, NX)),
         ],
         compiler_params=MIDDLE,
-    )(here, *map(in_hbm, (weights, feats, every, place)))
+    )(here, in_hbm(weights), in_hbm(feats), in_hbm(every), norms, in_hbm(place))
 
 
 def update(rate, in_weight, out_weight_t, grads):
@@ -492,10 +493,15 @@
     place, own[1] = lax.optimization_barrier((token_place(image_ids), own[1]))
     other = [swap_cores(piece) for piece in own]
     feats, rows, pairs = sort_tokens(here, own, other, place)
-    parts = project(here, rows, pairs, weights).reshape(IMAGES, 2 * TOK_IMG, WIDE)
+    parts = project(here, rows, weights).reshape(IMAGES, 2 * TOK_IMG, HID)
     summed = lax.psum_scatter(parts, "z", scatter_dimension=0)
-    every = lax.all_gather(activate(here, summed), "z")
-    grads, mine, theirs = all_grads(here, weights, feats, every, place)
+    pairs = exchange(pairs.reshape(IMAGES * PAIR_ROWS, TOK_IMG), "z")
+    pairs = jnp.sum(pairs.reshape(NZ, PAIR_ROWS, TOK_IMG), axis=0)
+    pairs = lax.all_gather(pairs, ("x", "core"), axis=0, tiled=True)
+    sent, norms = activate(here, summed, pairs)
+    every = lax.all_gather(sent, "z")
+    norms = exchange(jnp.tile(norms, (NZ, 1)), "z").reshape(NZ, NORM_ROWS, 128)
+    grads, mine, theirs = all_grads(here, weights, feats, every, norms, place)
     grads = exchange(grads.reshape(NY * 2 * FEAT, HID), "y").reshape(NY, 2, FEAT, HID)
     merged = (mine.astype(f32) + swap_cores(theirs).astype(f32)).astype(bf16)
     along_x = ring_sum(merged, "x").astype(bf16)

time: 224 us -> 218 us (0.973)
  waiting for transfers between devices: 128 us -> 80.4 us
  blocking collectives: 0 us -> 41.8 us
    reduce_scatter x1, waiting for transfers between devices: 52.3 us -> 14.9 us  [shards(): summed = lax.psum_scatter(parts, 'z', scatter_dimension=0)]
    all_to_all x0 -> x2, blocking collectives: none -> 27 us  [exchange(): return lax.all_to_all(value, axes, 0, 0, tiled=True)]
    all_gather x0 -> x1, blocking collectives: none -> 14.8 us  [shards(): pairs = lax.all_gather(pairs, ('x', 'core'), axis=0, tiled=True)]
    all_gather x1, waiting for transfers between devices: 46 us -> 35.2 us  [shards(): every = lax.all_gather(sent, 'z')]
where the time goes in v4:
time: 218 us; the launch traced here: 217 us
  waiting for transfers between devices  80.4 us (37%)
  blocking collectives  41.8 us (19%)
  starting transfers between devices  36.9 us (17%)
  Pallas kernels  36.2 us (17%)
  between operations  14.9 us (7%)
  local copies, waits for them, and re-layouts  3.63 us (2%)
  other arithmetic  3.61 us (2%)
    all_gather x1, waiting for transfers between devices, shards(): every = lax.all_gather(sent, 'z')  35.2 us
    ppermute x12, waiting for transfers between devices, ahead(): return lax.ppermute(value, axis, [(i, (i + step) % 4) for i in range(4)])  28.1 us
    all_to_all x2, blocking collectives, exchange(): return lax.all_to_all(value, axes, 0, 0, tiled=True)  27 us
    ppermute x12, starting transfers between devices, ahead(): return lax.ppermute(value, axis, [(i, (i + step) % 4) for i in range(4)])  19.2 us
    reduce_scatter x1, waiting for transfers between devices, shards(): summed = lax.psum_scatter(parts, 'z', scatter_dimension=0)  14.9 us
    all_gather x1, blocking collectives, shards(): pairs = lax.all_gather(pairs, ('x', 'core'), axis=0, tiled=True)  14.8 us
    pallas_call x1, Pallas kernels, all_grads(): pl.pallas_call(body, in_specs=[SMEM] + [HBM] * 3 + [ANY, HBM], out_specs=...  11.3 us
    ppermute x5, starting transfers between devices, swap_cores(): return lax.ppermute(value, 'core', [(0, 1), (1, 0)])  9.66 us
  transfers between devices with their start and end apart: 21, of which 9 were waited for; matrix products, arithmetic and copies ran while one was open for 2% of the time, Pallas kernels for 6%

profile of v4, /device:TPU:1, one launch (start us, length us, event | category | flops | bytes accessed | tf_op | source)
XLA Modules:
  0.0 217.4 jit_solution(9038266779120458625)
XLA Ops:
  8.0 2.2 %collective-permute-start = (bf16[2,192,128]{2,1,0:T(8,128)(2,1)S(1)}, bf16[2,192,128]{2,1,0:T(8,128)(2,1)S(1)}, u32[]{:S(2)}, u32[]{:S(2)}) collective-permute-start(bf16[2,192,128]{2,1,0:T(8,128)(2,1)S(1)} %get-tuple-element.39), channel_id=1, source_target_pairs={{0,64},{64,128},{128,192},{192,0},{1,65},{65,129},{129,193},{193,1... | collective-permute-start | bytes 294920 | tf_op jit(solution)/shard_map/ppermute | solution.py:463
  10.2 2.6 %collective-permute-start.1 = (bf16[2,192,128]{2,1,0:T(8,128)(2,1)S(1)}, bf16[2,192,128]{2,1,0:T(8,128)(2,1)S(1)}, u32[]{:S(2)}, u32[]{:S(2)}) collective-permute-start(bf16[2,192,128]{2,1,0:T(8,128)(2,1)S(1)} %get-tuple-element.39), channel_id=1, source_target_pairs={{0,128},{64,192},{128,0},{192,64},{1,129},{65,193},{129,1},{193,65... | collective-permute-start | bytes 294920 | tf_op jit(solution)/shard_map/ppermute | solution.py:463
  13.9 4.3 %shard_map.93 = bf16[4,2,192,768]{3,2,1,0:T(8,128)(2,1)} custom-call(f32[192,3072]{1,0:T(8,128)} %a_ref.3, f32[192,3072]{1,0:T(8,128)} %bitcast.53), custom_call_target="tpu_custom_call" | custom-call | tf_op jit(solution)/shard_map/pallas_call | solution.py:54
  18.3 3.8 %all-to-all-start = ((bf16[4,384,768]{2,1,0:T(8,128)(2,1)}), bf16[4,384,768]{2,1,0:T(8,128)(2,1)S(1)}, u32[]{:S(2)}, u32[]{:S(2)}) async-start(bf16[4,384,768]{2,1,0:T(8,128)(2,1)} %bitcast.55), calls=%async_computation | async-start | bytes 4718592 | tf_op jit(solution)/shard_map/all_to_all | solution.py:455
  23.4 2.5 %collective-permute-start.4 = (bf16[4,2,192,128]{3,2,1,0:T(8,128)(2,1)S(1)}, bf16[4,2,192,128]{3,2,1,0:T(8,128)(2,1)S(1)}, u32[]{:S(2)}, u32[]{:S(2)}) collective-permute-start(bf16[4,2,192,128]{3,2,1,0:T(8,128)(2,1)S(1)} %pad_maximum_fusion.refs_0_), channel_id=1, source_target_pairs={{0,4},{2,6},{4,0},{6,2},{1,5},{3,7},{5,1},{7,3},{8,12},{10,14},{12... | collective-permute-start | bytes 1179656 | tf_op jit(solution)/shard_map/ppermute | solution.py:463
  27.6 2.4 %collective-permute-start.6 = (bf16[4,2,192,128]{3,2,1,0:T(8,128)(2,1)S(1)}, bf16[4,2,192,128]{3,2,1,0:T(8,128)(2,1)}, u32[]{:S(2)}, u32[]{:S(2)}) collective-permute-start(bf16[4,2,192,128]{3,2,1,0:T(8,128)(2,1)S(1)} %pad_maximum_fusion.refs_0_), channel_id=1, source_target_pairs={{0,1},{1,0},{2,3},{3,2},{4,5},{5,4},{6,7},{7,6},{8,9},{9,8},{10,11... | collective-permute-start | bytes 1179656 | tf_op jit(solution)/shard_map/ppermute | solution.py:459
  30.0 2.5 %collective-permute-done.3.refs_1_ = bf16[4,2,192,128]{3,2,1,0:T(8,128)(2,1)S(1)} collective-permute-done((bf16[4,2,192,128]{3,2,1,0:T(8,128)(2,1)S(1)}, bf16[4,2,192,128]{3,2,1,0:T(8,128)(2,1)S(1)}, u32[]{:S(2)}, u32[]{:S(2)}) %collective-permute-start.3) | collective-permute-done | bytes 393248 | tf_op jit(solution)/shard_map/ppermute | solution.py:463
  33.5 3.5 %collective-permute-start.7 = (bf16[4,2,192,128]{3,2,1,0:T(8,128)(2,1)S(1)}, bf16[4,2,192,128]{3,2,1,0:T(8,128)(2,1)}, u32[]{:S(2)}, u32[]{:S(2)}) collective-permute-start(bf16[4,2,192,128]{3,2,1,0:T(8,128)(2,1)S(1)} %collective-permute-done.3.refs_1_), channel_id=1, source_target_pairs={{0,1},{1,0},{2,3},{3,2},{4,5},{5,4},{6,7},{7,6},{8,9},{9,8},{10,11... | collective-permute-start | bytes 1179656 | tf_op jit(solution)/shard_map/ppermute | solution.py:459
  37.0 4.9 %collective-permute-done.4.refs_2_ = bf16[4,2,192,128]{3,2,1,0:T(8,128)(2,1)S(1)} collective-permute-done((bf16[4,2,192,128]{3,2,1,0:T(8,128)(2,1)S(1)}, bf16[4,2,192,128]{3,2,1,0:T(8,128)(2,1)S(1)}, u32[]{:S(2)}, u32[]{:S(2)}) %collective-permute-start.4) | collective-permute-done | bytes 393248 | tf_op jit(solution)/shard_map/ppermute | solution.py:463
  41.9 2.4 %collective-permute-start.8 = (bf16[4,2,192,128]{3,2,1,0:T(8,128)(2,1)S(1)}, bf16[4,2,192,128]{3,2,1,0:T(8,128)(2,1)}, u32[]{:S(2)}, u32[]{:S(2)}) collective-permute-start(bf16[4,2,192,128]{3,2,1,0:T(8,128)(2,1)S(1)} %collective-permute-done.4.refs_2_), channel_id=1, source_target_pairs={{0,1},{1,0},{2,3},{3,2},{4,5},{5,4},{6,7},{7,6},{8,9},{9,8},{10,11... | collective-permute-start | bytes 1179656 | tf_op jit(solution)/shard_map/ppermute | solution.py:459
  46.6 8.6 %shard_map.94 = (bf16[2,768,1024]{2,1,0:T(8,128)(2,1)}, bf16[2,1024,768]{2,1,0:T(8,128)(2,1)}, f32[8,32,128]{2,1,0:T(8,128)}) custom-call(s32[4]{0:T(128)S(1)} %pad_add_fusion.here_ref, bf16[4,2,192,128]{3,2,1,0:T(8,128)(2,1)} %copy-done.2, bf16[4,2,192,128]{3,2,1,0:T(8,128)(2,1)} %copy-done.4, bf16[4,2,192,128]{3,2,1,0:T(8,128)(2,1)} %copy-done.5, ...), custom_call_target="tpu_custom_call" | custom-call | tf_op jit(solution)/shard_map/pallas_call | solution.py:145
  55.3 6.4 %shard_map.95 = bf16[8,2,128,768]{3,2,1,0:T(8,128)(2,1)} custom-call(s32[4]{0:T(128)S(1)} %pad_add_fusion.here_ref, bf16[2,1024,768]{2,1,0:T(8,128)(2,1)} %get-tuple-element.23.r_ref, bf16[4,2,192,768]{3,2,1,0:T(8,128)(2,1)S(1)} %bitcast.48), custom_call_target="tpu_custom_call" | custom-call | tf_op jit(solution)/shard_map/pallas_call | solution.py:215
  62.6 15.9 %all_to_all.30 = f32[8,32,128]{2,1,0:T(8,128)S(1)} all-to-all(f32[8,32,128]{2,1,0:T(8,128)S(1)} %copy-done.6), channel_id=1, replica_groups=mesh['y'=4,'z'=8,'x'=4,'core'=2] {'z'}, dimensions={0} | all-to-all | bytes 262144 | tf_op jit(solution)/shard_map/all_to_all | solution.py:455
  78.5 14.8 %all_gather.9.p_ref = f32[256,128]{1,0:T(8,128)S(1)} all-gather(f32[32,128]{1,0:T(8,128)S(1)} %reduce_sum.28), channel_id=1, replica_groups=mesh['y'=4,'z'=8,'x'=4,'core'=2] {'x','core'}, dimensions={0}, use_global_device_ids=true | all-gather | bytes 147456 | tf_op jit(solution)/shard_map/all_gather | solution.py:500
  93.3 14.9 %reduce-scatter.2.cloned.1.call-done = bf16[1,256,768]{2,1,0:T(8,128)(2,1)} async-done(((bf16[8,256,768]{2,1,0:T(8,128)(2,1)}), bf16[1,256,768]{2,1,0:T(8,128)(2,1)}) %reduce-scatter.2.cloned.1.call-update) | async-done | bytes 393232 | tf_op jit(solution)/shard_map/reduce_scatter | solution.py:497
  109.2 1.7 shard_map.96
  111.0 11.1 %all_to_all.31.n_ref = bf16[8,16,128]{2,1,0:T(8,128)(2,1)S(1)} all-to-all(bf16[8,16,128]{2,1,0:T(8,128)(2,1)S(1)} %tile.2), channel_id=1, replica_groups=mesh['y'=4,'z'=8,'x'=4,'core'=2] {'z'}, dimensions={0} | all-to-all | bytes 65536 | tf_op jit(solution)/shard_map/all_to_all | solution.py:455
  122.1 35.2 %all-gather.3.cloned.1.call-done = bf16[2048,768]{1,0:T(8,128)(2,1)} async-done(((bf16[256,768]{1,0:T(8,128)(2,1)}), bf16[2048,768]{1,0:T(8,128)(2,1)}) %all-gather.3.cloned.1.call-update) | async-done | bytes 3145744 | tf_op jit(solution)/shard_map/all_gather | solution.py:502
  157.3 11.3 %shard_map.97 = (bf16[4,2,192,768]{3,2,1,0:T(8,128)(2,1)}, bf16[4,4,208,128]{3,2,1,0:T(8,128)(2,1)}, bf16[4,4,208,128]{3,2,1,0:T(8,128)(2,1)}) custom-call(s32[4]{0:T(128)S(1)} %pad_add_fusion.here_ref, bf16[4,2,192,768]{3,2,1,0:T(8,128)(2,1)} %bitcast.49, bf16[2,768,1024]{2,1,0:T(8,128)(2,1)} %get-tuple-element.22.x_ref, bf16[8,256,768]{2,1,0:T(8,128)(2,1)} %bitcast.56, ...), custom_call_target="tpu_custom_call" | custom-call | tf_op jit(solution)/shard_map/pallas_call | solution.py:367
  169.8 4.1 %all-to-all-start.3 = ((bf16[4,384,768]{2,1,0:T(8,128)(2,1)}), bf16[4,384,768]{2,1,0:T(8,128)(2,1)S(1)}, u32[]{:S(2)}, u32[]{:S(2)}) async-start(bf16[4,384,768]{2,1,0:T(8,128)(2,1)} %bitcast.57), calls=%async_computation.4 | async-start | bytes 4718592 | tf_op jit(solution)/shard_map/all_to_all | solution.py:455
  179.6 3.6 %collective-permute-done.11 = bf16[4,208,128]{2,1,0:T(8,128)(2,1)S(1)} collective-permute-done((bf16[4,208,128]{2,1,0:T(8,128)(2,1)S(1)}, bf16[4,208,128]{2,1,0:T(8,128)(2,1)S(1)}, u32[]{:S(2)}, u32[]{:S(2)}) %collective-permute-start.11) | collective-permute-done | bytes 213024 | tf_op jit(solution)/shard_map/ppermute | solution.py:463
  183.2 5.5 %collective-permute-done.13 = bf16[4,208,128]{2,1,0:T(8,128)(2,1)S(1)} collective-permute-done((bf16[4,208,128]{2,1,0:T(8,128)(2,1)S(1)}, bf16[4,208,128]{2,1,0:T(8,128)(2,1)S(1)}, u32[]{:S(2)}, u32[]{:S(2)}) %collective-permute-start.13) | collective-permute-done | bytes 213024 | tf_op jit(solution)/shard_map/ppermute | solution.py:463
  193.7 11.6 %collective-permute-done.14 = bf16[208,128]{1,0:T(8,128)(2,1)S(1)} collective-permute-done((bf16[208,128]{1,0:T(8,128)(2,1)S(1)}, bf16[208,128]{1,0:T(8,128)(2,1)S(1)}, u32[]{:S(2)}, u32[]{:S(2)}) %collective-permute-start.14) | collective-permute-done | bytes 53280 | tf_op jit(solution)/shard_map/ppermute | solution.py:463
  206.6 4.0 %shard_map.98 = (f32[192,3072]{1,0:T(8,128)}, f32[192,3072]{1,0:T(8,128)}) custom-call(f32[1]{0:T(128)S(6)} %copy.10.rate_ref, f32[192,3072]{1,0:T(8,128)} %a_ref.3, f32[192,3072]{1,0:T(8,128)} %bitcast.54, bf16[4,2,192,768]{3,2,1,0:T(8,128)(2,1)S(1)} %bitcast.50), custom_call_target="tpu_custom_call" | custom-call | tf_op jit(solution)/shard_map/pallas_call | solution.py:433
  (63 shorter events, 22.7 us)
Async XLA Ops:
  8.0 10.2 %collective-permute-start = (bf16[2,192,128]{2,1,0:T(8,128)(2,1)S(1)}, bf16[2,192,128]{2,1,0:T(8,128)(2,1)S(1)}, u32[]{:S(2)}, u32[]{:S(2)}) collective-permute-start(bf16[2,192,128]{2,1,0:T(8,128)(2,1)S(1)} %get-tuple-element.39), channel_id=1, source_target_pairs={{0,64},{64,128},{128,192},{192,0},{1,65},{65,129},{129,193},{193,1... | collective-permute-start | bytes 294920 | tf_op jit(solution)/shard_map/ppermute | solution.py:463
  10.2 8.0 %collective-permute-start.1 = (bf16[2,192,128]{2,1,0:T(8,128)(2,1)S(1)}, bf16[2,192,128]{2,1,0:T(8,128)(2,1)S(1)}, u32[]{:S(2)}, u32[]{:S(2)}) collective-permute-start(bf16[2,192,128]{2,1,0:T(8,128)(2,1)S(1)} %get-tuple-element.39), channel_id=1, source_target_pairs={{0,128},{64,192},{128,0},{192,64},{1,129},{65,193},{129,1},{193,65... | collective-permute-start | bytes 294920 | tf_op jit(solution)/shard_map/ppermute | solution.py:463
  12.8 5.4 %collective-permute-start.2 = (bf16[2,192,128]{2,1,0:T(8,128)(2,1)S(1)}, bf16[2,192,128]{2,1,0:T(8,128)(2,1)S(1)}, u32[]{:S(2)}, u32[]{:S(2)}) collective-permute-start(bf16[2,192,128]{2,1,0:T(8,128)(2,1)S(1)} %get-tuple-element.39), channel_id=1, source_target_pairs={{0,192},{64,0},{128,64},{192,128},{1,193},{65,1},{129,65},{193,129... | collective-permute-start | bytes 294920 | tf_op jit(solution)/shard_map/ppermute | solution.py:463
  18.3 9.3 %copy-start.2 = (bf16[4,2,192,128]{3,2,1,0:T(8,128)(2,1)}, bf16[4,2,192,128]{3,2,1,0:T(8,128)(2,1)S(1)}, u32[]{:S(2)}) copy-start(bf16[4,2,192,128]{3,2,1,0:T(8,128)(2,1)S(1)} %pad_maximum_fusion.refs_0_) | copy-start | bytes 1179652
  18.3 8.7 %copy-start.7 = (s32[1024]{0:T(1024)S(1)}, s32[1024]{0:T(1024)}, u32[]{:S(2)}) copy-start(s32[1024]{0:T(1024)} %param.8) | copy-start | bytes 12292
  18.3 37.0 %all-to-all-start = ((bf16[4,384,768]{2,1,0:T(8,128)(2,1)}), bf16[4,384,768]{2,1,0:T(8,128)(2,1)S(1)}, u32[]{:S(2)}, u32[]{:S(2)}) async-start(bf16[4,384,768]{2,1,0:T(8,128)(2,1)} %bitcast.55), calls=%async_computation | async-start | bytes 4718592 | tf_op jit(solution)/shard_map/all_to_all | solution.py:455
  22.1 86.2 %reduce-scatter.2.cloned.1.call-start = ((), (), s32[]{:S(2)}) async-start(), calls=%async_computation.5 | async-start | bytes 3538944 | tf_op jit(solution)/shard_map/reduce_scatter | solution.py:497
  22.1 10.4 %collective-permute-start.3 = (bf16[4,2,192,128]{3,2,1,0:T(8,128)(2,1)S(1)}, bf16[4,2,192,128]{3,2,1,0:T(8,128)(2,1)S(1)}, u32[]{:S(2)}, u32[]{:S(2)}) collective-permute-start(bf16[4,2,192,128]{3,2,1,0:T(8,128)(2,1)S(1)} %pad_maximum_fusion.refs_0_), channel_id=1, source_target_pairs={{0,2},{2,4},{4,6},{6,0},{1,3},{3,5},{5,7},{7,1},{8,10},{10,12},{12... | collective-permute-start | bytes 1179656 | tf_op jit(solution)/shard_map/ppermute | solution.py:463
  23.4 18.5 %collective-permute-start.4 = (bf16[4,2,192,128]{3,2,1,0:T(8,128)(2,1)S(1)}, bf16[4,2,192,128]{3,2,1,0:T(8,128)(2,1)S(1)}, u32[]{:S(2)}, u32[]{:S(2)}) collective-permute-start(bf16[4,2,192,128]{3,2,1,0:T(8,128)(2,1)S(1)} %pad_maximum_fusion.refs_0_), channel_id=1, source_target_pairs={{0,4},{2,6},{4,0},{6,2},{1,5},{3,7},{5,1},{7,3},{8,12},{10,14},{12... | collective-permute-start | bytes 1179656 | tf_op jit(solution)/shard_map/ppermute | solution.py:463
  25.9 18.5 %collective-permute-start.5 = (bf16[4,2,192,128]{3,2,1,0:T(8,128)(2,1)S(1)}, bf16[4,2,192,128]{3,2,1,0:T(8,128)(2,1)}, u32[]{:S(2)}, u32[]{:S(2)}) collective-permute-start(bf16[4,2,192,128]{3,2,1,0:T(8,128)(2,1)S(1)} %pad_maximum_fusion.refs_0_), channel_id=1, source_target_pairs={{0,6},{2,0},{4,2},{6,4},{1,7},{3,1},{5,3},{7,5},{8,14},{10,8},{12,... | collective-permute-start | bytes 1179656 | tf_op jit(solution)/shard_map/ppermute | solution.py:463
  27.6 17.0 %collective-permute-start.6 = (bf16[4,2,192,128]{3,2,1,0:T(8,128)(2,1)S(1)}, bf16[4,2,192,128]{3,2,1,0:T(8,128)(2,1)}, u32[]{:S(2)}, u32[]{:S(2)}) collective-permute-start(bf16[4,2,192,128]{3,2,1,0:T(8,128)(2,1)S(1)} %pad_maximum_fusion.refs_0_), channel_id=1, source_target_pairs={{0,1},{1,0},{2,3},{3,2},{4,5},{5,4},{6,7},{7,6},{8,9},{9,8},{10,11... | collective-permute-start | bytes 1179656 | tf_op jit(solution)/shard_map/ppermute | solution.py:459
  32.5 14.1 %copy-start.4 = (bf16[4,2,192,128]{3,2,1,0:T(8,128)(2,1)}, bf16[4,2,192,128]{3,2,1,0:T(8,128)(2,1)S(1)}, u32[]{:S(2)}) copy-start(bf16[4,2,192,128]{3,2,1,0:T(8,128)(2,1)S(1)} %collective-permute-done.3.refs_1_) | copy-start | bytes 1179652
  33.5 11.0 %collective-permute-start.7 = (bf16[4,2,192,128]{3,2,1,0:T(8,128)(2,1)S(1)}, bf16[4,2,192,128]{3,2,1,0:T(8,128)(2,1)}, u32[]{:S(2)}, u32[]{:S(2)}) collective-permute-start(bf16[4,2,192,128]{3,2,1,0:T(8,128)(2,1)S(1)} %collective-permute-done.3.refs_1_), channel_id=1, source_target_pairs={{0,1},{1,0},{2,3},{3,2},{4,5},{5,4},{6,7},{7,6},{8,9},{9,8},{10,11... | collective-permute-start | bytes 1179656 | tf_op jit(solution)/shard_map/ppermute | solution.py:459
  41.9 3.9 %collective-permute-start.8 = (bf16[4,2,192,128]{3,2,1,0:T(8,128)(2,1)S(1)}, bf16[4,2,192,128]{3,2,1,0:T(8,128)(2,1)}, u32[]{:S(2)}, u32[]{:S(2)}) collective-permute-start(bf16[4,2,192,128]{3,2,1,0:T(8,128)(2,1)S(1)} %collective-permute-done.4.refs_2_), channel_id=1, source_target_pairs={{0,1},{1,0},{2,3},{3,2},{4,5},{5,4},{6,7},{7,6},{8,9},{9,8},{10,11... | collective-permute-start | bytes 1179656 | tf_op jit(solution)/shard_map/ppermute | solution.py:459
  44.4 2.3 %collective-permute-start.9 = (bf16[4,2,192,128]{3,2,1,0:T(8,128)(2,1)}, bf16[4,2,192,128]{3,2,1,0:T(8,128)(2,1)}, u32[]{:S(2)}, u32[]{:S(2)}) collective-permute-start(bf16[4,2,192,128]{3,2,1,0:T(8,128)(2,1)} %collective-permute-done.5.refs_3_), channel_id=1, source_target_pairs={{0,1},{1,0},{2,3},{3,2},{4,5},{5,4},{6,7},{7,6},{8,9},{9,8},{10,11... | collective-permute-start | bytes 1179656 | tf_op jit(solution)/shard_map/ppermute | solution.py:459
  61.7 95.6 %all-gather.3.cloned.1.call-start = ((), (), s32[]{:S(2)}) async-start(), calls=%async_computation.6 | async-start | bytes 3538944 | tf_op jit(solution)/shard_map/all_gather | solution.py:502
  168.6 5.3 %collective-permute-start.10 = (bf16[4,4,208,128]{3,2,1,0:T(8,128)(2,1)}, bf16[4,4,208,128]{3,2,1,0:T(8,128)(2,1)}, u32[]{:S(2)}, u32[]{:S(2)}) collective-permute-start(bf16[4,4,208,128]{3,2,1,0:T(8,128)(2,1)} %get-tuple-element.28), channel_id=1, source_target_pairs={{0,1},{1,0},{2,3},{3,2},{4,5},{5,4},{6,7},{7,6},{8,9},{9,8},{10,11... | collective-permute-start | bytes 2555912 | tf_op jit(solution)/shard_map/ppermute | solution.py:459
  169.8 36.8 %all-to-all-start.3 = ((bf16[4,384,768]{2,1,0:T(8,128)(2,1)}), bf16[4,384,768]{2,1,0:T(8,128)(2,1)S(1)}, u32[]{:S(2)}, u32[]{:S(2)}) async-start(bf16[4,384,768]{2,1,0:T(8,128)(2,1)} %bitcast.57), calls=%async_computation.4 | async-start | bytes 4718592 | tf_op jit(solution)/shard_map/all_to_all | solution.py:455
  175.4 7.8 %collective-permute-start.11 = (bf16[4,208,128]{2,1,0:T(8,128)(2,1)S(1)}, bf16[4,208,128]{2,1,0:T(8,128)(2,1)S(1)}, u32[]{:S(2)}, u32[]{:S(2)}) collective-permute-start(bf16[4,208,128]{2,1,0:T(8,128)(2,1)S(1)} %get-tuple-element.32), channel_id=1, source_target_pairs={{0,2},{2,4},{4,6},{6,0},{1,3},{3,5},{5,7},{7,1},{8,10},{10,12},{12... | collective-permute-start | bytes 638984 | tf_op jit(solution)/shard_map/ppermute | solution.py:463
  176.6 6.6 %collective-permute-start.12 = (bf16[4,208,128]{2,1,0:T(8,128)(2,1)S(1)}, bf16[4,208,128]{2,1,0:T(8,128)(2,1)S(1)}, u32[]{:S(2)}, u32[]{:S(2)}) collective-permute-start(bf16[4,208,128]{2,1,0:T(8,128)(2,1)S(1)} %get-tuple-element.34), channel_id=1, source_target_pairs={{0,6},{2,0},{4,2},{6,4},{1,7},{3,1},{5,3},{7,5},{8,14},{10,8},{12,... | collective-permute-start | bytes 638984 | tf_op jit(solution)/shard_map/ppermute | solution.py:463
  178.1 10.5 %collective-permute-start.13 = (bf16[4,208,128]{2,1,0:T(8,128)(2,1)S(1)}, bf16[4,208,128]{2,1,0:T(8,128)(2,1)S(1)}, u32[]{:S(2)}, u32[]{:S(2)}) collective-permute-start(bf16[4,208,128]{2,1,0:T(8,128)(2,1)S(1)} %get-tuple-element.33), channel_id=1, source_target_pairs={{0,4},{2,6},{4,0},{6,2},{1,5},{3,7},{5,1},{7,3},{8,12},{10,14},{12... | collective-permute-start | bytes 638984 | tf_op jit(solution)/shard_map/ppermute | solution.py:463
  188.8 16.4 %collective-permute-start.14 = (bf16[208,128]{1,0:T(8,128)(2,1)S(1)}, bf16[208,128]{1,0:T(8,128)(2,1)S(1)}, u32[]{:S(2)}, u32[]{:S(2)}) collective-permute-start(bf16[208,128]{1,0:T(8,128)(2,1)S(1)} %get-tuple-element.35), channel_id=1, source_target_pairs={{0,64},{64,128},{128,192},{192,0},{1,65},{65,129},{129,193},{193,1... | collective-permute-start | bytes 159752 | tf_op jit(solution)/shard_map/ppermute | solution.py:463
  190.0 15.2 %collective-permute-start.15 = (bf16[208,128]{1,0:T(8,128)(2,1)S(1)}, bf16[208,128]{1,0:T(8,128)(2,1)S(1)}, u32[]{:S(2)}, u32[]{:S(2)}) collective-permute-start(bf16[208,128]{1,0:T(8,128)(2,1)S(1)} %get-tuple-element.37), channel_id=1, source_target_pairs={{0,192},{64,0},{128,64},{192,128},{1,193},{65,1},{129,65},{193,129... | collective-permute-start | bytes 159752 | tf_op jit(solution)/shard_map/ppermute | solution.py:463
  191.6 13.7 %collective-permute-start.16 = (bf16[208,128]{1,0:T(8,128)(2,1)S(1)}, bf16[208,128]{1,0:T(8,128)(2,1)S(1)}, u32[]{:S(2)}, u32[]{:S(2)}) collective-permute-start(bf16[208,128]{1,0:T(8,128)(2,1)S(1)} %get-tuple-element.36), channel_id=1, source_target_pairs={{0,128},{64,192},{128,0},{192,64},{1,129},{65,193},{129,1},{193,65... | collective-permute-start | bytes 159752 | tf_op jit(solution)/shard_map/ppermute | solution.py:463
  (5 other events, 17.2 us)
Sparse Core Ops, SparseCore 0:
  61.9 46.3 reduce-scatter.1
  111.1 46.2 all-gather.2

commit v5 on v4

--- a/solution.py
+++ b/solution.py
@@ -47,16 +47,49 @@
 
 
 def split_hidden(in_weight, out_weight_t):
-    def body(a_ref, b_ref, o_ref):
-        o_ref[0, 0] = a_ref[...].astype(bf16)
-        o_ref[0, 1] = b_ref[...].astype(bf16)
+    def body(a_ref, b_ref, o_ref, w_buf, o_buf, w_sem, o_sem):
+        def loads(y):
+            cols = pl.ds(pl.multiple_of(y * HID, HID), HID)
+            return (
+                pltpu.make_async_copy(a_ref.at[:, cols], w_buf.at[0, y], w_sem.at[0, y]),
+                pltpu.make_async_copy(b_ref.at[:, cols], w_buf.at[1, y], w_sem.at[1, y]),
+            )
+
+        def store(y):
+            return pltpu.make_async_copy(o_buf.at[y], o_ref.at[y], o_sem.at[y])
+
+        def begin(y, carry):
+            for copy in loads(y):
+                copy.start()
+            return carry
+
+        def one(y, carry):
+            for copy in loads(y):
+                copy.wait()
+            for w in range(2):
+                o_buf[y, w] = w_buf[w, y].astype(bf16)
+            store(y).start()
+            return carry
+
+        def finish(y, carry):
+            store(y).wait()
+            return carry
+
+        lax.fori_loop(0, NY, begin, 0)
+        lax.fori_loop(0, NY, one, 0)
+        lax.fori_loop(0, NY, finish, 0)
 
     return pl.pallas_call(
         body,
-        grid=(NY,),
-        in_specs=[pl.BlockSpec((FEAT, HID), lambda i: (0, i))] * 2,
-        out_specs=pl.BlockSpec((1, 2, FEAT, HID), lambda i: (i, 0, 0, 0)),
+        in_specs=[HBM] * 2,
+        out_specs=HBM,
         out_shape=pltpu.HBM((NY, 2, FEAT, HID), bf16),
+        scratch_shapes=[
+            pltpu.VMEM((2, NY, FEAT, HID), f32),
+            pltpu.VMEM((NY, 2, FEAT, HID), bf16),
+            pltpu.SemaphoreType.DMA((2, NY)),
+            pltpu.SemaphoreType.DMA((NY,)),
+        ],
         compiler_params=MIDDLE,
     )(in_hbm(in_weight), in_hbm(out_weight_t))
 
@@ -208,7 +241,7 @@
             store(lax.div(i, TILES), lax.rem(i, TILES)).wait()
             return carry
 
-        lax.fori_loop(0, 2 * TILES, one, 0)
+        lax.fori_loop(0, 2 * TILES, one, 0, unroll=True)
         lax.fori_loop(0, 2 * TILES, finish, 0)
 
     given = (IMAGES, 2, TOK_IMG, HID)
@@ -308,26 +341,29 @@
         e_load(0).wait()
         w_load.wait()
 
-        def one(x, carry):
-            at = pl.multiple_of(x * PAIR, PAIR)
+        def one(i, carry):
+            at = pl.multiple_of(i * TILE, TILE)
             hidden = e_buf[0].reshape(TOKENS, HID)
-            placed = dot(p_buf[pl.ds(at, PAIR), :], hidden, ((1,), (0,))).astype(bf16)
+            placed = dot(p_buf[pl.ds(at, TILE), :], hidden, ((1,), (0,))).astype(bf16)
             weight = w_buf[...].reshape(NY * FEAT, HID)
             grad = (dot(weight, placed, ((1,), (1,))) * SCALE_IN).astype(bf16)
-            u = lax.rem(x - here_ref[2] + NX, NX)
-            for core in range(2):
-                o = lax.rem(core + here_ref[3], 2)
-                half = grad[:, core * 128 : (core + 1) * 128]
-                for y in range(NY):
-                    v = lax.rem(y - here_ref[0] + NY, NY)
-                    o_buf[o, u, v, 0:FEAT, :] = half[y * FEAT : (y + 1) * FEAT]
-                    o_buf[o, u, v, FEAT:, :] = norms
-            for copy in stores(x):
-                copy.start()
-            return carry
-
-        lax.fori_loop(0, NX, one, 0)
-        tile = 256
+            for k in range(TILE // PAIR):
+                x = TILE // PAIR * i + k
+                u = lax.rem(x - here_ref[2] + NX, NX)
+                for core in range(2):
+                    o = lax.rem(core + here_ref[3], 2)
+                    lane = k * PAIR + core * 128
+                    half = grad[:, lane : lane + 128]
+                    for y in range(NY):
+                        v = lax.rem(y - here_ref[0] + NY, NY)
+                        o_buf[o, u, v, 0:FEAT, :] = half[y * FEAT : (y + 1) * FEAT]
+                        o_buf[o, u, v, FEAT:, :] = norms
+                for copy in stores(x):
+                    copy.start()
+            return carry
+
+        lax.fori_loop(0, TILES, one, 0)
+        tile = HID
         steps = HID // tile
 
         def two(i, carry):
@@ -391,7 +427,10 @@
 
 
 def update(rate, in_weight, out_weight_t, grads):
-    def body(rate_ref, a_ref, b_ref, g_ref, a_out, b_out, w_buf, g_buf, w_sem, g_sem, o_sem):
+    def body(rate_ref, a_ref, b_ref, g_ref, a_out, b_out, zero_out, *refs):
+        w_buf, g_buf, w_sem, g_sem, o_sem = refs
+        zero_out[...] = jnp.zeros((8, 128), f32)
+
         def loads(y):
             cols = pl.ds(pl.multiple_of(y * HID, HID), HID)
             return (
@@ -433,8 +472,9 @@
     return pl.pallas_call(
         body,
         in_specs=[SMEM, HBM, HBM, ANY],
-        out_specs=[HBM] * 2,
-        out_shape=[pltpu.HBM(in_weight.shape, f32)] * 2,
+        out_specs=[HBM, HBM, VMEM],
+        out_shape=[pltpu.HBM(in_weight.shape, f32)] * 2
+        + [jax.ShapeDtypeStruct((8, 128), f32)],
         scratch_shapes=[
             pltpu.VMEM((2, NY, FEAT, HID), f32),
             pltpu.VMEM((NY, 2, FEAT, HID), bf16),
@@ -505,11 +545,11 @@
     grads = exchange(grads.reshape(NY * 2 * FEAT, HID), "y").reshape(NY, 2, FEAT, HID)
     merged = (mine.astype(f32) + swap_cores(theirs).astype(f32)).astype(bf16)
     along_x = ring_sum(merged, "x").astype(bf16)
-    got = ring_sum(along_x, "y")
+    in_next, out_next, zero = update(learn_rate, in_weight, out_weight_t, grads)
+    got = ring_sum(along_x, "y") + zero[0, 0]
     input_grad = got[:FEAT].astype(bf16).T
     example_sq = jnp.sum(got[FEAT:].reshape(NORM_ROWS * 16, IMAGES), axis=0)
     example_norm = 0.5 * jnp.log(example_sq + 1e-06)
-    in_next, out_next = update(learn_rate, in_weight, out_weight_t, grads)
     return (input_grad, in_next, out_next.T, example_norm)
 
 

time: 218 us -> 215 us (0.986)
  Pallas kernels: 36.2 us -> 33.6 us
  waiting for transfers between devices: 80.4 us -> 78 us
    ppermute x12, waiting for transfers between devices: 28.1 us -> 16.2 us  [ahead(): return lax.ppermute(value, axis, [(i, (i + step) % 4) for i in range(4)])]
    all_to_all x2, waiting for transfers between devices: 0.01 us -> 9.27 us  [exchange(): return lax.all_to_all(value, axes, 0, 0, tiled=True)]
  transfers between devices with their start and end apart: 21 -> 21, of which waited for: 9 -> 9; matrix products, arithmetic and copies ran while one was open for 2% -> 2% of each run, Pallas kernels for 6% -> 8%
where the time goes in v5:
time: 215 us; the launch traced here: 214 us
  waiting for transfers between devices  78 us (36%)
  blocking collectives  41.7 us (19%)
  starting transfers between devices  37 us (17%)
  Pallas kernels  33.6 us (16%)
  between operations  14.9 us (7%)
  other arithmetic  4.26 us (2%)
  local copies, waits for them, and re-layouts  4.15 us (2%)
    all_gather x1, waiting for transfers between devices, shards(): every = lax.all_gather(sent, 'z')  35.4 us
    all_to_all x2, blocking collectives, exchange(): return lax.all_to_all(value, axes, 0, 0, tiled=True)  26.8 us
    ppermute x12, starting transfers between devices, ahead(): return lax.ppermute(value, axis, [(i, (i + step) % 4) for i in range(4)])  19.2 us
    ppermute x12, waiting for transfers between devices, ahead(): return lax.ppermute(value, axis, [(i, (i + step) % 4) for i in range(4)])  16.2 us
    reduce_scatter x1, waiting for transfers between devices, shards(): summed = lax.psum_scatter(parts, 'z', scatter_dimension=0)  15 us
    all_gather x1, blocking collectives, shards(): pairs = lax.all_gather(pairs, ('x', 'core'), axis=0, tiled=True)  14.8 us
    ppermute x5, starting transfers between devices, swap_cores(): return lax.ppermute(value, 'core', [(0, 1), (1, 0)])  9.77 us
    pallas_call x1, Pallas kernels, all_grads(): pl.pallas_call(body, in_specs=[SMEM] + [HBM] * 3 + [ANY, HBM], out_specs=...  9.76 us
  transfers between devices with their start and end apart: 21, of which 9 were waited for; matrix products, arithmetic and copies ran while one was open for 2% of the time, Pallas kernels for 8%

profile of v5, /device:TPU:1, one launch (start us, length us, event | category | flops | bytes accessed | tf_op | source)
XLA Modules:
  0.0 213.6 jit_solution(2415026706646828166)
XLA Ops:
  8.0 2.2 %collective-permute-start = (bf16[2,192,128]{2,1,0:T(8,128)(2,1)S(1)}, bf16[2,192,128]{2,1,0:T(8,128)(2,1)S(1)}, u32[]{:S(2)}, u32[]{:S(2)}) collective-permute-start(bf16[2,192,128]{2,1,0:T(8,128)(2,1)S(1)} %get-tuple-element.41), channel_id=1, source_target_pairs={{0,64},{64,128},{128,192},{192,0},{1,65},{65,129},{129,193},{193,1... | collective-permute-start | bytes 294920 | tf_op jit(solution)/shard_map/ppermute | solution.py:503
  10.2 2.6 %collective-permute-start.1 = (bf16[2,192,128]{2,1,0:T(8,128)(2,1)S(1)}, bf16[2,192,128]{2,1,0:T(8,128)(2,1)S(1)}, u32[]{:S(2)}, u32[]{:S(2)}) collective-permute-start(bf16[2,192,128]{2,1,0:T(8,128)(2,1)S(1)} %get-tuple-element.41), channel_id=1, source_target_pairs={{0,128},{64,192},{128,0},{192,64},{1,129},{65,193},{129,1},{193,65... | collective-permute-start | bytes 294920 | tf_op jit(solution)/shard_map/ppermute | solution.py:503
  13.9 3.5 %shard_map.93 = bf16[4,2,192,768]{3,2,1,0:T(8,128)(2,1)} custom-call(f32[192,3072]{1,0:T(8,128)} %a_ref.3, f32[192,3072]{1,0:T(8,128)} %bitcast.54), custom_call_target="tpu_custom_call" | custom-call | tf_op jit(solution)/shard_map/pallas_call | solution.py:82
  17.5 3.8 %all-to-all-start = ((bf16[4,384,768]{2,1,0:T(8,128)(2,1)}), bf16[4,384,768]{2,1,0:T(8,128)(2,1)S(1)}, u32[]{:S(2)}, u32[]{:S(2)}) async-start(bf16[4,384,768]{2,1,0:T(8,128)(2,1)} %bitcast.56), calls=%async_computation | async-start | bytes 4718592 | tf_op jit(solution)/shard_map/all_to_all | solution.py:495
  22.7 2.5 %collective-permute-start.4 = (bf16[4,2,192,128]{3,2,1,0:T(8,128)(2,1)S(1)}, bf16[4,2,192,128]{3,2,1,0:T(8,128)(2,1)S(1)}, u32[]{:S(2)}, u32[]{:S(2)}) collective-permute-start(bf16[4,2,192,128]{3,2,1,0:T(8,128)(2,1)S(1)} %pad_maximum_fusion.refs_0_), channel_id=1, source_target_pairs={{0,4},{2,6},{4,0},{6,2},{1,5},{3,7},{5,1},{7,3},{8,12},{10,14},{12... | collective-permute-start | bytes 1179656 | tf_op jit(solution)/shard_map/ppermute | solution.py:503
  26.8 2.4 %collective-permute-start.6 = (bf16[4,2,192,128]{3,2,1,0:T(8,128)(2,1)S(1)}, bf16[4,2,192,128]{3,2,1,0:T(8,128)(2,1)}, u32[]{:S(2)}, u32[]{:S(2)}) collective-permute-start(bf16[4,2,192,128]{3,2,1,0:T(8,128)(2,1)S(1)} %pad_maximum_fusion.refs_0_), channel_id=1, source_target_pairs={{0,1},{1,0},{2,3},{3,2},{4,5},{5,4},{6,7},{7,6},{8,9},{9,8},{10,11... | collective-permute-start | bytes 1179656 | tf_op jit(solution)/shard_map/ppermute | solution.py:499
  29.2 2.2 %collective-permute-done.3.refs_1_ = bf16[4,2,192,128]{3,2,1,0:T(8,128)(2,1)S(1)} collective-permute-done((bf16[4,2,192,128]{3,2,1,0:T(8,128)(2,1)S(1)}, bf16[4,2,192,128]{3,2,1,0:T(8,128)(2,1)S(1)}, u32[]{:S(2)}, u32[]{:S(2)}) %collective-permute-start.3) | collective-permute-done | bytes 393248 | tf_op jit(solution)/shard_map/ppermute | solution.py:503
  32.4 3.8 %collective-permute-start.7 = (bf16[4,2,192,128]{3,2,1,0:T(8,128)(2,1)S(1)}, bf16[4,2,192,128]{3,2,1,0:T(8,128)(2,1)}, u32[]{:S(2)}, u32[]{:S(2)}) collective-permute-start(bf16[4,2,192,128]{3,2,1,0:T(8,128)(2,1)S(1)} %collective-permute-done.3.refs_1_), channel_id=1, source_target_pairs={{0,1},{1,0},{2,3},{3,2},{4,5},{5,4},{6,7},{7,6},{8,9},{9,8},{10,11... | collective-permute-start | bytes 1179656 | tf_op jit(solution)/shard_map/ppermute | solution.py:499
  36.2 4.9 %collective-permute-done.4.refs_2_ = bf16[4,2,192,128]{3,2,1,0:T(8,128)(2,1)S(1)} collective-permute-done((bf16[4,2,192,128]{3,2,1,0:T(8,128)(2,1)S(1)}, bf16[4,2,192,128]{3,2,1,0:T(8,128)(2,1)S(1)}, u32[]{:S(2)}, u32[]{:S(2)}) %collective-permute-start.4) | collective-permute-done | bytes 393248 | tf_op jit(solution)/shard_map/ppermute | solution.py:503
  41.2 2.4 %collective-permute-start.8 = (bf16[4,2,192,128]{3,2,1,0:T(8,128)(2,1)S(1)}, bf16[4,2,192,128]{3,2,1,0:T(8,128)(2,1)}, u32[]{:S(2)}, u32[]{:S(2)}) collective-permute-start(bf16[4,2,192,128]{3,2,1,0:T(8,128)(2,1)S(1)} %collective-permute-done.4.refs_2_), channel_id=1, source_target_pairs={{0,1},{1,0},{2,3},{3,2},{4,5},{5,4},{6,7},{7,6},{8,9},{9,8},{10,11... | collective-permute-start | bytes 1179656 | tf_op jit(solution)/shard_map/ppermute | solution.py:499
  45.9 8.6 %shard_map.94 = (bf16[2,768,1024]{2,1,0:T(8,128)(2,1)}, bf16[2,1024,768]{2,1,0:T(8,128)(2,1)}, f32[8,32,128]{2,1,0:T(8,128)}) custom-call(s32[4]{0:T(128)S(1)} %pad_add_fusion.here_ref, bf16[4,2,192,128]{3,2,1,0:T(8,128)(2,1)} %copy-done.2, bf16[4,2,192,128]{3,2,1,0:T(8,128)(2,1)} %copy-done.4, bf16[4,2,192,128]{3,2,1,0:T(8,128)(2,1)} %copy-done.5, ...), custom_call_target="tpu_custom_call" | custom-call | tf_op jit(solution)/shard_map/pallas_call | solution.py:178
  54.5 6.1 %shard_map.95 = bf16[8,2,128,768]{3,2,1,0:T(8,128)(2,1)} custom-call(s32[4]{0:T(128)S(1)} %pad_add_fusion.here_ref, bf16[2,1024,768]{2,1,0:T(8,128)(2,1)} %get-tuple-element.24.r_ref, bf16[4,2,192,768]{3,2,1,0:T(8,128)(2,1)S(1)} %bitcast.49), custom_call_target="tpu_custom_call" | custom-call | tf_op jit(solution)/shard_map/pallas_call | solution.py:248
  61.5 15.9 %all_to_all.30 = f32[8,32,128]{2,1,0:T(8,128)S(1)} all-to-all(f32[8,32,128]{2,1,0:T(8,128)S(1)} %copy-done.6), channel_id=1, replica_groups=mesh['y'=4,'z'=8,'x'=4,'core'=2] {'z'}, dimensions={0} | all-to-all | bytes 262144 | tf_op jit(solution)/shard_map/all_to_all | solution.py:495
  77.4 14.8 %all_gather.9.p_ref = f32[256,128]{1,0:T(8,128)S(1)} all-gather(f32[32,128]{1,0:T(8,128)S(1)} %reduce_sum.28), channel_id=1, replica_groups=mesh['y'=4,'z'=8,'x'=4,'core'=2] {'x','core'}, dimensions={0}, use_global_device_ids=true | all-gather | bytes 147456 | tf_op jit(solution)/shard_map/all_gather | solution.py:540
  92.2 15.0 %reduce-scatter.2.cloned.1.call-done = bf16[1,256,768]{2,1,0:T(8,128)(2,1)} async-done(((bf16[8,256,768]{2,1,0:T(8,128)(2,1)}), bf16[1,256,768]{2,1,0:T(8,128)(2,1)}) %reduce-scatter.2.cloned.1.call-update) | async-done | bytes 393232 | tf_op jit(solution)/shard_map/reduce_scatter | solution.py:537
  108.2 1.7 shard_map.96
  109.9 11.0 %all_to_all.31.n_ref = bf16[8,16,128]{2,1,0:T(8,128)(2,1)S(1)} all-to-all(bf16[8,16,128]{2,1,0:T(8,128)(2,1)S(1)} %tile.2), channel_id=1, replica_groups=mesh['y'=4,'z'=8,'x'=4,'core'=2] {'z'}, dimensions={0} | all-to-all | bytes 65536 | tf_op jit(solution)/shard_map/all_to_all | solution.py:495
  120.9 35.4 %all-gather.3.cloned.1.call-done = bf16[2048,768]{1,0:T(8,128)(2,1)} async-done(((bf16[256,768]{1,0:T(8,128)(2,1)}), bf16[2048,768]{1,0:T(8,128)(2,1)}) %all-gather.3.cloned.1.call-update) | async-done | bytes 3145744 | tf_op jit(solution)/shard_map/all_gather | solution.py:542
  156.4 9.8 %shard_map.97 = (bf16[4,2,192,768]{3,2,1,0:T(8,128)(2,1)}, bf16[4,4,208,128]{3,2,1,0:T(8,128)(2,1)}, bf16[4,4,208,128]{3,2,1,0:T(8,128)(2,1)}) custom-call(s32[4]{0:T(128)S(1)} %pad_add_fusion.here_ref, bf16[4,2,192,768]{3,2,1,0:T(8,128)(2,1)} %bitcast.50, bf16[2,768,1024]{2,1,0:T(8,128)(2,1)} %get-tuple-element.23.x_ref, bf16[8,256,768]{2,1,0:T(8,128)(2,1)} %bitcast.57, ...), custom_call_target="tpu_custom_call" | custom-call | tf_op jit(solution)/shard_map/pallas_call | solution.py:403
  167.1 4.1 %all-to-all-start.3 = ((bf16[4,384,768]{2,1,0:T(8,128)(2,1)}), bf16[4,384,768]{2,1,0:T(8,128)(2,1)S(1)}, u32[]{:S(2)}, u32[]{:S(2)}) async-start(bf16[4,384,768]{2,1,0:T(8,128)(2,1)} %bitcast.58), calls=%async_computation.4 | async-start | bytes 4718592 | tf_op jit(solution)/shard_map/all_to_all | solution.py:495
  176.9 3.6 %collective-permute-done.11 = bf16[4,208,128]{2,1,0:T(8,128)(2,1)S(1)} collective-permute-done((bf16[4,208,128]{2,1,0:T(8,128)(2,1)S(1)}, bf16[4,208,128]{2,1,0:T(8,128)(2,1)S(1)}, u32[]{:S(2)}, u32[]{:S(2)}) %collective-permute-start.11) | collective-permute-done | bytes 213024 | tf_op jit(solution)/shard_map/ppermute | solution.py:503
  180.5 5.5 %collective-permute-done.13 = bf16[4,208,128]{2,1,0:T(8,128)(2,1)S(1)} collective-permute-done((bf16[4,208,128]{2,1,0:T(8,128)(2,1)S(1)}, bf16[4,208,128]{2,1,0:T(8,128)(2,1)S(1)}, u32[]{:S(2)}, u32[]{:S(2)}) %collective-permute-start.13) | collective-permute-done | bytes 213024 | tf_op jit(solution)/shard_map/ppermute | solution.py:503
  191.0 9.3 %all-to-all-done.3 = bf16[4,384,768]{2,1,0:T(8,128)(2,1)S(1)} async-done(((bf16[4,384,768]{2,1,0:T(8,128)(2,1)}), bf16[4,384,768]{2,1,0:T(8,128)(2,1)S(1)}, u32[]{:S(2)}, u32[]{:S(2)}) %all-to-all-start.3) | async-done | bytes 2359328 | tf_op jit(solution)/shard_map/all_to_all | solution.py:495
  200.3 4.0 %shard_map.98 = (f32[192,3072]{1,0:T(8,128)}, f32[192,3072]{1,0:T(8,128)}, f32[8,128]{1,0:T(8,128)S(1)}) custom-call(f32[1]{0:T(128)S(6)} %copy.10.rate_ref, f32[192,3072]{1,0:T(8,128)} %a_ref.3, f32[192,3072]{1,0:T(8,128)} %bitcast.55, bf16[4,2,192,768]{3,2,1,0:T(8,128)(2,1)S(1)} %bitcast.51), custom_call_target="tpu_custom_call" | custom-call | tf_op jit(solution)/shard_map/pallas_call | solution.py:472
  (64 shorter events, 23.7 us)
Async XLA Ops:
  8.0 9.4 %collective-permute-start = (bf16[2,192,128]{2,1,0:T(8,128)(2,1)S(1)}, bf16[2,192,128]{2,1,0:T(8,128)(2,1)S(1)}, u32[]{:S(2)}, u32[]{:S(2)}) collective-permute-start(bf16[2,192,128]{2,1,0:T(8,128)(2,1)S(1)} %get-tuple-element.41), channel_id=1, source_target_pairs={{0,64},{64,128},{128,192},{192,0},{1,65},{65,129},{129,193},{193,1... | collective-permute-start | bytes 294920 | tf_op jit(solution)/shard_map/ppermute | solution.py:503
  10.2 7.2 %collective-permute-start.1 = (bf16[2,192,128]{2,1,0:T(8,128)(2,1)S(1)}, bf16[2,192,128]{2,1,0:T(8,128)(2,1)S(1)}, u32[]{:S(2)}, u32[]{:S(2)}) collective-permute-start(bf16[2,192,128]{2,1,0:T(8,128)(2,1)S(1)} %get-tuple-element.41), channel_id=1, source_target_pairs={{0,128},{64,192},{128,0},{192,64},{1,129},{65,193},{129,1},{193,65... | collective-permute-start | bytes 294920 | tf_op jit(solution)/shard_map/ppermute | solution.py:503
  12.8 4.6 %collective-permute-start.2 = (bf16[2,192,128]{2,1,0:T(8,128)(2,1)S(1)}, bf16[2,192,128]{2,1,0:T(8,128)(2,1)S(1)}, u32[]{:S(2)}, u32[]{:S(2)}) collective-permute-start(bf16[2,192,128]{2,1,0:T(8,128)(2,1)S(1)} %get-tuple-element.41), channel_id=1, source_target_pairs={{0,192},{64,0},{128,64},{192,128},{1,193},{65,1},{129,65},{193,129... | collective-permute-start | bytes 294920 | tf_op jit(solution)/shard_map/ppermute | solution.py:503
  17.5 9.3 %copy-start.2 = (bf16[4,2,192,128]{3,2,1,0:T(8,128)(2,1)}, bf16[4,2,192,128]{3,2,1,0:T(8,128)(2,1)S(1)}, u32[]{:S(2)}) copy-start(bf16[4,2,192,128]{3,2,1,0:T(8,128)(2,1)S(1)} %pad_maximum_fusion.refs_0_) | copy-start | bytes 1179652
  17.5 8.7 %copy-start.7 = (s32[1024]{0:T(1024)S(1)}, s32[1024]{0:T(1024)}, u32[]{:S(2)}) copy-start(s32[1024]{0:T(1024)} %param.8) | copy-start | bytes 12292
  17.5 37.0 %all-to-all-start = ((bf16[4,384,768]{2,1,0:T(8,128)(2,1)}), bf16[4,384,768]{2,1,0:T(8,128)(2,1)S(1)}, u32[]{:S(2)}, u32[]{:S(2)}) async-start(bf16[4,384,768]{2,1,0:T(8,128)(2,1)} %bitcast.56), calls=%async_computation | async-start | bytes 4718592 | tf_op jit(solution)/shard_map/all_to_all | solution.py:495
  21.3 85.9 %reduce-scatter.2.cloned.1.call-start = ((), (), s32[]{:S(2)}) async-start(), calls=%async_computation.5 | async-start | bytes 3538944 | tf_op jit(solution)/shard_map/reduce_scatter | solution.py:537
  21.4 10.1 %collective-permute-start.3 = (bf16[4,2,192,128]{3,2,1,0:T(8,128)(2,1)S(1)}, bf16[4,2,192,128]{3,2,1,0:T(8,128)(2,1)S(1)}, u32[]{:S(2)}, u32[]{:S(2)}) collective-permute-start(bf16[4,2,192,128]{3,2,1,0:T(8,128)(2,1)S(1)} %pad_maximum_fusion.refs_0_), channel_id=1, source_target_pairs={{0,2},{2,4},{4,6},{6,0},{1,3},{3,5},{5,7},{7,1},{8,10},{10,12},{12... | collective-permute-start | bytes 1179656 | tf_op jit(solution)/shard_map/ppermute | solution.py:503
  22.7 18.5 %collective-permute-start.4 = (bf16[4,2,192,128]{3,2,1,0:T(8,128)(2,1)S(1)}, bf16[4,2,192,128]{3,2,1,0:T(8,128)(2,1)S(1)}, u32[]{:S(2)}, u32[]{:S(2)}) collective-permute-start(bf16[4,2,192,128]{3,2,1,0:T(8,128)(2,1)S(1)} %pad_maximum_fusion.refs_0_), channel_id=1, source_target_pairs={{0,4},{2,6},{4,0},{6,2},{1,5},{3,7},{5,1},{7,3},{8,12},{10,14},{12... | collective-permute-start | bytes 1179656 | tf_op jit(solution)/shard_map/ppermute | solution.py:503
  25.1 18.5 %collective-permute-start.5 = (bf16[4,2,192,128]{3,2,1,0:T(8,128)(2,1)S(1)}, bf16[4,2,192,128]{3,2,1,0:T(8,128)(2,1)}, u32[]{:S(2)}, u32[]{:S(2)}) collective-permute-start(bf16[4,2,192,128]{3,2,1,0:T(8,128)(2,1)S(1)} %pad_maximum_fusion.refs_0_), channel_id=1, source_target_pairs={{0,6},{2,0},{4,2},{6,4},{1,7},{3,1},{5,3},{7,5},{8,14},{10,8},{12,... | collective-permute-start | bytes 1179656 | tf_op jit(solution)/shard_map/ppermute | solution.py:503
  26.8 17.0 %collective-permute-start.6 = (bf16[4,2,192,128]{3,2,1,0:T(8,128)(2,1)S(1)}, bf16[4,2,192,128]{3,2,1,0:T(8,128)(2,1)}, u32[]{:S(2)}, u32[]{:S(2)}) collective-permute-start(bf16[4,2,192,128]{3,2,1,0:T(8,128)(2,1)S(1)} %pad_maximum_fusion.refs_0_), channel_id=1, source_target_pairs={{0,1},{1,0},{2,3},{3,2},{4,5},{5,4},{6,7},{7,6},{8,9},{9,8},{10,11... | collective-permute-start | bytes 1179656 | tf_op jit(solution)/shard_map/ppermute | solution.py:499
  31.4 14.4 %copy-start.4 = (bf16[4,2,192,128]{3,2,1,0:T(8,128)(2,1)}, bf16[4,2,192,128]{3,2,1,0:T(8,128)(2,1)S(1)}, u32[]{:S(2)}) copy-start(bf16[4,2,192,128]{3,2,1,0:T(8,128)(2,1)S(1)} %collective-permute-done.3.refs_1_) | copy-start | bytes 1179652
  32.4 11.3 %collective-permute-start.7 = (bf16[4,2,192,128]{3,2,1,0:T(8,128)(2,1)S(1)}, bf16[4,2,192,128]{3,2,1,0:T(8,128)(2,1)}, u32[]{:S(2)}, u32[]{:S(2)}) collective-permute-start(bf16[4,2,192,128]{3,2,1,0:T(8,128)(2,1)S(1)} %collective-permute-done.3.refs_1_), channel_id=1, source_target_pairs={{0,1},{1,0},{2,3},{3,2},{4,5},{5,4},{6,7},{7,6},{8,9},{9,8},{10,11... | collective-permute-start | bytes 1179656 | tf_op jit(solution)/shard_map/ppermute | solution.py:499
  41.2 3.9 %collective-permute-start.8 = (bf16[4,2,192,128]{3,2,1,0:T(8,128)(2,1)S(1)}, bf16[4,2,192,128]{3,2,1,0:T(8,128)(2,1)}, u32[]{:S(2)}, u32[]{:S(2)}) collective-permute-start(bf16[4,2,192,128]{3,2,1,0:T(8,128)(2,1)S(1)} %collective-permute-done.4.refs_2_), channel_id=1, source_target_pairs={{0,1},{1,0},{2,3},{3,2},{4,5},{5,4},{6,7},{7,6},{8,9},{9,8},{10,11... | collective-permute-start | bytes 1179656 | tf_op jit(solution)/shard_map/ppermute | solution.py:499
  43.6 2.3 %collective-permute-start.9 = (bf16[4,2,192,128]{3,2,1,0:T(8,128)(2,1)}, bf16[4,2,192,128]{3,2,1,0:T(8,128)(2,1)}, u32[]{:S(2)}, u32[]{:S(2)}) collective-permute-start(bf16[4,2,192,128]{3,2,1,0:T(8,128)(2,1)} %collective-permute-done.5.refs_3_), channel_id=1, source_target_pairs={{0,1},{1,0},{2,3},{3,2},{4,5},{5,4},{6,7},{7,6},{8,9},{9,8},{10,11... | collective-permute-start | bytes 1179656 | tf_op jit(solution)/shard_map/ppermute | solution.py:499
  60.6 95.7 %all-gather.3.cloned.1.call-start = ((), (), s32[]{:S(2)}) async-start(), calls=%async_computation.6 | async-start | bytes 3538944 | tf_op jit(solution)/shard_map/all_gather | solution.py:542
  166.1 5.1 %collective-permute-start.10 = (bf16[4,4,208,128]{3,2,1,0:T(8,128)(2,1)}, bf16[4,4,208,128]{3,2,1,0:T(8,128)(2,1)}, u32[]{:S(2)}, u32[]{:S(2)}) collective-permute-start(bf16[4,4,208,128]{3,2,1,0:T(8,128)(2,1)} %get-tuple-element.29), channel_id=1, source_target_pairs={{0,1},{1,0},{2,3},{3,2},{4,5},{5,4},{6,7},{7,6},{8,9},{9,8},{10,11... | collective-permute-start | bytes 2555912 | tf_op jit(solution)/shard_map/ppermute | solution.py:499
  167.1 33.1 %all-to-all-start.3 = ((bf16[4,384,768]{2,1,0:T(8,128)(2,1)}), bf16[4,384,768]{2,1,0:T(8,128)(2,1)S(1)}, u32[]{:S(2)}, u32[]{:S(2)}) async-start(bf16[4,384,768]{2,1,0:T(8,128)(2,1)} %bitcast.58), calls=%async_computation.4 | async-start | bytes 4718592 | tf_op jit(solution)/shard_map/all_to_all | solution.py:495
  172.7 7.8 %collective-permute-start.11 = (bf16[4,208,128]{2,1,0:T(8,128)(2,1)S(1)}, bf16[4,208,128]{2,1,0:T(8,128)(2,1)S(1)}, u32[]{:S(2)}, u32[]{:S(2)}) collective-permute-start(bf16[4,208,128]{2,1,0:T(8,128)(2,1)S(1)} %get-tuple-element.34), channel_id=1, source_target_pairs={{0,2},{2,4},{4,6},{6,0},{1,3},{3,5},{5,7},{7,1},{8,10},{10,12},{12... | collective-permute-start | bytes 638984 | tf_op jit(solution)/shard_map/ppermute | solution.py:503
  174.0 6.6 %collective-permute-start.12 = (bf16[4,208,128]{2,1,0:T(8,128)(2,1)S(1)}, bf16[4,208,128]{2,1,0:T(8,128)(2,1)S(1)}, u32[]{:S(2)}, u32[]{:S(2)}) collective-permute-start(bf16[4,208,128]{2,1,0:T(8,128)(2,1)S(1)} %get-tuple-element.36), channel_id=1, source_target_pairs={{0,6},{2,0},{4,2},{6,4},{1,7},{3,1},{5,3},{7,5},{8,14},{10,8},{12,... | collective-permute-start | bytes 638984 | tf_op jit(solution)/shard_map/ppermute | solution.py:503
  175.5 10.5 %collective-permute-start.13 = (bf16[4,208,128]{2,1,0:T(8,128)(2,1)S(1)}, bf16[4,208,128]{2,1,0:T(8,128)(2,1)S(1)}, u32[]{:S(2)}, u32[]{:S(2)}) collective-permute-start(bf16[4,208,128]{2,1,0:T(8,128)(2,1)S(1)} %get-tuple-element.35), channel_id=1, source_target_pairs={{0,4},{2,6},{4,0},{6,2},{1,5},{3,7},{5,1},{7,3},{8,12},{10,14},{12... | collective-permute-start | bytes 638984 | tf_op jit(solution)/shard_map/ppermute | solution.py:503
  186.2 18.6 %collective-permute-start.14 = (bf16[208,128]{1,0:T(8,128)(2,1)S(1)}, bf16[208,128]{1,0:T(8,128)(2,1)S(1)}, u32[]{:S(2)}, u32[]{:S(2)}) collective-permute-start(bf16[208,128]{1,0:T(8,128)(2,1)S(1)} %get-tuple-element.37), channel_id=1, source_target_pairs={{0,64},{64,128},{128,192},{192,0},{1,65},{65,129},{129,193},{193,1... | collective-permute-start | bytes 159752 | tf_op jit(solution)/shard_map/ppermute | solution.py:503
  187.4 17.4 %collective-permute-start.15 = (bf16[208,128]{1,0:T(8,128)(2,1)S(1)}, bf16[208,128]{1,0:T(8,128)(2,1)S(1)}, u32[]{:S(2)}, u32[]{:S(2)}) collective-permute-start(bf16[208,128]{1,0:T(8,128)(2,1)S(1)} %get-tuple-element.39), channel_id=1, source_target_pairs={{0,192},{64,0},{128,64},{192,128},{1,193},{65,1},{129,65},{193,129... | collective-permute-start | bytes 159752 | tf_op jit(solution)/shard_map/ppermute | solution.py:503
  188.9 15.9 %collective-permute-start.16 = (bf16[208,128]{1,0:T(8,128)(2,1)S(1)}, bf16[208,128]{1,0:T(8,128)(2,1)S(1)}, u32[]{:S(2)}, u32[]{:S(2)}) collective-permute-start(bf16[208,128]{1,0:T(8,128)(2,1)S(1)} %get-tuple-element.38), channel_id=1, source_target_pairs={{0,128},{64,192},{128,0},{192,64},{1,129},{65,193},{129,1},{193,65... | collective-permute-start | bytes 159752 | tf_op jit(solution)/shard_map/ppermute | solution.py:503
  (5 other events, 16.8 us)
Sparse Core Ops, SparseCore 0:
  60.7 46.4 reduce-scatter.1
  110.0 46.2 all-gather.2

commit v6 on v5

--- a/solution.py
+++ b/solution.py
@@ -263,13 +263,26 @@
 
 
 def activate(here, summed, pairs):
-    def body(here_ref, s_ref, p_ref, o_ref, n_ref):
-        pre = s_ref[0:TOK_IMG, :].astype(f32)
-        act, slope = gelu_and_slope(pre)
+    def body(here_ref, s_ref, p_ref, o_ref, n_ref, s_buf, o_buf, s_sem, o_sem):
+        def load(a):
+            part = pl.ds(a * TOK_IMG, TOK_IMG)
+            return pltpu.make_async_copy(s_ref.at[part], s_buf.at[a], s_sem.at[a])
+
+        def store(a):
+            part = pl.ds(a * TOK_IMG, TOK_IMG)
+            return pltpu.make_async_copy(o_buf.at[a], o_ref.at[part], o_sem.at[a])
+
+        load(0).start()
+        load(1).start()
+        load(0).wait()
+        act, slope = gelu_and_slope(s_buf[0].astype(f32))
         act = act.astype(bf16)
-        hid = (s_ref[TOK_IMG:, :].astype(f32) * slope).astype(bf16)
-        o_ref[0:TOK_IMG, :] = act
-        o_ref[TOK_IMG:, :] = hid
+        o_buf[0] = act
+        store(0).start()
+        load(1).wait()
+        hid = (s_buf[1].astype(f32) * slope).astype(bf16)
+        o_buf[1] = hid
+        store(1).start()
         both = dot(hid, hid, ((1,), (1,))) * p_ref[0:TOK_IMG] * (SCALE_IN * SCALE_IN)
         both += dot(act, act, ((1,), (1,))) * p_ref[TOK_IMG:] * (SCALE_OUT * SCALE_OUT)
         square = jnp.sum(jnp.sum(both, axis=0, keepdims=True), axis=1, keepdims=True)
@@ -284,17 +297,25 @@
         value = jnp.where(kind == 0, high, jnp.where(kind == 1, middle, low))
         kept = (lane == spot) & (kind >= 0) & (kind < 3)
         n_ref[...] = jnp.where(kept, value, 0.0).astype(bf16)
+        store(0).wait()
+        store(1).wait()
 
     return pl.pallas_call(
         body,
-        in_specs=[SMEM, VMEM, VMEM],
-        out_specs=[VMEM, VMEM],
+        in_specs=[SMEM, HBM, VMEM],
+        out_specs=[HBM, VMEM],
         out_shape=[
-            jax.ShapeDtypeStruct((2 * TOK_IMG, HID), bf16),
+            pltpu.HBM((2 * TOK_IMG, HID), bf16),
             jax.ShapeDtypeStruct((NORM_ROWS, 128), bf16),
         ],
+        scratch_shapes=[
+            pltpu.VMEM((2, TOK_IMG, HID), bf16),
+            pltpu.VMEM((2, TOK_IMG, HID), bf16),
+            pltpu.SemaphoreType.DMA((2,)),
+            pltpu.SemaphoreType.DMA((2,)),
+        ],
         compiler_params=SMALL,
-    )(here, summed, pairs)
+    )(here, in_hbm(summed), pairs)
 
 
 def all_grads(here, weights, feats, every, norms, place):

time: 215 us -> 214 us (level)
  no operation moved by 1% of the time
where the time goes in v6:
time: 214 us
  waiting for transfers between devices  78 us (36%)
  blocking collectives  41.7 us (19%)
  starting transfers between devices  37 us (17%)
  Pallas kernels  34.5 us (16%)
  between operations  14.9 us (7%)
  other arithmetic  4.26 us (2%)
  local copies, waits for them, and re-layouts  3.14 us (1%)
    all_gather x1, waiting for transfers between devices, shards(): every = lax.all_gather(sent, 'z')  35.4 us
    all_to_all x2, blocking collectives, exchange(): return lax.all_to_all(value, axes, 0, 0, tiled=True)  26.8 us
    ppermute x12, starting transfers between devices, ahead(): return lax.ppermute(value, axis, [(i, (i + step) % 4) for i in range(4)])  19.2 us
    ppermute x12, waiting for transfers between devices, ahead(): return lax.ppermute(value, axis, [(i, (i + step) % 4) for i in range(4)])  16.2 us
    reduce_scatter x1, waiting for transfers between devices, shards(): summed = lax.psum_scatter(parts, 'z', scatter_dimension=0)  15 us
    all_gather x1, blocking collectives, shards(): pairs = lax.all_gather(pairs, ('x', 'core'), axis=0, tiled=True)  14.8 us
    pallas_call x1, Pallas kernels, all_grads(): pl.pallas_call(body, in_specs=[SMEM] + [HBM] * 3 + [ANY, HBM], out_specs=...  9.77 us
    ppermute x5, starting transfers between devices, swap_cores(): return lax.ppermute(value, 'core', [(0, 1), (1, 0)])  9.76 us
  transfers between devices with their start and end apart: 21, of which 9 were waited for; matrix products, arithmetic and copies ran while one was open for 2% of the time, Pallas kernels for 8%

profile of v6, /device:TPU:1, one launch (start us, length us, event | category | flops | bytes accessed | tf_op | source)
XLA Modules:
  0.0 213.5 jit_solution(7287580051845552951)
XLA Ops:
  8.0 2.2 %collective-permute-start = (bf16[2,192,128]{2,1,0:T(8,128)(2,1)S(1)}, bf16[2,192,128]{2,1,0:T(8,128)(2,1)S(1)}, u32[]{:S(2)}, u32[]{:S(2)}) collective-permute-start(bf16[2,192,128]{2,1,0:T(8,128)(2,1)S(1)} %get-tuple-element.41), channel_id=1, source_target_pairs={{0,64},{64,128},{128,192},{192,0},{1,65},{65,129},{129,193},{193,1... | collective-permute-start | bytes 294920 | tf_op jit(solution)/shard_map/ppermute | solution.py:524
  10.2 2.6 %collective-permute-start.1 = (bf16[2,192,128]{2,1,0:T(8,128)(2,1)S(1)}, bf16[2,192,128]{2,1,0:T(8,128)(2,1)S(1)}, u32[]{:S(2)}, u32[]{:S(2)}) collective-permute-start(bf16[2,192,128]{2,1,0:T(8,128)(2,1)S(1)} %get-tuple-element.41), channel_id=1, source_target_pairs={{0,128},{64,192},{128,0},{192,64},{1,129},{65,193},{129,1},{193,65... | collective-permute-start | bytes 294920 | tf_op jit(solution)/shard_map/ppermute | solution.py:524
  13.9 3.5 %shard_map.93 = bf16[4,2,192,768]{3,2,1,0:T(8,128)(2,1)} custom-call(f32[192,3072]{1,0:T(8,128)} %a_ref.3, f32[192,3072]{1,0:T(8,128)} %bitcast.53), custom_call_target="tpu_custom_call" | custom-call | tf_op jit(solution)/shard_map/pallas_call | solution.py:82
  17.5 3.8 %all-to-all-start = ((bf16[4,384,768]{2,1,0:T(8,128)(2,1)}), bf16[4,384,768]{2,1,0:T(8,128)(2,1)S(1)}, u32[]{:S(2)}, u32[]{:S(2)}) async-start(bf16[4,384,768]{2,1,0:T(8,128)(2,1)} %bitcast.55), calls=%async_computation | async-start | bytes 4718592 | tf_op jit(solution)/shard_map/all_to_all | solution.py:516
  22.7 2.5 %collective-permute-start.4 = (bf16[4,2,192,128]{3,2,1,0:T(8,128)(2,1)S(1)}, bf16[4,2,192,128]{3,2,1,0:T(8,128)(2,1)S(1)}, u32[]{:S(2)}, u32[]{:S(2)}) collective-permute-start(bf16[4,2,192,128]{3,2,1,0:T(8,128)(2,1)S(1)} %pad_maximum_fusion.refs_0_), channel_id=1, source_target_pairs={{0,4},{2,6},{4,0},{6,2},{1,5},{3,7},{5,1},{7,3},{8,12},{10,14},{12... | collective-permute-start | bytes 1179656 | tf_op jit(solution)/shard_map/ppermute | solution.py:524
  26.8 2.4 %collective-permute-start.6 = (bf16[4,2,192,128]{3,2,1,0:T(8,128)(2,1)S(1)}, bf16[4,2,192,128]{3,2,1,0:T(8,128)(2,1)}, u32[]{:S(2)}, u32[]{:S(2)}) collective-permute-start(bf16[4,2,192,128]{3,2,1,0:T(8,128)(2,1)S(1)} %pad_maximum_fusion.refs_0_), channel_id=1, source_target_pairs={{0,1},{1,0},{2,3},{3,2},{4,5},{5,4},{6,7},{7,6},{8,9},{9,8},{10,11... | collective-permute-start | bytes 1179656 | tf_op jit(solution)/shard_map/ppermute | solution.py:520
  29.2 2.2 %collective-permute-done.3.refs_1_ = bf16[4,2,192,128]{3,2,1,0:T(8,128)(2,1)S(1)} collective-permute-done((bf16[4,2,192,128]{3,2,1,0:T(8,128)(2,1)S(1)}, bf16[4,2,192,128]{3,2,1,0:T(8,128)(2,1)S(1)}, u32[]{:S(2)}, u32[]{:S(2)}) %collective-permute-start.3) | collective-permute-done | bytes 393248 | tf_op jit(solution)/shard_map/ppermute | solution.py:524
  32.4 3.8 %collective-permute-start.7 = (bf16[4,2,192,128]{3,2,1,0:T(8,128)(2,1)S(1)}, bf16[4,2,192,128]{3,2,1,0:T(8,128)(2,1)}, u32[]{:S(2)}, u32[]{:S(2)}) collective-permute-start(bf16[4,2,192,128]{3,2,1,0:T(8,128)(2,1)S(1)} %collective-permute-done.3.refs_1_), channel_id=1, source_target_pairs={{0,1},{1,0},{2,3},{3,2},{4,5},{5,4},{6,7},{7,6},{8,9},{9,8},{10,11... | collective-permute-start | bytes 1179656 | tf_op jit(solution)/shard_map/ppermute | solution.py:520
  36.2 4.9 %collective-permute-done.4.refs_2_ = bf16[4,2,192,128]{3,2,1,0:T(8,128)(2,1)S(1)} collective-permute-done((bf16[4,2,192,128]{3,2,1,0:T(8,128)(2,1)S(1)}, bf16[4,2,192,128]{3,2,1,0:T(8,128)(2,1)S(1)}, u32[]{:S(2)}, u32[]{:S(2)}) %collective-permute-start.4) | collective-permute-done | bytes 393248 | tf_op jit(solution)/shard_map/ppermute | solution.py:524
  41.2 2.4 %collective-permute-start.8 = (bf16[4,2,192,128]{3,2,1,0:T(8,128)(2,1)S(1)}, bf16[4,2,192,128]{3,2,1,0:T(8,128)(2,1)}, u32[]{:S(2)}, u32[]{:S(2)}) collective-permute-start(bf16[4,2,192,128]{3,2,1,0:T(8,128)(2,1)S(1)} %collective-permute-done.4.refs_2_), channel_id=1, source_target_pairs={{0,1},{1,0},{2,3},{3,2},{4,5},{5,4},{6,7},{7,6},{8,9},{9,8},{10,11... | collective-permute-start | bytes 1179656 | tf_op jit(solution)/shard_map/ppermute | solution.py:520
  45.9 8.6 %shard_map.94 = (bf16[2,768,1024]{2,1,0:T(8,128)(2,1)}, bf16[2,1024,768]{2,1,0:T(8,128)(2,1)}, f32[8,32,128]{2,1,0:T(8,128)}) custom-call(s32[4]{0:T(128)S(1)} %pad_add_fusion.here_ref, bf16[4,2,192,128]{3,2,1,0:T(8,128)(2,1)} %copy-done.1, bf16[4,2,192,128]{3,2,1,0:T(8,128)(2,1)} %copy-done.3, bf16[4,2,192,128]{3,2,1,0:T(8,128)(2,1)} %copy-done.4, ...), custom_call_target="tpu_custom_call" | custom-call | tf_op jit(solution)/shard_map/pallas_call | solution.py:178
  54.5 6.0 %shard_map.95 = bf16[8,2,128,768]{3,2,1,0:T(8,128)(2,1)} custom-call(s32[4]{0:T(128)S(1)} %pad_add_fusion.here_ref, bf16[2,1024,768]{2,1,0:T(8,128)(2,1)} %get-tuple-element.24.r_ref, bf16[4,2,192,768]{3,2,1,0:T(8,128)(2,1)S(1)} %bitcast.49), custom_call_target="tpu_custom_call" | custom-call | tf_op jit(solution)/shard_map/pallas_call | solution.py:248
  61.4 15.9 %all_to_all.30 = f32[8,32,128]{2,1,0:T(8,128)S(1)} all-to-all(f32[8,32,128]{2,1,0:T(8,128)S(1)} %copy-done.5), channel_id=1, replica_groups=mesh['y'=4,'z'=8,'x'=4,'core'=2] {'z'}, dimensions={0} | all-to-all | bytes 262144 | tf_op jit(solution)/shard_map/all_to_all | solution.py:516
  77.3 14.8 %all_gather.9.p_ref = f32[256,128]{1,0:T(8,128)S(1)} all-gather(f32[32,128]{1,0:T(8,128)S(1)} %reduce_sum.28), channel_id=1, replica_groups=mesh['y'=4,'z'=8,'x'=4,'core'=2] {'x','core'}, dimensions={0}, use_global_device_ids=true | all-gather | bytes 147456 | tf_op jit(solution)/shard_map/all_gather | solution.py:561
  92.1 15.0 %reduce-scatter.2.cloned.1.call-done = bf16[1,256,768]{2,1,0:T(8,128)(2,1)} async-done(((bf16[8,256,768]{2,1,0:T(8,128)(2,1)}), bf16[1,256,768]{2,1,0:T(8,128)(2,1)}) %reduce-scatter.2.cloned.1.call-update) | async-done | bytes 393232 | tf_op jit(solution)/shard_map/reduce_scatter | solution.py:558
  107.2 2.6 %shard_map.96 = (bf16[256,768]{1,0:T(8,128)(2,1)}, bf16[16,128]{1,0:T(8,128)(2,1)S(1)}) custom-call(s32[4]{0:T(128)S(1)} %pad_add_fusion.here_ref, bf16[256,768]{1,0:T(8,128)(2,1)} %bitcast.58, f32[256,128]{1,0:T(8,128)S(1)} %all_gather.9.p_ref), custom_call_target="tpu_custom_call" | custom-call | tf_op jit(solution)/shard_map/pallas_call | solution.py:303
  109.8 11.0 %all_to_all.31.n_ref = bf16[8,16,128]{2,1,0:T(8,128)(2,1)S(1)} all-to-all(bf16[8,16,128]{2,1,0:T(8,128)(2,1)S(1)} %tile.2), channel_id=1, replica_groups=mesh['y'=4,'z'=8,'x'=4,'core'=2] {'z'}, dimensions={0} | all-to-all | bytes 65536 | tf_op jit(solution)/shard_map/all_to_all | solution.py:516
  120.8 35.4 %all-gather.3.cloned.1.call-done = bf16[2048,768]{1,0:T(8,128)(2,1)} async-done(((bf16[256,768]{1,0:T(8,128)(2,1)}), bf16[2048,768]{1,0:T(8,128)(2,1)}) %all-gather.3.cloned.1.call-update) | async-done | bytes 3145744 | tf_op jit(solution)/shard_map/all_gather | solution.py:563
  156.3 9.8 %shard_map.97 = (bf16[4,2,192,768]{3,2,1,0:T(8,128)(2,1)}, bf16[4,4,208,128]{3,2,1,0:T(8,128)(2,1)}, bf16[4,4,208,128]{3,2,1,0:T(8,128)(2,1)}) custom-call(s32[4]{0:T(128)S(1)} %pad_add_fusion.here_ref, bf16[4,2,192,768]{3,2,1,0:T(8,128)(2,1)} %bitcast.50, bf16[2,768,1024]{2,1,0:T(8,128)(2,1)} %get-tuple-element.23.x_ref, bf16[8,256,768]{2,1,0:T(8,128)(2,1)} %bitcast.56, ...), custom_call_target="tpu_custom_call" | custom-call | tf_op jit(solution)/shard_map/pallas_call | solution.py:424
  167.0 4.1 %all-to-all-start.3 = ((bf16[4,384,768]{2,1,0:T(8,128)(2,1)}), bf16[4,384,768]{2,1,0:T(8,128)(2,1)S(1)}, u32[]{:S(2)}, u32[]{:S(2)}) async-start(bf16[4,384,768]{2,1,0:T(8,128)(2,1)} %bitcast.57), calls=%async_computation.4 | async-start | bytes 4718592 | tf_op jit(solution)/shard_map/all_to_all | solution.py:516
  176.8 3.6 %collective-permute-done.11 = bf16[4,208,128]{2,1,0:T(8,128)(2,1)S(1)} collective-permute-done((bf16[4,208,128]{2,1,0:T(8,128)(2,1)S(1)}, bf16[4,208,128]{2,1,0:T(8,128)(2,1)S(1)}, u32[]{:S(2)}, u32[]{:S(2)}) %collective-permute-start.11) | collective-permute-done | bytes 213024 | tf_op jit(solution)/shard_map/ppermute | solution.py:524
  180.4 5.5 %collective-permute-done.13 = bf16[4,208,128]{2,1,0:T(8,128)(2,1)S(1)} collective-permute-done((bf16[4,208,128]{2,1,0:T(8,128)(2,1)S(1)}, bf16[4,208,128]{2,1,0:T(8,128)(2,1)S(1)}, u32[]{:S(2)}, u32[]{:S(2)}) %collective-permute-start.13) | collective-permute-done | bytes 213024 | tf_op jit(solution)/shard_map/ppermute | solution.py:524
  190.9 9.3 %all-to-all-done.3 = bf16[4,384,768]{2,1,0:T(8,128)(2,1)S(1)} async-done(((bf16[4,384,768]{2,1,0:T(8,128)(2,1)}), bf16[4,384,768]{2,1,0:T(8,128)(2,1)S(1)}, u32[]{:S(2)}, u32[]{:S(2)}) %all-to-all-start.3) | async-done | bytes 2359328 | tf_op jit(solution)/shard_map/all_to_all | solution.py:516
  200.2 4.0 %shard_map.98 = (f32[192,3072]{1,0:T(8,128)}, f32[192,3072]{1,0:T(8,128)}, f32[8,128]{1,0:T(8,128)S(1)}) custom-call(f32[1]{0:T(128)S(6)} %copy.10.rate_ref, f32[192,3072]{1,0:T(8,128)} %a_ref.3, f32[192,3072]{1,0:T(8,128)} %bitcast.54, bf16[4,2,192,768]{3,2,1,0:T(8,128)(2,1)S(1)} %bitcast.51), custom_call_target="tpu_custom_call" | custom-call | tf_op jit(solution)/shard_map/pallas_call | solution.py:493
  (62 shorter events, 22.7 us)
Async XLA Ops:
  8.0 9.4 %collective-permute-start = (bf16[2,192,128]{2,1,0:T(8,128)(2,1)S(1)}, bf16[2,192,128]{2,1,0:T(8,128)(2,1)S(1)}, u32[]{:S(2)}, u32[]{:S(2)}) collective-permute-start(bf16[2,192,128]{2,1,0:T(8,128)(2,1)S(1)} %get-tuple-element.41), channel_id=1, source_target_pairs={{0,64},{64,128},{128,192},{192,0},{1,65},{65,129},{129,193},{193,1... | collective-permute-start | bytes 294920 | tf_op jit(solution)/shard_map/ppermute | solution.py:524
  10.2 7.2 %collective-permute-start.1 = (bf16[2,192,128]{2,1,0:T(8,128)(2,1)S(1)}, bf16[2,192,128]{2,1,0:T(8,128)(2,1)S(1)}, u32[]{:S(2)}, u32[]{:S(2)}) collective-permute-start(bf16[2,192,128]{2,1,0:T(8,128)(2,1)S(1)} %get-tuple-element.41), channel_id=1, source_target_pairs={{0,128},{64,192},{128,0},{192,64},{1,129},{65,193},{129,1},{193,65... | collective-permute-start | bytes 294920 | tf_op jit(solution)/shard_map/ppermute | solution.py:524
  12.8 4.6 %collective-permute-start.2 = (bf16[2,192,128]{2,1,0:T(8,128)(2,1)S(1)}, bf16[2,192,128]{2,1,0:T(8,128)(2,1)S(1)}, u32[]{:S(2)}, u32[]{:S(2)}) collective-permute-start(bf16[2,192,128]{2,1,0:T(8,128)(2,1)S(1)} %get-tuple-element.41), channel_id=1, source_target_pairs={{0,192},{64,0},{128,64},{192,128},{1,193},{65,1},{129,65},{193,129... | collective-permute-start | bytes 294920 | tf_op jit(solution)/shard_map/ppermute | solution.py:524
  17.5 9.3 %copy-start.1 = (bf16[4,2,192,128]{3,2,1,0:T(8,128)(2,1)}, bf16[4,2,192,128]{3,2,1,0:T(8,128)(2,1)S(1)}, u32[]{:S(2)}) copy-start(bf16[4,2,192,128]{3,2,1,0:T(8,128)(2,1)S(1)} %pad_maximum_fusion.refs_0_) | copy-start | bytes 1179652
  17.5 8.7 %copy-start.6 = (s32[1024]{0:T(1024)S(1)}, s32[1024]{0:T(1024)}, u32[]{:S(2)}) copy-start(s32[1024]{0:T(1024)} %param.8) | copy-start | bytes 12292
  17.5 36.9 %all-to-all-start = ((bf16[4,384,768]{2,1,0:T(8,128)(2,1)}), bf16[4,384,768]{2,1,0:T(8,128)(2,1)S(1)}, u32[]{:S(2)}, u32[]{:S(2)}) async-start(bf16[4,384,768]{2,1,0:T(8,128)(2,1)} %bitcast.55), calls=%async_computation | async-start | bytes 4718592 | tf_op jit(solution)/shard_map/all_to_all | solution.py:516
  21.3 85.9 %reduce-scatter.2.cloned.1.call-start = ((), (), s32[]{:S(2)}) async-start(), calls=%async_computation.5 | async-start | bytes 3538944 | tf_op jit(solution)/shard_map/reduce_scatter | solution.py:558
  21.4 10.1 %collective-permute-start.3 = (bf16[4,2,192,128]{3,2,1,0:T(8,128)(2,1)S(1)}, bf16[4,2,192,128]{3,2,1,0:T(8,128)(2,1)S(1)}, u32[]{:S(2)}, u32[]{:S(2)}) collective-permute-start(bf16[4,2,192,128]{3,2,1,0:T(8,128)(2,1)S(1)} %pad_maximum_fusion.refs_0_), channel_id=1, source_target_pairs={{0,2},{2,4},{4,6},{6,0},{1,3},{3,5},{5,7},{7,1},{8,10},{10,12},{12... | collective-permute-start | bytes 1179656 | tf_op jit(solution)/shard_map/ppermute | solution.py:524
  22.7 18.5 %collective-permute-start.4 = (bf16[4,2,192,128]{3,2,1,0:T(8,128)(2,1)S(1)}, bf16[4,2,192,128]{3,2,1,0:T(8,128)(2,1)S(1)}, u32[]{:S(2)}, u32[]{:S(2)}) collective-permute-start(bf16[4,2,192,128]{3,2,1,0:T(8,128)(2,1)S(1)} %pad_maximum_fusion.refs_0_), channel_id=1, source_target_pairs={{0,4},{2,6},{4,0},{6,2},{1,5},{3,7},{5,1},{7,3},{8,12},{10,14},{12... | collective-permute-start | bytes 1179656 | tf_op jit(solution)/shard_map/ppermute | solution.py:524
  25.1 18.5 %collective-permute-start.5 = (bf16[4,2,192,128]{3,2,1,0:T(8,128)(2,1)S(1)}, bf16[4,2,192,128]{3,2,1,0:T(8,128)(2,1)}, u32[]{:S(2)}, u32[]{:S(2)}) collective-permute-start(bf16[4,2,192,128]{3,2,1,0:T(8,128)(2,1)S(1)} %pad_maximum_fusion.refs_0_), channel_id=1, source_target_pairs={{0,6},{2,0},{4,2},{6,4},{1,7},{3,1},{5,3},{7,5},{8,14},{10,8},{12,... | collective-permute-start | bytes 1179656 | tf_op jit(solution)/shard_map/ppermute | solution.py:524
  26.8 17.0 %collective-permute-start.6 = (bf16[4,2,192,128]{3,2,1,0:T(8,128)(2,1)S(1)}, bf16[4,2,192,128]{3,2,1,0:T(8,128)(2,1)}, u32[]{:S(2)}, u32[]{:S(2)}) collective-permute-start(bf16[4,2,192,128]{3,2,1,0:T(8,128)(2,1)S(1)} %pad_maximum_fusion.refs_0_), channel_id=1, source_target_pairs={{0,1},{1,0},{2,3},{3,2},{4,5},{5,4},{6,7},{7,6},{8,9},{9,8},{10,11... | collective-permute-start | bytes 1179656 | tf_op jit(solution)/shard_map/ppermute | solution.py:520
  31.4 14.4 %copy-start.3 = (bf16[4,2,192,128]{3,2,1,0:T(8,128)(2,1)}, bf16[4,2,192,128]{3,2,1,0:T(8,128)(2,1)S(1)}, u32[]{:S(2)}) copy-start(bf16[4,2,192,128]{3,2,1,0:T(8,128)(2,1)S(1)} %collective-permute-done.3.refs_1_) | copy-start | bytes 1179652
  32.4 11.3 %collective-permute-start.7 = (bf16[4,2,192,128]{3,2,1,0:T(8,128)(2,1)S(1)}, bf16[4,2,192,128]{3,2,1,0:T(8,128)(2,1)}, u32[]{:S(2)}, u32[]{:S(2)}) collective-permute-start(bf16[4,2,192,128]{3,2,1,0:T(8,128)(2,1)S(1)} %collective-permute-done.3.refs_1_), channel_id=1, source_target_pairs={{0,1},{1,0},{2,3},{3,2},{4,5},{5,4},{6,7},{7,6},{8,9},{9,8},{10,11... | collective-permute-start | bytes 1179656 | tf_op jit(solution)/shard_map/ppermute | solution.py:520
  41.2 3.9 %collective-permute-start.8 = (bf16[4,2,192,128]{3,2,1,0:T(8,128)(2,1)S(1)}, bf16[4,2,192,128]{3,2,1,0:T(8,128)(2,1)}, u32[]{:S(2)}, u32[]{:S(2)}) collective-permute-start(bf16[4,2,192,128]{3,2,1,0:T(8,128)(2,1)S(1)} %collective-permute-done.4.refs_2_), channel_id=1, source_target_pairs={{0,1},{1,0},{2,3},{3,2},{4,5},{5,4},{6,7},{7,6},{8,9},{9,8},{10,11... | collective-permute-start | bytes 1179656 | tf_op jit(solution)/shard_map/ppermute | solution.py:520
  43.6 2.3 %collective-permute-start.9 = (bf16[4,2,192,128]{3,2,1,0:T(8,128)(2,1)}, bf16[4,2,192,128]{3,2,1,0:T(8,128)(2,1)}, u32[]{:S(2)}, u32[]{:S(2)}) collective-permute-start(bf16[4,2,192,128]{3,2,1,0:T(8,128)(2,1)} %collective-permute-done.5.refs_3_), channel_id=1, source_target_pairs={{0,1},{1,0},{2,3},{3,2},{4,5},{5,4},{6,7},{7,6},{8,9},{9,8},{10,11... | collective-permute-start | bytes 1179656 | tf_op jit(solution)/shard_map/ppermute | solution.py:520
  60.6 95.7 %all-gather.3.cloned.1.call-start = ((), (), s32[]{:S(2)}) async-start(), calls=%async_computation.6 | async-start | bytes 3538944 | tf_op jit(solution)/shard_map/all_gather | solution.py:563
  166.0 5.1 %collective-permute-start.10 = (bf16[4,4,208,128]{3,2,1,0:T(8,128)(2,1)}, bf16[4,4,208,128]{3,2,1,0:T(8,128)(2,1)}, u32[]{:S(2)}, u32[]{:S(2)}) collective-permute-start(bf16[4,4,208,128]{3,2,1,0:T(8,128)(2,1)} %get-tuple-element.29), channel_id=1, source_target_pairs={{0,1},{1,0},{2,3},{3,2},{4,5},{5,4},{6,7},{7,6},{8,9},{9,8},{10,11... | collective-permute-start | bytes 2555912 | tf_op jit(solution)/shard_map/ppermute | solution.py:520
  167.0 33.1 %all-to-all-start.3 = ((bf16[4,384,768]{2,1,0:T(8,128)(2,1)}), bf16[4,384,768]{2,1,0:T(8,128)(2,1)S(1)}, u32[]{:S(2)}, u32[]{:S(2)}) async-start(bf16[4,384,768]{2,1,0:T(8,128)(2,1)} %bitcast.57), calls=%async_computation.4 | async-start | bytes 4718592 | tf_op jit(solution)/shard_map/all_to_all | solution.py:516
  172.6 7.8 %collective-permute-start.11 = (bf16[4,208,128]{2,1,0:T(8,128)(2,1)S(1)}, bf16[4,208,128]{2,1,0:T(8,128)(2,1)S(1)}, u32[]{:S(2)}, u32[]{:S(2)}) collective-permute-start(bf16[4,208,128]{2,1,0:T(8,128)(2,1)S(1)} %get-tuple-element.34), channel_id=1, source_target_pairs={{0,2},{2,4},{4,6},{6,0},{1,3},{3,5},{5,7},{7,1},{8,10},{10,12},{12... | collective-permute-start | bytes 638984 | tf_op jit(solution)/shard_map/ppermute | solution.py:524
  173.9 6.5 %collective-permute-start.12 = (bf16[4,208,128]{2,1,0:T(8,128)(2,1)S(1)}, bf16[4,208,128]{2,1,0:T(8,128)(2,1)S(1)}, u32[]{:S(2)}, u32[]{:S(2)}) collective-permute-start(bf16[4,208,128]{2,1,0:T(8,128)(2,1)S(1)} %get-tuple-element.36), channel_id=1, source_target_pairs={{0,6},{2,0},{4,2},{6,4},{1,7},{3,1},{5,3},{7,5},{8,14},{10,8},{12,... | collective-permute-start | bytes 638984 | tf_op jit(solution)/shard_map/ppermute | solution.py:524
  175.4 10.5 %collective-permute-start.13 = (bf16[4,208,128]{2,1,0:T(8,128)(2,1)S(1)}, bf16[4,208,128]{2,1,0:T(8,128)(2,1)S(1)}, u32[]{:S(2)}, u32[]{:S(2)}) collective-permute-start(bf16[4,208,128]{2,1,0:T(8,128)(2,1)S(1)} %get-tuple-element.35), channel_id=1, source_target_pairs={{0,4},{2,6},{4,0},{6,2},{1,5},{3,7},{5,1},{7,3},{8,12},{10,14},{12... | collective-permute-start | bytes 638984 | tf_op jit(solution)/shard_map/ppermute | solution.py:524
  186.0 18.6 %collective-permute-start.14 = (bf16[208,128]{1,0:T(8,128)(2,1)S(1)}, bf16[208,128]{1,0:T(8,128)(2,1)S(1)}, u32[]{:S(2)}, u32[]{:S(2)}) collective-permute-start(bf16[208,128]{1,0:T(8,128)(2,1)S(1)} %get-tuple-element.37), channel_id=1, source_target_pairs={{0,64},{64,128},{128,192},{192,0},{1,65},{65,129},{129,193},{193,1... | collective-permute-start | bytes 159752 | tf_op jit(solution)/shard_map/ppermute | solution.py:524
  187.3 17.4 %collective-permute-start.15 = (bf16[208,128]{1,0:T(8,128)(2,1)S(1)}, bf16[208,128]{1,0:T(8,128)(2,1)S(1)}, u32[]{:S(2)}, u32[]{:S(2)}) collective-permute-start(bf16[208,128]{1,0:T(8,128)(2,1)S(1)} %get-tuple-element.39), channel_id=1, source_target_pairs={{0,192},{64,0},{128,64},{192,128},{1,193},{65,1},{129,65},{193,129... | collective-permute-start | bytes 159752 | tf_op jit(solution)/shard_map/ppermute | solution.py:524
  188.8 15.9 %collective-permute-start.16 = (bf16[208,128]{1,0:T(8,128)(2,1)S(1)}, bf16[208,128]{1,0:T(8,128)(2,1)S(1)}, u32[]{:S(2)}, u32[]{:S(2)}) collective-permute-start(bf16[208,128]{1,0:T(8,128)(2,1)S(1)} %get-tuple-element.38), channel_id=1, source_target_pairs={{0,128},{64,192},{128,0},{192,64},{1,129},{65,193},{129,1},{193,65... | collective-permute-start | bytes 159752 | tf_op jit(solution)/shard_map/ppermute | solution.py:524
  (4 other events, 15.8 us)
Sparse Core Ops, SparseCore 0:
  60.7 46.4 reduce-scatter.1
  109.9 46.2 all-gather.2
